TPU v7x, 32 devices: a whole 2x2x4 slice. The times are simulated.
32 devices in a mesh: dp: 2 (over core), expert: 16 (over z, y, x).
Axes of the slice: x: 2, y: 2, z: 4, core: 2. Of those that a mesh axis runs over, the one named last changes fastest.
Arguments:
- tokens: bfloat16 [4096, 2048], P(('dp', 'expert')), may hold values from -6 to 6
- gates: float32 [4096, 8], P(('dp', 'expert')), may hold values from 0.05 to 0.5
- expert_ids: int32 [4096, 8], P(('dp', 'expert')), may hold values from 0 to 15, as said below
- slots: int32 [4096, 8], P(('dp', 'expert')), may hold values from -1 to 63, as said below
- grad_out: bfloat16 [4096, 2048], P(('dp', 'expert')), may hold values from -6 to 6
- expert_weights: bfloat16 [16, 3, 2048, 768], P('expert', None, None, 'dp'), may hold values from -0.125 to 0.125
Outputs:
- combined: bfloat16 [4096, 2048], P(('dp', 'expert'))
- gate_grads: float32 [4096, 8], P(('dp', 'expert'))
- token_grads: bfloat16 [4096, 2048], P(('dp', 'expert'))
- weight_grads: bfloat16 [16, 3, 2048, 768], P('expert', None, None, 'dp')
Inputs may be any that keep to these rules, and one draw needn't show every extreme that they name: `expert_ids`: each token names 8 distinct experts. Within each device block of 128 tokens, the choices are counted in token then choice order for each expert; slots holds that count, or -1 once 64 earlier choices of the block went to that expert.
All inputs are finite; a program needn't handle non-finite values.
Results may differ from a plain program's by a relative error of at most 0.008.
Values may be sent and summed in bfloat16 or wider, within the bound.
No kernel may reach another device: no remote copies, remote signals or barrier semaphores. Data moves between devices by JAX's collectives and lax.ppermute only.
A program may use at most 192 MiB of HBM per device.

v0:
```python
import jax
import jax.numpy as jnp
from jax import lax
from jax.sharding import PartitionSpec as P


def contract_rows(left, right):
    return lax.dot_general(
        left, right, (((0,), (0,)), ((), ())), preferred_element_type=jnp.float32
    )


def contract_last(left, right):
    return lax.dot_general(
        left, right, (((1,), (1,)), ((), ())), preferred_element_type=jnp.float32
    )


def local(tokens, gates, expert_ids, slots, grad_out, expert_weights):
    n_expert = lax.axis_size("expert")
    tok_count, top_count = expert_ids.shape
    capacity = tok_count * top_count // n_expert
    slot_rows = n_expert * capacity
    width = tokens.shape[1]
    target = jnp.where(slots >= 0, expert_ids * capacity + slots, slot_rows).reshape(-1)
    anchor = jnp.broadcast_to(
        jnp.arange(tok_count, dtype=jnp.int32)[:, None], (tok_count, top_count)
    ).reshape(-1)
    holder = jnp.full((slot_rows,), tok_count, jnp.int32).at[target].set(anchor, mode="drop")
    slot_gate = jnp.zeros((slot_rows,), jnp.float32).at[target].set(gates.reshape(-1), mode="drop")
    padding = jnp.zeros((1, width), jnp.bfloat16)
    send_tokens = jnp.concatenate([tokens, padding], 0)[holder]
    send_grads = (
        slot_gate[:, None] * jnp.concatenate([grad_out, padding], 0)[holder].astype(jnp.float32)
    ).astype(jnp.bfloat16)
    arrived_tokens = lax.all_to_all(send_tokens, "expert", split_axis=0, concat_axis=0, tiled=True)
    weights = lax.all_gather(expert_weights, "dp", axis=3, tiled=True)[0]
    inputs = arrived_tokens
    gate_pre = jnp.dot(inputs, weights[0], preferred_element_type=jnp.float32)
    up_pre = jnp.dot(inputs, weights[1], preferred_element_type=jnp.float32)
    sigmoid_gate = jax.nn.sigmoid(gate_pre)
    activated = (gate_pre * sigmoid_gate * up_pre).astype(jnp.bfloat16)
    summand = contract_last(activated, weights[2])
    results = summand.astype(jnp.bfloat16)
    back_out = lax.all_to_all(results, "expert", split_axis=0, concat_axis=0, tiled=True)
    arrived_grads = lax.all_to_all(send_grads, "expert", split_axis=0, concat_axis=0, tiled=True)
    weights, inputs, gate_pre, up_pre, sigmoid_gate, activated = (
        weights,
        inputs,
        gate_pre,
        up_pre,
        sigmoid_gate,
        activated,
    )
    grad_act = jnp.dot(arrived_grads, weights[2], preferred_element_type=jnp.float32)
    grad_gate = (grad_act * up_pre * sigmoid_gate * (1.0 + gate_pre * (1.0 - sigmoid_gate))).astype(
        jnp.bfloat16
    )
    grad_up = (grad_act * gate_pre * sigmoid_gate).astype(jnp.bfloat16)
    summand = contract_last(grad_gate, weights[0]) + contract_last(grad_up, weights[1])
    stacked = jnp.stack(
        [
            contract_rows(inputs, grad_gate),
            contract_rows(inputs, grad_up),
            contract_rows(arrived_grads, activated),
        ]
    )[None]
    row_grads = summand.astype(jnp.bfloat16)
    weight_grads = lax.psum_scatter(stacked, "dp", scatter_dimension=3, tiled=True).astype(
        jnp.bfloat16
    )
    row_grads, weight_grads = (row_grads, weight_grads)
    back_grads = lax.all_to_all(row_grads, "expert", split_axis=0, concat_axis=0, tiled=True)
    returned = jnp.concatenate([back_out, padding], 0)[target].reshape(tok_count, top_count, width)
    combined = jnp.einsum("tk,tkd->td", gates, returned, preferred_element_type=jnp.float32).astype(
        jnp.bfloat16
    )
    gate_grads = jnp.einsum("td,tkd->tk", grad_out, returned, preferred_element_type=jnp.float32)
    returned_grads = jnp.concatenate([back_grads, padding], 0)[target].reshape(
        tok_count, top_count, width
    )
    token_grads = jnp.sum(returned_grads.astype(jnp.float32), axis=1).astype(jnp.bfloat16)
    return (combined, gate_grads, token_grads, weight_grads)


def solution(mesh):
    placed = (
        P(("dp", "expert"), None),
        P(("dp", "expert"), None),
        P(("dp", "expert"), None),
        P(("dp", "expert"), None),
        P(("dp", "expert"), None),
        P("expert", None, None, "dp"),
    )
    return jax.shard_map(
        local,
        mesh=mesh,
        in_specs=placed,
        out_specs=(
            P(("dp", "expert"), None),
            P(("dp", "expert"), None),
            P(("dp", "expert"), None),
            P("expert", None, None, "dp"),
        ),
        check_vma=False,
    )
```

profile of v0, /device:TPU:8, one launch (start us, length us, event | category | flops | bytes accessed | tf_op | source)
XLA Modules:
  0.0 489.3 jit_solution(786893756705248994)
XLA Ops:
  8.2 4.3 scatter_custom_fusion
  13.6 6.0 %gather_fusion = bf16[1024,2048]{1,0:T(8,128)(2,1)} fusion(bf16[129,2048]{1,0:T(8,128)(2,1)S(1)} %concatenate.12, s32[1024]{0:T(1024)S(1)} %fusion.10), kind=kCustom, calls=%fused_computation | custom fusion | bytes 8392704 | tf_op jit(solution)/shard_map/gather | solution.py:32
  19.6 7.2 %all-to-all-start = ((bf16[16,64,2048]{2,1,0:T(8,128)(2,1)}), bf16[16,64,2048]{2,1,0:T(8,128)(2,1)}, u32[]{:S(2)}, u32[]{:S(2)}) async-start(bf16[16,64,2048]{2,1,0:T(8,128)(2,1)} %bitcast.60), calls=%async_computation | async-start | bytes 8388608 | tf_op jit(solution)/shard_map/all_to_all | solution.py:36
  27.9 6.1 %gather_fusion.2 = bf16[1024,2048]{1,0:T(8,128)(2,1)} fusion(bf16[129,2048]{1,0:T(8,128)(2,1)S(1)} %concatenate.14, s32[1024]{0:T(1024)S(1)} %fusion.10), kind=kCustom, calls=%fused_computation.2 | custom fusion | bytes 8392704 | tf_op jit(solution)/shard_map/gather | solution.py:34
  34.2 4.3 scatter_custom_fusion.1
  38.6 5.8 %fusion = bf16[16,64,2048]{2,1,0:T(8,128)(2,1)} fusion(bf16[16,64,2048]{2,1,0:T(8,128)(2,1)} %bitcast.59, f32[16,64]{1,0:T(8,128)S(1)} %mul.45), kind=kLoop, calls=%fused_computation.8 | loop fusion | flops 6291456 | bytes 8392704 | tf_op jit(solution)/shard_map/convert_element_type | solution.py:35
  44.4 73.2 %all-to-all-done = bf16[16,64,2048]{2,1,0:T(8,128)(2,1)} async-done(((bf16[16,64,2048]{2,1,0:T(8,128)(2,1)}), bf16[16,64,2048]{2,1,0:T(8,128)(2,1)}, u32[]{:S(2)}, u32[]{:S(2)}) %all-to-all-start) | async-done | bytes 4194336 | tf_op jit(solution)/shard_map/all_to_all | solution.py:36
  117.7 8.9 %all-to-all-start.2 = ((bf16[16,64,2048]{2,1,0:T(8,128)(2,1)}), bf16[16,64,2048]{2,1,0:T(8,128)(2,1)}, u32[]{:S(2)}, u32[]{:S(2)}) async-start(bf16[16,64,2048]{2,1,0:T(8,128)(2,1)} %fusion), calls=%async_computation.2 | async-start | bytes 8388608 | tf_op jit(solution)/shard_map/all_to_all | solution.py:46
  126.8 8.2 %fusion.6 = f32[1024,768]{1,0:T(8,128)} fusion(bf16[1024,2048]{1,0:T(8,128)(2,1)} %bitcast.2, bf16[1,3,2048,768]{3,2,1,0:T(8,128)(2,1)} %all-gather.2.cloned.1.call-done), kind=kOutput, calls=%fused_computation.27 | convolution fusion | flops 3221225472 | bytes 10485760 | tf_op jit(solution)/shard_map/dot_general | solution.py:39
  135.1 8.2 %fusion.7 = f32[1024,768]{1,0:T(8,128)} fusion(bf16[1024,2048]{1,0:T(8,128)(2,1)} %bitcast.2, bf16[1,3,2048,768]{3,2,1,0:T(8,128)(2,1)} %all-gather.2.cloned.1.call-done), kind=kOutput, calls=%fused_computation.28 | convolution fusion | flops 3221225472 | bytes 10485760 | tf_op jit(solution)/shard_map/dot_general | solution.py:40
  143.3 73.0 %all-to-all-done.2 = bf16[16,64,2048]{2,1,0:T(8,128)(2,1)} async-done(((bf16[16,64,2048]{2,1,0:T(8,128)(2,1)}), bf16[16,64,2048]{2,1,0:T(8,128)(2,1)}, u32[]{:S(2)}, u32[]{:S(2)}) %all-to-all-start.2) | async-done | bytes 4194336 | tf_op jit(solution)/shard_map/all_to_all | solution.py:46
  216.3 9.3 %multiply_convert_fusion = (bf16[1024,768]{1,0:T(8,128)(2,1)S(1)}, bf16[1024,768]{1,0:T(8,128)(2,1)S(1)}, bf16[1024,768]{1,0:T(8,128)(2,1)S(1)}) fusion(f32[1024,768]{1,0:T(8,128)} %fusion.6, f32[1024,768]{1,0:T(8,128)} %fusion.7, bf16[1024,2048]{1,0:T(8,128)(2,1)} %bitcast.15, bf16[1,3,2048,768]{3,2,1,0:T(8,128)(2,1)} %all-gather.2.cloned.1.call-done), kind=kOutput, calls=%fused_computation.22 | convolution fusion | flops 3233808384 | bytes 18350080 | tf_op jit(solution)/shard_map/dot_general | solution.py:55
  225.6 6.6 %convolution_bitcast_fusion = f32[1,2048,768]{2,1,0:T(8,128)S(1)} fusion(bf16[1024,2048]{1,0:T(8,128)(2,1)} %bitcast.15, bf16[1024,768]{1,0:T(8,128)(2,1)S(1)} %get-tuple-element.6), kind=kOutput, calls=%fused_computation.15 | convolution fusion | flops 3221225472 | bytes 12058624 | tf_op jit(solution)/shard_map/dot_general | solution.py:8
  232.2 5.4 %convolution_bitcast_fusion.1 = f32[1,2048,768]{2,1,0:T(8,128)S(1)} fusion(bf16[1024,2048]{1,0:T(8,128)(2,1)} %bitcast.2, bf16[1024,768]{1,0:T(8,128)(2,1)S(1)} %get-tuple-element.4), kind=kOutput, calls=%fused_computation.16 | convolution fusion | flops 3221225472 | bytes 12058624 | tf_op jit(solution)/shard_map/dot_general | solution.py:8
  237.7 5.5 %convolution_bitcast_fusion.2 = f32[1,2048,768]{2,1,0:T(8,128)S(1)} fusion(bf16[1024,2048]{1,0:T(8,128)(2,1)} %bitcast.2, bf16[1024,768]{1,0:T(8,128)(2,1)S(1)} %get-tuple-element.5), kind=kOutput, calls=%fused_computation.17 | convolution fusion | flops 3221225472 | bytes 12058624 | tf_op jit(solution)/shard_map/dot_general | solution.py:8
  243.2 6.7 %maximum_bitcast_fusion = f32[1,3,2048,768]{3,2,1,0:T(8,128)} fusion(f32[1,2048,768]{2,1,0:T(8,128)S(1)} %convolution_bitcast_fusion, f32[1,2048,768]{2,1,0:T(8,128)S(1)} %convolution_bitcast_fusion.1, f32[1,2048,768]{2,1,0:T(8,128)S(1)} %convolution_bitcast_fusion.2), kind=kLoop, calls=%fused_computation.6 | loop fusion | flops 9437184 | bytes 37748736 | tf_op jit(solution)/shard_map/broadcast_in_dim | solution.py:61
  249.9 7.8 %convolution_convert_fusion = bf16[1024,2048]{1,0:T(8,128)(2,1)} fusion(bf16[1024,768]{1,0:T(8,128)(2,1)} %copy-done.5, bf16[1,3,2048,768]{3,2,1,0:T(8,128)(2,1)} %all-gather.2.cloned.1.call-done), kind=kOutput, calls=%fused_computation.18 | convolution fusion | flops 3223322624 | bytes 8912896 | tf_op jit(solution)/shard_map/dot_general | solution.py:14
  257.7 8.1 %all-to-all-start.1 = ((bf16[16,64,2048]{2,1,0:T(8,128)(2,1)}), bf16[16,64,2048]{2,1,0:T(8,128)(2,1)}, u32[]{:S(2)}, u32[]{:S(2)}) async-start(bf16[16,64,2048]{2,1,0:T(8,128)(2,1)} %bitcast.62), calls=%async_computation.1 | async-start | bytes 8388608 | tf_op jit(solution)/shard_map/all_to_all | solution.py:45
  265.8 6.3 %fusion.5 = f32[1024,2048]{1,0:T(8,128)S(1)} fusion(bf16[1024,768]{1,0:T(8,128)(2,1)S(1)} %get-tuple-element.5, bf16[1,3,2048,768]{3,2,1,0:T(8,128)(2,1)} %all-gather.2.cloned.1.call-done), kind=kOutput, calls=%fused_computation.26 | convolution fusion | flops 3221225472 | bytes 13107200 | tf_op jit(solution)/shard_map/dot_general | solution.py:14
  272.1 7.6 %add_convert_fusion = bf16[1024,2048]{1,0:T(8,128)(2,1)} fusion(f32[1024,2048]{1,0:T(8,128)S(1)} %fusion.5, bf16[1024,768]{1,0:T(8,128)(2,1)S(1)} %copy-done.4, bf16[1,3,2048,768]{3,2,1,0:T(8,128)(2,1)} %all-gather.2.cloned.1.call-done), kind=kOutput, calls=%fused_computation.9 | convolution fusion | flops 3225419776 | bytes 17301504 | tf_op jit(solution)/shard_map/dot_general | solution.py:14
  279.8 75.9 %all-to-all-done.1 = bf16[16,64,2048]{2,1,0:T(8,128)(2,1)} async-done(((bf16[16,64,2048]{2,1,0:T(8,128)(2,1)}), bf16[16,64,2048]{2,1,0:T(8,128)(2,1)}, u32[]{:S(2)}, u32[]{:S(2)}) %all-to-all-start.1) | async-done | bytes 4194336 | tf_op jit(solution)/shard_map/all_to_all | solution.py:45
  355.7 8.1 %all-to-all-start.3 = ((bf16[16,64,2048]{2,1,0:T(8,128)(2,1)}), bf16[16,64,2048]{2,1,0:T(8,128)(2,1)}, u32[]{:S(2)}, u32[]{:S(2)}) async-start(bf16[16,64,2048]{2,1,0:T(8,128)(2,1)} %bitcast.61), calls=%async_computation.3 | async-start | bytes 8388608 | tf_op jit(solution)/shard_map/all_to_all | solution.py:73
  363.9 4.8 concatenate.13
  368.7 11.6 %gather_fusion.1 = bf16[1024,2048]{1,0:T(8,128)(2,1)} fusion(bf16[1025,2048]{1,0:T(8,128)(2,1)} %concatenate.13, s32[1024]{0:T(1024)S(1)} %broadcast_clamp_fusion), kind=kCustom, calls=%fused_computation.1 | custom fusion | bytes 8392704 | tf_op jit(solution)/shard_map/gather | solution.py:74
  380.3 3.6 fusion.3
  383.8 1.1 copy.19
  384.9 2.7 fusion.1
  388.3 65.1 %all-to-all-done.3 = bf16[16,64,2048]{2,1,0:T(8,128)(2,1)} async-done(((bf16[16,64,2048]{2,1,0:T(8,128)(2,1)}), bf16[16,64,2048]{2,1,0:T(8,128)(2,1)}, u32[]{:S(2)}, u32[]{:S(2)}) %all-to-all-start.3) | async-done | bytes 4194336 | tf_op jit(solution)/shard_map/all_to_all | solution.py:73
  453.4 4.8 concatenate.15
  458.2 11.5 %gather_fusion.3 = bf16[1024,2048]{1,0:T(8,128)(2,1)} fusion(bf16[1025,2048]{1,0:T(8,128)(2,1)} %concatenate.15, s32[1024]{0:T(1024)S(1)} %broadcast_clamp_fusion), kind=kCustom, calls=%fused_computation.3 | custom fusion | bytes 8392704 | tf_op jit(solution)/shard_map/gather | solution.py:79
  469.7 5.9 %bitcast_reduce_fusion = bf16[128,2048]{1,0:T(8,128)(2,1)} fusion(bf16[1024,2048]{1,0:T(8,128)(2,1)} %gather_fusion.3), kind=kLoop, calls=%fused_computation.10 | loop fusion | flops 1835008 | bytes 4718592 | tf_op jit(solution)/shard_map/reduce_sum | solution.py:82
  475.6 6.4 %convert_element_type.43 = bf16[1,3,2048,384]{3,2,1,0:T(8,128)(2,1)} convert(f32[1,3,2048,384]{3,2,1,0:T(8,128)} %reduce-scatter.2.cloned.1.call-done) | non-fusion elementwise | flops 2359296 | bytes 14155776 | tf_op jit(solution)/shard_map/convert_element_type | solution.py:69
  (33 shorter events, 4.5 us)
Async XLA Ops:
  19.6 98.1 %all-to-all-start = ((bf16[16,64,2048]{2,1,0:T(8,128)(2,1)}), bf16[16,64,2048]{2,1,0:T(8,128)(2,1)}, u32[]{:S(2)}, u32[]{:S(2)}) async-start(bf16[16,64,2048]{2,1,0:T(8,128)(2,1)} %bitcast.60), calls=%async_computation | async-start | bytes 8388608 | tf_op jit(solution)/shard_map/all_to_all | solution.py:36
  26.8 1.0 copy-start.1
  26.8 100.0 %all-gather.2.cloned.1.call-start = ((), (), s32[]{:S(2)}) async-start(), calls=%async_computation.5 | async-start | bytes 14155776 | tf_op jit(solution)/shard_map/all_gather | solution.py:37
  27.9 6.1 %copy-start.2 = (f32[128,8]{0,1:T(8,128)S(1)}, f32[128,8]{0,1:T(8,128)}, u32[]{:S(2)}) copy-start(f32[128,8]{0,1:T(8,128)} %param.7) | copy-start | bytes 12292
  117.7 98.6 %all-to-all-start.2 = ((bf16[16,64,2048]{2,1,0:T(8,128)(2,1)}), bf16[16,64,2048]{2,1,0:T(8,128)(2,1)}, u32[]{:S(2)}, u32[]{:S(2)}) async-start(bf16[16,64,2048]{2,1,0:T(8,128)(2,1)} %fusion), calls=%async_computation.2 | async-start | bytes 8388608 | tf_op jit(solution)/shard_map/all_to_all | solution.py:46
  126.6 349.0 %reduce-scatter.2.cloned.1.call-start = ((), (), s32[]{:S(2)}) async-start(), calls=%async_computation.6 | async-start | bytes 28311552 | tf_op jit(solution)/shard_map/reduce_scatter | solution.py:69
  225.6 6.6 %copy-start.5 = (bf16[1024,768]{1,0:T(8,128)(2,1)}, bf16[1024,768]{1,0:T(8,128)(2,1)S(1)}, u32[]{:S(2)}) copy-start(bf16[1024,768]{1,0:T(8,128)(2,1)S(1)} %get-tuple-element.6) | copy-start | bytes 4718596
  225.6 6.6 %copy-start.3 = (bf16[1024,768]{1,0:T(8,128)(2,1)}, bf16[1024,768]{1,0:T(8,128)(2,1)S(1)}, u32[]{:S(2)}) copy-start(bf16[1024,768]{1,0:T(8,128)(2,1)S(1)} %get-tuple-element.4) | copy-start | bytes 4718596
  257.7 97.9 %all-to-all-start.1 = ((bf16[16,64,2048]{2,1,0:T(8,128)(2,1)}), bf16[16,64,2048]{2,1,0:T(8,128)(2,1)}, u32[]{:S(2)}, u32[]{:S(2)}) async-start(bf16[16,64,2048]{2,1,0:T(8,128)(2,1)} %bitcast.62), calls=%async_computation.1 | async-start | bytes 8388608 | tf_op jit(solution)/shard_map/all_to_all | solution.py:45
  265.8 6.3 %copy-start.4 = (bf16[1024,768]{1,0:T(8,128)(2,1)S(1)}, bf16[1024,768]{1,0:T(8,128)(2,1)}, u32[]{:S(2)}) copy-start(bf16[1024,768]{1,0:T(8,128)(2,1)} %copy-done.3) | copy-start | bytes 4718596
  355.7 97.7 %all-to-all-start.3 = ((bf16[16,64,2048]{2,1,0:T(8,128)(2,1)}), bf16[16,64,2048]{2,1,0:T(8,128)(2,1)}, u32[]{:S(2)}, u32[]{:S(2)}) async-start(bf16[16,64,2048]{2,1,0:T(8,128)(2,1)} %bitcast.61), calls=%async_computation.3 | async-start | bytes 8388608 | tf_op jit(solution)/shard_map/all_to_all | solution.py:73
  380.3 4.7 copy-start
Sparse Core Ops, SparseCore 0:
  29.2 22.9 all-gather.1
  250.0 30.6 reduce-scatter.1
where the time goes:
time: 497 us; the launch traced here: 489 us
  waiting for transfers between devices  288 us (58%)
  matrix products  71.3 us (14%)
  local copies, waits for them, and re-layouts  57.3 us (12%)
  starting transfers between devices  32.6 us (7%)
  other arithmetic  25.5 us (5%)
  between operations  14.7 us (3%)
    all_to_all x1, waiting for transfers between devices, local(): lax.all_to_all(results, 'expert', split_axis=0, concat_axis=0, tiled=True)  75.9 us
    all_to_all x1, waiting for transfers between devices, local(): lax.all_to_all(send_tokens, 'expert', split_axis=0, concat_axis=0, tiled=...  73.2 us
    all_to_all x1, waiting for transfers between devices, local(): lax.all_to_all(send_grads, 'expert', split_axis=0, concat_axis=0, tiled=T...  73 us
    all_to_all x1, waiting for transfers between devices, local(): lax.all_to_all(row_grads, 'expert', split_axis=0, concat_axis=0, tiled=True)  65.1 us
    dot_general x3, matrix products, contract_last(): lax.dot_general(left, right, (((1,), (1,)), ((), ())), preferred_element_...  21.8 us
    dot_general x3, matrix products, contract_rows(): lax.dot_general(left, right, (((0,), (0,)), ((), ())), preferred_element_...  17.5 us
    gather x1, local copies, waits for them, and re-layouts, local(): jnp.concatenate([back_out, padding], 0)[target]  11.6 us
    gather x1, local copies, waits for them, and re-layouts, local(): jnp.concatenate([back_grads, padding], 0)[target]  11.5 us
  transfers between devices with their start and end apart: 6, of which 4 were waited for; matrix products, arithmetic and copies ran while one was open for 21% of the time, Pallas kernels for 0%

commit v1 on v0

v1 whole, which is shorter than its diff:
```python
import functools

import jax
import jax.numpy as jnp
from jax import lax
from jax.experimental import pallas as pl
from jax.experimental.pallas import tpu as pltpu
from jax.sharding import PartitionSpec as P

F32 = jnp.float32
BF16 = jnp.bfloat16
MIB = 1 << 20
CHUNKS = 4
HBM = pl.BlockSpec(memory_space=pl.ANY)
WHOLE = pl.BlockSpec(memory_space=pltpu.VMEM)
SCALAR = pl.BlockSpec(memory_space=pltpu.SMEM)


def mask_of(table, expert, capacity):
    top = table.shape[0] // 2
    tokens = table.shape[1]
    wanted = (expert * capacity + lax.broadcasted_iota(jnp.int32, (capacity, tokens), 0)).astype(F32)
    hit = jnp.zeros((capacity, tokens), F32)
    for k in range(top):
        hit = hit + jnp.where(table[k : k + 1] == wanted, 1.0, 0.0)
    return hit


def gate_column(table, expert, capacity):
    top = table.shape[0] // 2
    tokens = table.shape[1]
    wanted = (expert * capacity + lax.broadcasted_iota(jnp.int32, (capacity, tokens), 0)).astype(F32)
    gate = jnp.zeros((capacity, tokens), F32)
    for k in range(top):
        gate = gate + jnp.where(table[k : k + 1] == wanted, table[top + k : top + k + 1], 0.0)
    return jnp.sum(gate, axis=1, keepdims=True)


def pick_kernel(capacity, n_half, blocks, me_ref, *refs):
    tables = refs[:n_half]
    arrays = refs[n_half : 3 * n_half]
    own_t, own_g, sent_t, sent_g = refs[3 * n_half :]
    me = me_ref[0]
    for expert, outs in ((me ^ 1, (sent_t, sent_g)), (me, (own_t, own_g))):
        for half in range(n_half):
            for b in range(blocks):
                mask = mask_of(tables[half][b], expert, capacity).astype(BF16)
                tokens = mask.shape[1]
                row = (half * blocks + b) * capacity
                for a in range(2):
                    source = arrays[2 * half + a][b * tokens : (b + 1) * tokens, :]
                    outs[a][row : row + capacity, :] = jnp.dot(
                        mask, source, preferred_element_type=F32
                    ).astype(BF16)


def pick(me, capacity, halves):
    n_half = len(halves)
    blocks = halves[0][0].shape[0]
    width = halves[0][1].shape[1]
    tile = 512
    rows = n_half * blocks * capacity
    in_rows = halves[0][1].shape[0]
    table_spec = pl.BlockSpec(halves[0][0].shape, lambda i: (0, 0, 0))
    in_spec = pl.BlockSpec((in_rows, tile), lambda i: (0, i))
    out_spec = pl.BlockSpec((rows, tile), lambda i: (0, i))
    return pl.pallas_call(
        functools.partial(pick_kernel, capacity, n_half, blocks),
        grid=(width // tile,),
        in_specs=[SCALAR] + [table_spec] * n_half + [in_spec] * (2 * n_half),
        out_specs=[out_spec] * 4,
        out_shape=[jax.ShapeDtypeStruct((rows, width), BF16)] * 4,
        compiler_params=pltpu.CompilerParams(vmem_limit_bytes=24 * MIB),
        cost_estimate=pl.CostEstimate(
            flops=8 * rows * in_rows * width // blocks // n_half,
            bytes_accessed=4 * (n_half * in_rows + 2 * rows) * width,
            transcendentals=0,
        ),
        name="pick",
    )(me, *[h[0] for h in halves], *[a for h in halves for a in h[1:]])


def expert_kernel(capacity, n_piece, blocks, me_ref, tables, w_own, w_other, *refs):
    x_refs = refs[:n_piece]
    g_refs = refs[n_piece : 2 * n_piece]
    (out_own, out_sent, back_own, back_sent, gate_rows, act_ref, dgate_ref, dup_ref) = refs[
        2 * n_piece : 2 * n_piece + 8
    ]
    w, x, g, sem = refs[2 * n_piece + 8 :]
    half = w_own.shape[2]
    hidden = 2 * half
    rows, width = x.shape
    copies = []
    for i in (0, 1, 2):
        pair = []
        for j, source in enumerate((w_own, w_other)):
            copy = pltpu.make_async_copy(
                source.at[i], w.at[i, :, pl.ds(j * half, half)], sem.at[i, j]
            )
            copy.start()
            pair.append(copy)
        copies.append(pair)
    row = 0
    for xr, gr in zip(x_refs, g_refs):
        count = xr.shape[0]
        x[row : row + count, :] = xr[...]
        g[row : row + count, :] = gr[...]
        row += count
    me = me_ref[0]
    groups = tables.shape[0]
    gates = jnp.concatenate(
        [gate_column(tables[i], me, capacity) for i in range(groups)], axis=0
    )
    for pair in copies:
        for copy in pair:
            copy.wait()
    step = 256

    def hidden_tile(n, total):
        cols = pl.ds(pl.multiple_of(n * step, step), step)
        gate_pre = jnp.dot(x[...], w[0, :, cols], preferred_element_type=F32)
        up_pre = jnp.dot(x[...], w[1, :, cols], preferred_element_type=F32)
        pulled = jnp.dot(g[...], w[2, :, cols], preferred_element_type=F32)
        sig = jax.nn.sigmoid(gate_pre)
        silu = gate_pre * sig
        act = silu * up_pre
        grad_act = pulled * gates
        act_ref[:, cols] = (act * gates).astype(BF16)
        dgate_ref[:, cols] = (grad_act * up_pre * sig * (1.0 + gate_pre * (1.0 - sig))).astype(BF16)
        dup_ref[:, cols] = (grad_act * silu).astype(BF16)
        return total + jnp.sum(act * pulled, axis=1, keepdims=True)

    total = lax.fori_loop(0, hidden // step, hidden_tile, jnp.zeros((rows, 1), F32))
    for i in range(groups):
        mask = mask_of(tables[i], me, capacity)
        gate_rows[i : i + 1, :] = jnp.sum(
            mask * total[i * capacity : (i + 1) * capacity], axis=0, keepdims=True
        )
    side = rows // 2
    nt = (((1,), (1,)), ((), ()))

    def width_tile(n, carry):
        cols = pl.ds(pl.multiple_of(n * step, step), step)
        out = lax.dot_general(act_ref[...], w[2, cols, :], nt, preferred_element_type=F32)
        out = out.astype(BF16)
        out_own[:, cols] = out[:side]
        out_sent[:, cols] = out[side:]
        back = lax.dot_general(dgate_ref[...], w[0, cols, :], nt, preferred_element_type=F32)
        back += lax.dot_general(dup_ref[...], w[1, cols, :], nt, preferred_element_type=F32)
        back = back.astype(BF16)
        back_own[:, cols] = back[:side]
        back_sent[:, cols] = back[side:]
        return carry

    lax.fori_loop(0, width // step, width_tile, 0)


def expert(me, capacity, tables, w_own, w_other, x_pieces, g_pieces):
    n_piece = len(x_pieces)
    rows = sum(p.shape[0] for p in x_pieces)
    width = x_pieces[0].shape[1]
    hidden = 2 * w_own.shape[2]
    groups, _, tokens = tables.shape
    return pl.pallas_call(
        functools.partial(expert_kernel, capacity, n_piece, groups),
        in_specs=[SCALAR, WHOLE, HBM, HBM] + [WHOLE] * (2 * n_piece),
        out_specs=[WHOLE] * 8,
        out_shape=[jax.ShapeDtypeStruct((rows // 2, width), BF16)] * 4
        + [jax.ShapeDtypeStruct((groups, tokens), F32)]
        + [jax.ShapeDtypeStruct((rows, hidden), BF16)] * 3,
        scratch_shapes=[
            pltpu.VMEM((3, width, hidden), BF16),
            pltpu.VMEM((rows, width), BF16),
            pltpu.VMEM((rows, width), BF16),
            pltpu.SemaphoreType.DMA((3, 2)),
        ],
        compiler_params=pltpu.CompilerParams(vmem_limit_bytes=44 * MIB),
        cost_estimate=pl.CostEstimate(
            flops=12 * rows * width * hidden,
            bytes_accessed=6 * width * hidden + 8 * rows * width,
            transcendentals=rows * hidden,
        ),
        name="expert",
    )(me, tables, w_own, w_other, *x_pieces, *g_pieces)


def spread(table, me, capacity, own, received):
    mask = jnp.concatenate(
        [mask_of(table, me, capacity), mask_of(table, me ^ 1, capacity)], axis=0
    )
    rows = jnp.concatenate([own, received], axis=0)
    return jnp.dot(mask.T.astype(BF16), rows, preferred_element_type=F32)


def partial_kernel(capacity, blocks, me_ref, tables, own, received, out):
    tokens = tables.shape[2]
    for b in range(blocks):
        rows = pl.ds(b * capacity, capacity)
        out[b * tokens : (b + 1) * tokens, :] = spread(
            tables[b], me_ref[0], capacity, own[rows, :], received[rows, :]
        ).astype(BF16)


def partial_sum(me, capacity, tables, own, received):
    blocks, _, tokens = tables.shape
    width = own.shape[1]
    tile = 1024
    row_spec = pl.BlockSpec((blocks * capacity, tile), lambda i: (1, i))
    return pl.pallas_call(
        functools.partial(partial_kernel, capacity, blocks),
        grid=(width // tile,),
        in_specs=[SCALAR, pl.BlockSpec(tables.shape, lambda i: (0, 0, 0)), row_spec, row_spec],
        out_specs=pl.BlockSpec((blocks * tokens, tile), lambda i: (0, i)),
        out_shape=jax.ShapeDtypeStruct((blocks * tokens, width), BF16),
        compiler_params=pltpu.CompilerParams(vmem_limit_bytes=24 * MIB),
        cost_estimate=pl.CostEstimate(
            flops=4 * blocks * tokens * capacity * width,
            bytes_accessed=2 * blocks * (tokens + 2 * capacity) * width,
            transcendentals=0,
        ),
        name="partial_sum",
    )(me, tables, own, received)


def block_kernel(capacity, me_ref, table, own, received, *refs):
    out = refs[-1]
    total = spread(table[0], me_ref[0], capacity, own[...], received[...])
    for other in refs[:-1]:
        total = total + other[...].astype(F32)
    out[...] = total.astype(BF16)


def block_sum(me, capacity, table, own, received, b, others):
    tokens = table.shape[2]
    width = own.shape[1]
    tile = 1024
    row_spec = pl.BlockSpec((capacity, tile), lambda i: (b, i))
    return pl.pallas_call(
        functools.partial(block_kernel, capacity),
        grid=(width // tile,),
        in_specs=[SCALAR, pl.BlockSpec(table.shape, lambda i: (0, 0, 0)), row_spec, row_spec]
        + [pl.BlockSpec((tokens, tile), lambda i, at=at: (at, i)) for _, at in others],
        out_specs=pl.BlockSpec((tokens, tile), lambda i: (0, i)),
        out_shape=jax.ShapeDtypeStruct((tokens, width), BF16),
        compiler_params=pltpu.CompilerParams(vmem_limit_bytes=24 * MIB),
        cost_estimate=pl.CostEstimate(
            flops=4 * tokens * capacity * width,
            bytes_accessed=2 * (tokens * (1 + len(others)) + 2 * capacity) * width,
            transcendentals=0,
        ),
        name="block_sum",
    )(me, table, own, received, *[a for a, _ in others])


def weight_kernel(n_piece, n_chunk, n_out, *refs):
    left = jnp.concatenate([r[...] for r in refs[:n_piece]], axis=0)
    rights = refs[n_piece : n_piece + n_out * n_chunk]
    outs = refs[n_piece + n_out * n_chunk :]
    tn = (((0,), (0,)), ((), ()))
    for i in range(n_out):
        right = jnp.concatenate([r[...] for r in rights[i * n_chunk : (i + 1) * n_chunk]], axis=0)
        total = lax.dot_general(left, right, tn, preferred_element_type=F32)
        half = total.shape[1] // 2
        outs[2 * i][...] = total[:, :half]
        outs[2 * i + 1][...] = total[:, half:].astype(BF16)


def weight_sums(pieces, rights):
    width = pieces[0].shape[1]
    hidden = rights[0][0].shape[1]
    rows = sum(p.shape[0] for p in pieces)
    tile = 256
    n_out = len(rights)
    flat = [r for group in rights for r in group]
    return pl.pallas_call(
        functools.partial(weight_kernel, len(pieces), len(rights[0]), n_out),
        grid=(width // tile,),
        in_specs=[pl.BlockSpec((p.shape[0], tile), lambda i: (0, i)) for p in pieces]
        + [pl.BlockSpec(r.shape, lambda i: (0, 0)) for r in flat],
        out_specs=[pl.BlockSpec((tile, hidden // 2), lambda i: (i, 0))] * (2 * n_out),
        out_shape=[
            jax.ShapeDtypeStruct((width, hidden // 2), F32),
            jax.ShapeDtypeStruct((width, hidden // 2), BF16),
        ]
        * n_out,
        compiler_params=pltpu.CompilerParams(vmem_limit_bytes=40 * MIB),
        cost_estimate=pl.CostEstimate(
            flops=2 * rows * width * hidden * n_out,
            bytes_accessed=2 * rows * width + n_out * (2 * rows * hidden + 3 * width * hidden),
            transcendentals=0,
        ),
        name="weight_sums",
    )(*pieces, *flat)


def local(tokens, gates, expert_ids, slots, grad_out, expert_weights):
    n_expert = lax.axis_size("expert")
    n_dp = lax.axis_size("dp")
    tok_count, top_count = expert_ids.shape
    capacity = tok_count * top_count // n_expert
    depth = n_expert // 4
    per_chunk = depth // CHUNKS

    def swap(array, flip):
        return lax.ppermute(array, "expert", [(i, i ^ flip) for i in range(n_expert)])

    def swap_dp(array):
        return lax.ppermute(array, "dp", [(i, n_dp - 1 - i) for i in range(n_dp)])

    index = lax.axis_index("expert").astype(jnp.int32)
    me = index.reshape(1)
    key = jnp.where(slots >= 0, expert_ids * capacity + slots, -1)
    table = jnp.concatenate([key.T.astype(F32), gates.T], axis=0)[None]

    pair = jnp.concatenate([table, swap(table, 2)], axis=0)
    near = [pair] + [swap(pair, 4 * s) for s in range(1, depth)]
    near = jnp.stack(near)
    far = swap(near, 1)

    w_own = expert_weights[0]
    w_other = swap_dp(w_own)

    pair_t = [tokens] + [swap(tokens, 4 * s) for s in range(1, depth)]
    pair_g = [grad_out] + [swap(grad_out, 4 * s) for s in range(1, depth)]

    def chunk_rows(blocks, c):
        part = blocks[c * per_chunk : (c + 1) * per_chunk]
        return part[0] if len(part) == 1 else jnp.concatenate(part, axis=0)

    x_pieces, g_pieces, acts, dgates, dups, gate_rows = [], [], [], [], [], []
    outs, backs = [], []
    for c in range(CHUNKS):
        zs = slice(c * per_chunk, (c + 1) * per_chunk)
        here_t, here_g = chunk_rows(pair_t, c), chunk_rows(pair_g, c)
        there_t, there_g = swap(here_t, 2), swap(here_g, 2)
        first = (near[zs, 0], here_t, here_g)
        second = (near[zs, 1], there_t, there_g)
        picks = [[first], [second]] if c == 0 else [[first, second]]
        own_t, own_g, got_t, got_g = [], [], [], []
        for halves in picks:
            a, b, sent_t, sent_g = pick(me, capacity, halves)
            own_t.append(a)
            own_g.append(b)
            got_t.append(swap(sent_t, 1))
            got_g.append(swap(sent_g, 1))
        tables = jnp.concatenate([near[zs, 0], near[zs, 1], far[zs, 0], far[zs, 1]], axis=0)
        out_own, out_sent, back_own, back_sent, rows, act, dgate, dup = expert(
            me, capacity, tables, w_own, w_other, own_t + got_t, own_g + got_g
        )
        x_pieces += own_t + got_t
        g_pieces += own_g + got_g
        acts.append(act)
        dgates.append(dgate)
        dups.append(dup)
        gate_rows.append(rows.reshape(2, 2, per_chunk, tok_count))
        outs.append((out_own, out_sent))
        backs.append((back_own, back_sent))

    results = []
    for sent in (outs, backs):
        waiting = []
        final = None
        for c in reversed(range(CHUNKS)):
            zs = slice(c * per_chunk, (c + 1) * per_chunk)
            own, given = sent[c]
            received = swap(given, 1)
            from_y = swap(partial_sum(me, capacity, near[zs, 1], own, received), 2)
            for b in reversed(range(per_chunk)):
                s = c * per_chunk + b
                if s > 0:
                    part = block_sum(
                        me, capacity, near[s : s + 1, 0], own, received, b, [(from_y, b)]
                    )
                    waiting.append((swap(part, 4 * s), 0))
                else:
                    final = block_sum(
                        me, capacity, near[0:1, 0], own, received, 0, [(from_y, 0)] + waiting
                    )
        results.append(final)
    combined, token_grads = results

    own0, other0, own1, other1 = weight_sums(x_pieces, [dgates, dups])
    own2, other2 = weight_sums(g_pieces, [acts])
    weight_grads = jnp.stack(
        [
            (own + swap_dp(other).astype(F32)).astype(BF16)
            for own, other in ((own0, other0), (own1, other1), (own2, other2))
        ]
    )[None]

    sums = jnp.stack(gate_rows)
    sums = sums.transpose(1, 2, 0, 3, 4).reshape(2, 2, depth, tok_count)
    sums = jnp.stack([sums[0], swap(sums[1], 1)])
    sums = jnp.stack([sums[:, 0], swap(sums[:, 1], 2)])
    sums = jnp.stack([sums[:, :, 0]] + [swap(sums[:, :, s], 4 * s) for s in range(1, depth)])
    sums = sums.reshape(n_expert, tok_count)
    source = jnp.arange(n_expert, dtype=jnp.int32) ^ index
    hit = (expert_ids[:, :, None] == source[None, None, :]) & (slots >= 0)[:, :, None]
    gate_grads = jnp.sum(jnp.where(hit, sums.T[:, None, :], 0.0), axis=2)
    return (combined, gate_grads, token_grads, weight_grads)


def solution(mesh):
    placed = (
        P(("dp", "expert"), None),
        P(("dp", "expert"), None),
        P(("dp", "expert"), None),
        P(("dp", "expert"), None),
        P(("dp", "expert"), None),
        P("expert", None, None, "dp"),
    )
    return jax.shard_map(
        local,
        mesh=mesh,
        in_specs=placed,
        out_specs=(
            P(("dp", "expert"), None),
            P(("dp", "expert"), None),
            P(("dp", "expert"), None),
            P("expert", None, None, "dp"),
        ),
        check_vma=False,
    )
```

time: 497 us -> 436 us (0.88); the launches traced: 489 us -> 435 us
  Pallas kernels: 0 us -> 86.2 us
  matrix products: 71.3 us -> 0 us
  waiting for transfers between devices: 288 us -> 234 us
  starting transfers between devices: 32.6 us -> 85 us
  local copies, waits for them, and re-layouts: 57.3 us -> 21.4 us
  other arithmetic: 25.5 us -> 7.16 us
  between operations: 14.7 us -> 1.67 us
    all_to_all x4 -> x0, waiting for transfers between devices: 287 us -> none  [the longest x1 75.9 us: local(): lax.all_to_all(results, 'expert', split_axis=0, concat_axis=0, tiled=True)]
    ppermute x0 -> x60, waiting for transfers between devices: none -> 234 us  [the longest x56 234 us: swap(): lax.ppermute(array, 'expert', [(i, i ^ flip) for i in range(n_expert)])]
    pallas_call x0 -> x27, Pallas kernels: none -> 86.2 us  [the longest x4 41.8 us: expert(): pl.pallas_call(functools.partial(expert_kernel, capacity, n_piece, groups...]
    ppermute x0 -> x60, starting transfers between devices: none -> 85 us  [the longest x56 84.2 us: swap(): lax.ppermute(array, 'expert', [(i, i ^ flip) for i in range(n_expert)])]
    dot_general x11 -> x0, matrix products: 71.3 us -> none  [the longest x3 21.8 us: contract_last(): lax.dot_general(left, right, (((1,), (1,)), ((), ())), preferred_element_...]
    gather x4 -> x0, local copies, waits for them, and re-layouts: 35.2 us -> none  [the longest x1 11.6 us: local(): jnp.concatenate([back_out, padding], 0)[target]]
    all_to_all x4 -> x0, starting transfers between devices: 32.3 us -> none  [the longest x1 8.94 us: local(): lax.all_to_all(send_grads, 'expert', split_axis=0, concat_axis=0, tiled=T...]
    unnamed x14 -> x148, local copies, waits for them, and re-layouts: 0.56 us -> 21.4 us
  transfers between devices with their start and end apart: 6 -> 60, of which waited for: 4 -> 36; matrix products, arithmetic and copies ran while one was open for 21% -> 1% of each run, Pallas kernels for 0% -> 20%
where the time goes in v1:
time: 436 us; the launch traced here: 435 us
  waiting for transfers between devices  234 us (54%)
  Pallas kernels  86.2 us (20%)
  starting transfers between devices  85 us (19%)
  local copies, waits for them, and re-layouts  21.4 us (5%)
  other arithmetic  7.16 us (2%)
    ppermute x56, waiting for transfers between devices, swap(): lax.ppermute(array, 'expert', [(i, i ^ flip) for i in range(n_expert)])  234 us
    ppermute x56, starting transfers between devices, swap(): lax.ppermute(array, 'expert', [(i, i ^ flip) for i in range(n_expert)])  84.2 us
    pallas_call x4, Pallas kernels, expert(): pl.pallas_call(functools.partial(expert_kernel, capacity, n_piece, groups...  41.8 us
    unnamed x148, local copies, waits for them, and re-layouts  21.4 us
    pallas_call x2, Pallas kernels, weight_sums(): pl.pallas_call(functools.partial(weight_kernel, len(pieces), len(rights[0...  16.6 us
    pallas_call x5, Pallas kernels, pick(): pl.pallas_call(functools.partial(pick_kernel, capacity, n_half, blocks),...  12.1 us
    pallas_call x8, Pallas kernels, block_sum(): pl.pallas_call(functools.partial(block_kernel, capacity), grid=(width //...  10.2 us
  transfers between devices with their start and end apart: 60, of which 36 were waited for; matrix products, arithmetic and copies ran while one was open for 1% of the time, Pallas kernels for 20%

profile of v1, /device:TPU:8, one launch (start us, length us, event | category | flops | bytes accessed | tf_op | source)
XLA Modules:
  0.0 435.4 jit_solution(16025069398734821616)
XLA Ops:
  20.2 18.1 %collective-permute-done.14.refs_2_ = bf16[128,2048]{1,0:T(8,128)(2,1)S(1)} collective-permute-done((bf16[128,2048]{1,0:T(8,128)(2,1)}, bf16[128,2048]{1,0:T(8,128)(2,1)S(1)}, u32[]{:S(2)}, u32[]{:S(2)}) %collective-permute-start.14) | collective-permute-done | bytes 524320 | tf_op jit(solution)/shard_map/ppermute | solution.py:305
  42.0 11.5 %collective-permute-done.32.refs_2_ = bf16[128,2048]{1,0:T(8,128)(2,1)S(1)} collective-permute-done((bf16[128,2048]{1,0:T(8,128)(2,1)}, bf16[128,2048]{1,0:T(8,128)(2,1)S(1)}, u32[]{:S(2)}, u32[]{:S(2)}) %collective-permute-start.32) | collective-permute-done | bytes 524320 | tf_op jit(solution)/shard_map/ppermute | solution.py:305
  55.1 9.9 %collective-permute-done.33.refs_3_ = bf16[128,2048]{1,0:T(8,128)(2,1)S(1)} collective-permute-done((bf16[128,2048]{1,0:T(8,128)(2,1)}, bf16[128,2048]{1,0:T(8,128)(2,1)S(1)}, u32[]{:S(2)}, u32[]{:S(2)}) %collective-permute-start.33) | collective-permute-done | bytes 524320 | tf_op jit(solution)/shard_map/ppermute | solution.py:305
  73.5 22.5 %collective-permute-done.24.refs_3_ = bf16[128,2048]{1,0:T(8,128)(2,1)S(1)} collective-permute-done((bf16[128,2048]{1,0:T(8,128)(2,1)}, bf16[128,2048]{1,0:T(8,128)(2,1)S(1)}, u32[]{:S(2)}, u32[]{:S(2)}) %collective-permute-start.24) | collective-permute-done | bytes 524320 | tf_op jit(solution)/shard_map/ppermute | solution.py:305
  106.0 5.0 %collective-permute-done.7.refs_2_ = bf16[128,2048]{1,0:T(8,128)(2,1)S(1)} collective-permute-done((bf16[128,2048]{1,0:T(8,128)(2,1)}, bf16[128,2048]{1,0:T(8,128)(2,1)S(1)}, u32[]{:S(2)}, u32[]{:S(2)}) %collective-permute-start.7) | collective-permute-done | bytes 524320 | tf_op jit(solution)/shard_map/ppermute | solution.py:305
  112.5 9.7 %collective-permute-done.25.refs_4_ = bf16[128,2048]{1,0:T(8,128)(2,1)S(1)} collective-permute-done((bf16[128,2048]{1,0:T(8,128)(2,1)S(1)}, bf16[128,2048]{1,0:T(8,128)(2,1)S(1)}, u32[]{:S(2)}, u32[]{:S(2)}) %collective-permute-start.25) | collective-permute-done | bytes 524320 | tf_op jit(solution)/shard_map/ppermute | solution.py:305
  122.3 11.2 %collective-permute-done.26.refs_5_ = bf16[128,2048]{1,0:T(8,128)(2,1)S(1)} collective-permute-done((bf16[128,2048]{1,0:T(8,128)(2,1)S(1)}, bf16[128,2048]{1,0:T(8,128)(2,1)S(1)}, u32[]{:S(2)}, u32[]{:S(2)}) %collective-permute-start.26) | collective-permute-done | bytes 524320 | tf_op jit(solution)/shard_map/ppermute | solution.py:305
  135.2 4.6 %collective-permute-done.16.refs_4_ = bf16[128,2048]{1,0:T(8,128)(2,1)S(1)} collective-permute-done((bf16[128,2048]{1,0:T(8,128)(2,1)S(1)}, bf16[128,2048]{1,0:T(8,128)(2,1)S(1)}, u32[]{:S(2)}, u32[]{:S(2)}) %collective-permute-start.16) | collective-permute-done | bytes 524320 | tf_op jit(solution)/shard_map/ppermute | solution.py:305
  139.8 5.6 %collective-permute-done.17.refs_5_ = bf16[128,2048]{1,0:T(8,128)(2,1)S(1)} collective-permute-done((bf16[128,2048]{1,0:T(8,128)(2,1)S(1)}, bf16[128,2048]{1,0:T(8,128)(2,1)S(1)}, u32[]{:S(2)}, u32[]{:S(2)}) %collective-permute-start.17) | collective-permute-done | bytes 524320 | tf_op jit(solution)/shard_map/ppermute | solution.py:305
  154.0 10.2 %expert.7 = (bf16[128,2048]{1,0:T(8,128)(2,1)S(1)}, bf16[128,2048]{1,0:T(8,128)(2,1)S(1)}, bf16[128,2048]{1,0:T(8,128)(2,1)S(1)}, bf16[128,2048]{1,0:T(8,128)(2,...) custom-call(s32[1]{0:T(128)} %bitcast.me_ref, ...), custom_call_target="tpu_custom_call" | custom-call | flops 4831838208 | bytes 13631488 | tf_op jit(solution)/shard_map/expert/pallas_call | solution.py:164
  170.3 10.2 %expert.6 = (bf16[128,2048]{1,0:T(8,128)(2,1)S(1)}, bf16[128,2048]{1,0:T(8,128)(2,1)S(1)}, bf16[128,2048]{1,0:T(8,128)(2,1)S(1)}, bf16[128,2048]{1,0:T(8,128)(2,...) custom-call(s32[1]{0:T(128)} %bitcast.me_ref, ...), custom_call_target="tpu_custom_call" | custom-call | flops 4831838208 | bytes 13631488 | tf_op jit(solution)/shard_map/expert/pallas_call | solution.py:164
  182.8 4.3 collective-permute-done.18.refs_1_.refs_9_
  187.2 11.2 %collective-permute-done.19.refs_3_.refs_9_ = bf16[128,2048]{1,0:T(8,128)(2,1)S(1)} collective-permute-done((bf16[128,2048]{1,0:T(8,128)(2,1)S(1)}, bf16[128,2048]{1,0:T(8,128)(2,1)S(1)}, u32[]{:S(2)}, u32[]{:S(2)}) %collective-permute-start.19) | collective-permute-done | bytes 524320 | tf_op jit(solution)/shard_map/ppermute | solution.py:305
  198.4 11.0 %expert.5 = (bf16[128,2048]{1,0:T(8,128)(2,1)S(1)}, bf16[128,2048]{1,0:T(8,128)(2,1)}, bf16[128,2048]{1,0:T(8,128)(2,1)S(1)}, bf16[128,2048]{1,0:T(8,128)(2,1)S(...) custom-call(s32[1]{0:T(128)} %bitcast.me_ref, ...), custom_call_target="tpu_custom_call" | custom-call | flops 4831838208 | bytes 13631488 | tf_op jit(solution)/shard_map/expert/pallas_call | solution.py:164
  219.1 10.4 %expert.4 = (bf16[128,2048]{1,0:T(8,128)(2,1)S(1)}, bf16[128,2048]{1,0:T(8,128)(2,1)S(1)}, bf16[128,2048]{1,0:T(8,128)(2,1)S(1)}, bf16[128,2048]{1,0:T(8,128)(2,...) custom-call(s32[1]{0:T(128)} %bitcast.me_ref, ...), custom_call_target="tpu_custom_call" | custom-call | flops 4831838208 | bytes 13631488 | tf_op jit(solution)/shard_map/expert/pallas_call | solution.py:164
  242.9 6.9 %collective-permute-done.54.received = bf16[128,2048]{1,0:T(8,128)(2,1)S(1)} collective-permute-done((bf16[128,2048]{1,0:T(8,128)(2,1)S(1)}, bf16[128,2048]{1,0:T(8,128)(2,1)S(1)}, u32[]{:S(2)}, u32[]{:S(2)}) %collective-permute-start.54) | collective-permute-done | bytes 524320 | tf_op jit(solution)/shard_map/ppermute | solution.py:305
  252.4 8.6 %collective-permute-done.29.received = bf16[128,2048]{1,0:T(8,128)(2,1)S(1)} collective-permute-done((bf16[128,2048]{1,0:T(8,128)(2,1)S(1)}, bf16[128,2048]{1,0:T(8,128)(2,1)S(1)}, u32[]{:S(2)}, u32[]{:S(2)}) %collective-permute-start.29) | collective-permute-done | bytes 524320 | tf_op jit(solution)/shard_map/ppermute | solution.py:305
  264.3 7.7 %collective-permute-done.51.received = bf16[128,2048]{1,0:T(8,128)(2,1)S(1)} collective-permute-done((bf16[128,2048]{1,0:T(8,128)(2,1)S(1)}, bf16[128,2048]{1,0:T(8,128)(2,1)S(1)}, u32[]{:S(2)}, u32[]{:S(2)}) %collective-permute-start.51) | collective-permute-done | bytes 524320 | tf_op jit(solution)/shard_map/ppermute | solution.py:305
  272.8 4.8 %collective-permute-done.20.received = bf16[128,2048]{1,0:T(8,128)(2,1)S(1)} collective-permute-done((bf16[128,2048]{1,0:T(8,128)(2,1)}, bf16[128,2048]{1,0:T(8,128)(2,1)S(1)}, u32[]{:S(2)}, u32[]{:S(2)}) %collective-permute-start.20) | collective-permute-done | bytes 524320 | tf_op jit(solution)/shard_map/ppermute | solution.py:305
  278.8 4.5 %collective-permute-done.48.received = bf16[128,2048]{1,0:T(8,128)(2,1)S(1)} collective-permute-done((bf16[128,2048]{1,0:T(8,128)(2,1)S(1)}, bf16[128,2048]{1,0:T(8,128)(2,1)S(1)}, u32[]{:S(2)}, u32[]{:S(2)}) %collective-permute-start.48) | collective-permute-done | bytes 524320 | tf_op jit(solution)/shard_map/ppermute | solution.py:305
  288.8 6.7 %collective-permute-start.45 = (f32[2,2,128]{2,1,0:T(2,128)S(1)}, f32[2,2,128]{2,1,0:T(2,128)S(1)}, u32[]{:S(2)}, u32[]{:S(2)}) collective-permute-start(f32[2,2,128]{2,1,0:T(2,128)S(1)} %bitcast.112), channel_id=1, source_target_pairs={{0,12},{1,13},{2,14},{3,15},{4,8},{5,9},{6,10},{7,11},{8,4},{9,5},... | collective-permute-start | bytes 6152 | tf_op jit(solution)/shard_map/ppermute | solution.py:305
  297.1 4.4 %collective-permute-start.44 = (f32[2,2,128]{2,1,0:T(2,128)S(1)}, f32[2,2,128]{2,1,0:T(2,128)S(1)}, u32[]{:S(2)}, u32[]{:S(2)}) collective-permute-start(f32[2,2,128]{2,1,0:T(2,128)S(1)} %bitcast.111), channel_id=1, source_target_pairs={{0,8},{1,9},{2,10},{3,11},{4,12},{5,13},{6,14},{7,15},{8,0},{9,1},... | collective-permute-start | bytes 6152 | tf_op jit(solution)/shard_map/ppermute | solution.py:305
  307.2 6.7 %weight_sums.3 = (f32[2048,384]{1,0:T(8,128)S(1)}, bf16[2048,384]{1,0:T(8,128)(2,1)}) custom-call(bf16[64,2048]{1,0:T(8,128)(2,1)S(1)} %copy-done.30, bf16[64,2048]{1,0:T(8,128)(2,1)S(1)} %copy-done.41, bf16[64,2048]{1,0:T(8,128)(2,1)S(1)} %copy-done.44, bf16[64,2048]{1,0:T(8,128)(2,1)S(1)} %copy-done.46, bf16[128,2048]{1,0:T(8,128)(2,1)S(1)} %copy-done.14, ...), custom_call_target="tpu_custom_call" | custom-call | flops 3221225472 | bytes 10485760 | tf_op jit(solution)/shard_map/weight_sums/pallas_call | solution.py:275
  317.8 9.8 %collective-permute-done.52.refs_0_ = bf16[128,2048]{1,0:T(8,128)(2,1)S(1)} collective-permute-done((bf16[128,2048]{1,0:T(8,128)(2,1)S(1)}, bf16[128,2048]{1,0:T(8,128)(2,1)S(1)}, u32[]{:S(2)}, u32[]{:S(2)}) %collective-permute-start.52) | collective-permute-done | bytes 524320 | tf_op jit(solution)/shard_map/ppermute | solution.py:305
  327.6 4.8 %collective-permute-start.40 = (bf16[128,2048]{1,0:T(8,128)(2,1)}, bf16[128,2048]{1,0:T(8,128)(2,1)S(1)}, u32[]{:S(2)}, u32[]{:S(2)}) collective-permute-start(bf16[128,2048]{1,0:T(8,128)(2,1)} %block_sum.10), channel_id=1, source_target_pairs={{0,4},{1,5},{2,6},{3,7},{4,0},{5,1},{6,2},{7,3},{8,12},{9,13},{10,... | collective-permute-start | bytes 1572872 | tf_op jit(solution)/shard_map/ppermute | solution.py:305
  332.4 5.0 %collective-permute-done.49.refs_0_ = bf16[128,2048]{1,0:T(8,128)(2,1)S(1)} collective-permute-done((bf16[128,2048]{1,0:T(8,128)(2,1)S(1)}, bf16[128,2048]{1,0:T(8,128)(2,1)S(1)}, u32[]{:S(2)}, u32[]{:S(2)}) %collective-permute-start.49) | collective-permute-done | bytes 524320 | tf_op jit(solution)/shard_map/ppermute | solution.py:305
  337.3 6.3 %collective-permute-start.56 = (bf16[128,2048]{1,0:T(8,128)(2,1)S(1)}, bf16[128,2048]{1,0:T(8,128)(2,1)S(1)}, u32[]{:S(2)}, u32[]{:S(2)}) collective-permute-start(bf16[128,2048]{1,0:T(8,128)(2,1)S(1)} %block_sum.14), channel_id=1, source_target_pairs={{0,4},{1,5},{2,6},{3,7},{4,0},{5,1},{6,2},{7,3},{8,12},{9,13},{10,... | collective-permute-start | bytes 1572872 | tf_op jit(solution)/shard_map/ppermute | solution.py:305
  348.7 5.2 %collective-permute-start.22 = (bf16[128,2048]{1,0:T(8,128)(2,1)S(1)}, bf16[128,2048]{1,0:T(8,128)(2,1)}, u32[]{:S(2)}, u32[]{:S(2)}) collective-permute-start(bf16[128,2048]{1,0:T(8,128)(2,1)S(1)} %block_sum.8), channel_id=1, source_target_pairs={{0,12},{1,13},{2,14},{3,15},{4,8},{5,9},{6,10},{7,11},{8,4},{9,5},... | collective-permute-start | bytes 1572872 | tf_op jit(solution)/shard_map/ppermute | solution.py:305
  357.1 9.9 %weight_sums.2 = (f32[2048,384]{1,0:T(8,128)S(1)}, bf16[2048,384]{1,0:T(8,128)(2,1)S(1)}, f32[2048,384]{1,0:T(8,128)}, bf16[2048,384]{1,0:T(8,128)(2,1)S(1)}) custom-call(bf16[64,2048]{1,0:T(8,128)(2,1)S(1)} %get-tuple-element.62.refs_0_, bf16[64,2048]{1,0:T(8,128)(2,1)S(1)} %copy-done.32, bf16[64,2048]{1,0:T(8,128)(2,1)S(1)} %copy-done.35, ...), custom_call_target="tpu_custom_call" | custom-call | flops 6442450944 | bytes 16777216 | tf_op jit(solution)/shard_map/weight_sums/pallas_call | solution.py:275
  369.1 16.7 %collective-permute-done.31.refs_2_ = bf16[128,2048]{1,0:T(8,128)(2,1)} collective-permute-done((bf16[128,2048]{1,0:T(8,128)(2,1)S(1)}, bf16[128,2048]{1,0:T(8,128)(2,1)}, u32[]{:S(2)}, u32[]{:S(2)}) %collective-permute-start.31) | collective-permute-done | bytes 524320 | tf_op jit(solution)/shard_map/ppermute | solution.py:305
  389.3 22.4 %collective-permute-done.22.refs_1_ = bf16[128,2048]{1,0:T(8,128)(2,1)} collective-permute-done((bf16[128,2048]{1,0:T(8,128)(2,1)S(1)}, bf16[128,2048]{1,0:T(8,128)(2,1)}, u32[]{:S(2)}, u32[]{:S(2)}) %collective-permute-start.22) | collective-permute-done | bytes 524320 | tf_op jit(solution)/shard_map/ppermute | solution.py:305
  418.1 8.3 %collective-permute-done.50.refs_1_ = bf16[128,2048]{1,0:T(8,128)(2,1)S(1)} collective-permute-done((bf16[128,2048]{1,0:T(8,128)(2,1)S(1)}, bf16[128,2048]{1,0:T(8,128)(2,1)S(1)}, u32[]{:S(2)}, u32[]{:S(2)}) %collective-permute-start.50) | collective-permute-done | bytes 524320 | tf_op jit(solution)/shard_map/ppermute | solution.py:305
  (288 shorter events, 139.6 us)
Async XLA Ops:
  0.6 151.5 %collective-permute-start.5 = (bf16[3,2048,384]{2,1,0:T(8,128)(2,1)}, bf16[3,2048,384]{2,1,0:T(8,128)(2,1)}, u32[]{:S(2)}, u32[]{:S(2)}) collective-permute-start(bf16[3,2048,384]{2,1,0:T(8,128)(2,1)} %bitcast.90), channel_id=1, source_target_pairs={{0,16},{16,0},{1,17},{17,1},{2,18},{18,2},{3,19},{19,3},{4,20},{20... | collective-permute-start | bytes 14155784 | tf_op jit(solution)/shard_map/ppermute | solution.py:308
  16.0 37.6 %collective-permute-start.32 = (bf16[128,2048]{1,0:T(8,128)(2,1)}, bf16[128,2048]{1,0:T(8,128)(2,1)S(1)}, u32[]{:S(2)}, u32[]{:S(2)}) collective-permute-start(bf16[128,2048]{1,0:T(8,128)(2,1)} %refs_1_.1), channel_id=1, source_target_pairs={{0,4},{1,5},{2,6},{3,7},{4,0},{5,1},{6,2},{7,3},{8,12},{9,13},{10,... | collective-permute-start | bytes 1572872 | tf_op jit(solution)/shard_map/ppermute | solution.py:305
  19.2 45.9 %collective-permute-start.33 = (bf16[128,2048]{1,0:T(8,128)(2,1)}, bf16[128,2048]{1,0:T(8,128)(2,1)S(1)}, u32[]{:S(2)}, u32[]{:S(2)}) collective-permute-start(bf16[128,2048]{1,0:T(8,128)(2,1)} %refs_2_.1), channel_id=1, source_target_pairs={{0,4},{1,5},{2,6},{3,7},{4,0},{5,1},{6,2},{7,3},{8,12},{9,13},{10,... | collective-permute-start | bytes 1572872 | tf_op jit(solution)/shard_map/ppermute | solution.py:305
  38.3 35.2 %collective-permute-start.23 = (bf16[128,2048]{1,0:T(8,128)(2,1)}, bf16[128,2048]{1,0:T(8,128)(2,1)S(1)}, u32[]{:S(2)}, u32[]{:S(2)}) collective-permute-start(bf16[128,2048]{1,0:T(8,128)(2,1)} %refs_1_.1), channel_id=1, source_target_pairs={{0,8},{1,9},{2,10},{3,11},{4,12},{5,13},{6,14},{7,15},{8,0},{9,1},... | collective-permute-start | bytes 1572872 | tf_op jit(solution)/shard_map/ppermute | solution.py:305
  39.1 56.8 %collective-permute-start.24 = (bf16[128,2048]{1,0:T(8,128)(2,1)}, bf16[128,2048]{1,0:T(8,128)(2,1)S(1)}, u32[]{:S(2)}, u32[]{:S(2)}) collective-permute-start(bf16[128,2048]{1,0:T(8,128)(2,1)} %refs_2_.1), channel_id=1, source_target_pairs={{0,8},{1,9},{2,10},{3,11},{4,12},{5,13},{6,14},{7,15},{8,0},{9,1},... | collective-permute-start | bytes 1572872 | tf_op jit(solution)/shard_map/ppermute | solution.py:305
  53.6 43.9 %collective-permute-start.34 = (bf16[128,2048]{1,0:T(8,128)(2,1)S(1)}, bf16[128,2048]{1,0:T(8,128)(2,1)S(1)}, u32[]{:S(2)}, u32[]{:S(2)}) collective-permute-start(bf16[128,2048]{1,0:T(8,128)(2,1)S(1)} %collective-permute-done.32.refs_2_), channel_id=1, source_target_pairs={{0,2},{1,3},{2,0},{3,1},{4,6},{5,7},{6,4},{7,5},{8,10},{9,11},{10,... | collective-permute-start | bytes 1572872 | tf_op jit(solution)/shard_map/ppermute | solution.py:305
  65.0 32.9 %collective-permute-start.35 = (bf16[128,2048]{1,0:T(8,128)(2,1)S(1)}, bf16[128,2048]{1,0:T(8,128)(2,1)}, u32[]{:S(2)}, u32[]{:S(2)}) collective-permute-start(bf16[128,2048]{1,0:T(8,128)(2,1)S(1)} %collective-permute-done.33.refs_3_), channel_id=1, source_target_pairs={{0,2},{1,3},{2,0},{3,1},{4,6},{5,7},{6,4},{7,5},{8,10},{9,11},{10,... | collective-permute-start | bytes 1572872 | tf_op jit(solution)/shard_map/ppermute | solution.py:305
  98.0 35.5 %collective-permute-start.26 = (bf16[128,2048]{1,0:T(8,128)(2,1)S(1)}, bf16[128,2048]{1,0:T(8,128)(2,1)S(1)}, u32[]{:S(2)}, u32[]{:S(2)}) collective-permute-start(bf16[128,2048]{1,0:T(8,128)(2,1)S(1)} %collective-permute-done.24.refs_3_), channel_id=1, source_target_pairs={{0,2},{1,3},{2,0},{3,1},{4,6},{5,7},{6,4},{7,5},{8,10},{9,11},{10,... | collective-permute-start | bytes 1572872 | tf_op jit(solution)/shard_map/ppermute | solution.py:305
  104.5 35.3 %collective-permute-start.16 = (bf16[128,2048]{1,0:T(8,128)(2,1)S(1)}, bf16[128,2048]{1,0:T(8,128)(2,1)S(1)}, u32[]{:S(2)}, u32[]{:S(2)}) collective-permute-start(bf16[128,2048]{1,0:T(8,128)(2,1)S(1)} %collective-permute-done.14.refs_2_), channel_id=1, source_target_pairs={{0,2},{1,3},{2,0},{3,1},{4,6},{5,7},{6,4},{7,5},{8,10},{9,11},{10,... | collective-permute-start | bytes 1572872 | tf_op jit(solution)/shard_map/ppermute | solution.py:305
  111.0 34.4 %collective-permute-start.17 = (bf16[128,2048]{1,0:T(8,128)(2,1)S(1)}, bf16[128,2048]{1,0:T(8,128)(2,1)S(1)}, u32[]{:S(2)}, u32[]{:S(2)}) collective-permute-start(bf16[128,2048]{1,0:T(8,128)(2,1)S(1)} %collective-permute-done.15.refs_3_), channel_id=1, source_target_pairs={{0,2},{1,3},{2,0},{3,1},{4,6},{5,7},{6,4},{7,5},{8,10},{9,11},{10,... | collective-permute-start | bytes 1572872 | tf_op jit(solution)/shard_map/ppermute | solution.py:305
  149.9 61.8 %collective-permute-start.8 = (bf16[64,2048]{1,0:T(8,128)(2,1)}, bf16[64,2048]{1,0:T(8,128)(2,1)S(1)}, u32[]{:S(2)}, u32[]{:S(2)}) collective-permute-start(bf16[64,2048]{1,0:T(8,128)(2,1)} %get-tuple-element.64), channel_id=1, source_target_pairs={{0,1},{1,0},{2,3},{3,2},{4,5},{5,4},{6,7},{7,6},{8,9},{9,8},{10,11... | collective-permute-start | bytes 786440 | tf_op jit(solution)/shard_map/ppermute | solution.py:305
  152.0 35.2 %collective-permute-start.18 = (bf16[128,2048]{1,0:T(8,128)(2,1)S(1)}, bf16[128,2048]{1,0:T(8,128)(2,1)S(1)}, u32[]{:S(2)}, u32[]{:S(2)}) collective-permute-start(bf16[128,2048]{1,0:T(8,128)(2,1)S(1)} %get-tuple-element.73), channel_id=1, source_target_pairs={{0,1},{1,0},{2,3},{3,2},{4,5},{5,4},{6,7},{7,6},{8,9},{9,8},{10,11... | collective-permute-start | bytes 1572872 | tf_op jit(solution)/shard_map/ppermute | solution.py:305
  152.1 46.3 %collective-permute-start.19 = (bf16[128,2048]{1,0:T(8,128)(2,1)S(1)}, bf16[128,2048]{1,0:T(8,128)(2,1)S(1)}, u32[]{:S(2)}, u32[]{:S(2)}) collective-permute-start(bf16[128,2048]{1,0:T(8,128)(2,1)S(1)} %get-tuple-element.75), channel_id=1, source_target_pairs={{0,1},{1,0},{2,3},{3,2},{4,5},{5,4},{6,7},{7,6},{8,9},{9,8},{10,11... | collective-permute-start | bytes 1572872 | tf_op jit(solution)/shard_map/ppermute | solution.py:305
  166.5 45.9 %collective-permute-start.10 = (bf16[64,2048]{1,0:T(8,128)(2,1)}, bf16[64,2048]{1,0:T(8,128)(2,1)S(1)}, u32[]{:S(2)}, u32[]{:S(2)}) collective-permute-start(bf16[64,2048]{1,0:T(8,128)(2,1)} %get-tuple-element.68), channel_id=1, source_target_pairs={{0,1},{1,0},{2,3},{3,2},{4,5},{5,4},{6,7},{7,6},{8,9},{9,8},{10,11... | collective-permute-start | bytes 786440 | tf_op jit(solution)/shard_map/ppermute | solution.py:305
  170.3 42.8 %collective-permute-start.9 = (bf16[64,2048]{1,0:T(8,128)(2,1)}, bf16[64,2048]{1,0:T(8,128)(2,1)S(1)}, u32[]{:S(2)}, u32[]{:S(2)}) collective-permute-start(bf16[64,2048]{1,0:T(8,128)(2,1)} %get-tuple-element.65), channel_id=1, source_target_pairs={{0,1},{1,0},{2,3},{3,2},{4,5},{5,4},{6,7},{7,6},{8,9},{9,8},{10,11... | collective-permute-start | bytes 786440 | tf_op jit(solution)/shard_map/ppermute | solution.py:305
  198.4 44.4 %collective-permute-start.38 = (bf16[128,2048]{1,0:T(8,128)(2,1)S(1)}, bf16[128,2048]{1,0:T(8,128)(2,1)S(1)}, u32[]{:S(2)}, u32[]{:S(2)}) collective-permute-start(bf16[128,2048]{1,0:T(8,128)(2,1)S(1)} %get-tuple-element.89), channel_id=1, source_target_pairs={{0,1},{1,0},{2,3},{3,2},{4,5},{5,4},{6,7},{7,6},{8,9},{9,8},{10,11... | collective-permute-start | bytes 1572872 | tf_op jit(solution)/shard_map/ppermute | solution.py:305
  238.8 33.1 %collective-permute-start.51 = (bf16[128,2048]{1,0:T(8,128)(2,1)S(1)}, bf16[128,2048]{1,0:T(8,128)(2,1)S(1)}, u32[]{:S(2)}, u32[]{:S(2)}) collective-permute-start(bf16[128,2048]{1,0:T(8,128)(2,1)S(1)} %get-tuple-element.99), channel_id=1, source_target_pairs={{0,1},{1,0},{2,3},{3,2},{4,5},{5,4},{6,7},{7,6},{8,9},{9,8},{10,11... | collective-permute-start | bytes 1572872 | tf_op jit(solution)/shard_map/ppermute | solution.py:305
  240.8 36.7 %collective-permute-start.20 = (bf16[128,2048]{1,0:T(8,128)(2,1)}, bf16[128,2048]{1,0:T(8,128)(2,1)S(1)}, u32[]{:S(2)}, u32[]{:S(2)}) collective-permute-start(bf16[128,2048]{1,0:T(8,128)(2,1)} %get-tuple-element.77), channel_id=1, source_target_pairs={{0,1},{1,0},{2,3},{3,2},{4,5},{5,4},{6,7},{7,6},{8,9},{9,8},{10,11... | collective-permute-start | bytes 1572872 | tf_op jit(solution)/shard_map/ppermute | solution.py:305
  242.8 40.4 %collective-permute-start.48 = (bf16[128,2048]{1,0:T(8,128)(2,1)S(1)}, bf16[128,2048]{1,0:T(8,128)(2,1)S(1)}, u32[]{:S(2)}, u32[]{:S(2)}) collective-permute-start(bf16[128,2048]{1,0:T(8,128)(2,1)S(1)} %get-tuple-element.97), channel_id=1, source_target_pairs={{0,1},{1,0},{2,3},{3,2},{4,5},{5,4},{6,7},{7,6},{8,9},{9,8},{10,11... | collective-permute-start | bytes 1572872 | tf_op jit(solution)/shard_map/ppermute | solution.py:305
  249.7 39.1 %collective-permute-start.12 = (bf16[128,2048]{1,0:T(8,128)(2,1)S(1)}, bf16[128,2048]{1,0:T(8,128)(2,1)S(1)}, u32[]{:S(2)}, u32[]{:S(2)}) collective-permute-start(bf16[128,2048]{1,0:T(8,128)(2,1)S(1)} %get-tuple-element.71), channel_id=1, source_target_pairs={{0,1},{1,0},{2,3},{3,2},{4,5},{5,4},{6,7},{7,6},{8,9},{9,8},{10,11... | collective-permute-start | bytes 1572872 | tf_op jit(solution)/shard_map/ppermute | solution.py:305
  261.0 40.5 %collective-permute-start.46 = (bf16[128,2048]{1,0:T(8,128)(2,1)S(1)}, bf16[128,2048]{1,0:T(8,128)(2,1)S(1)}, u32[]{:S(2)}, u32[]{:S(2)}) collective-permute-start(bf16[128,2048]{1,0:T(8,128)(2,1)S(1)} %get-tuple-element.95), channel_id=1, source_target_pairs={{0,1},{1,0},{2,3},{3,2},{4,5},{5,4},{6,7},{7,6},{8,9},{9,8},{10,11... | collective-permute-start | bytes 1572872 | tf_op jit(solution)/shard_map/ppermute | solution.py:305
  272.0 32.3 %collective-permute-start.39 = (bf16[128,2048]{1,0:T(8,128)(2,1)S(1)}, bf16[128,2048]{1,0:T(8,128)(2,1)S(1)}, u32[]{:S(2)}, u32[]{:S(2)}) collective-permute-start(bf16[128,2048]{1,0:T(8,128)(2,1)S(1)} %partial_sum.11), channel_id=1, source_target_pairs={{0,2},{1,3},{2,0},{3,1},{4,6},{5,7},{6,4},{7,5},{8,10},{9,11},{10,... | collective-permute-start | bytes 1572872 | tf_op jit(solution)/shard_map/ppermute | solution.py:305
  304.3 33.0 %collective-permute-start.49 = (bf16[128,2048]{1,0:T(8,128)(2,1)S(1)}, bf16[128,2048]{1,0:T(8,128)(2,1)S(1)}, u32[]{:S(2)}, u32[]{:S(2)}) collective-permute-start(bf16[128,2048]{1,0:T(8,128)(2,1)S(1)} %partial_sum.13), channel_id=1, source_target_pairs={{0,2},{1,3},{2,0},{3,1},{4,6},{5,7},{6,4},{7,5},{8,10},{9,11},{10,... | collective-permute-start | bytes 1572872 | tf_op jit(solution)/shard_map/ppermute | solution.py:305
  305.1 38.5 %collective-permute-start.13 = (bf16[128,2048]{1,0:T(8,128)(2,1)S(1)}, bf16[128,2048]{1,0:T(8,128)(2,1)}, u32[]{:S(2)}, u32[]{:S(2)}) collective-permute-start(bf16[128,2048]{1,0:T(8,128)(2,1)S(1)} %partial_sum.8), channel_id=1, source_target_pairs={{0,2},{1,3},{2,0},{3,1},{4,6},{5,7},{6,4},{7,5},{8,10},{9,11},{10,... | collective-permute-start | bytes 1572872 | tf_op jit(solution)/shard_map/ppermute | solution.py:305
  306.3 42.3 %collective-permute-start.47 = (bf16[128,2048]{1,0:T(8,128)(2,1)S(1)}, bf16[128,2048]{1,0:T(8,128)(2,1)}, u32[]{:S(2)}, u32[]{:S(2)}) collective-permute-start(bf16[128,2048]{1,0:T(8,128)(2,1)S(1)} %partial_sum.12), channel_id=1, source_target_pairs={{0,2},{1,3},{2,0},{3,1},{4,6},{5,7},{6,4},{7,5},{8,10},{9,11},{10,... | collective-permute-start | bytes 1572872 | tf_op jit(solution)/shard_map/ppermute | solution.py:305
  317.0 111.8 %collective-permute-start.59 = (bf16[2048,384]{1,0:T(8,128)(2,1)}, bf16[2048,384]{1,0:T(8,128)(2,1)}, u32[]{:S(2)}, u32[]{:S(2)}) collective-permute-start(bf16[2048,384]{1,0:T(8,128)(2,1)} %get-tuple-element.119), channel_id=1, source_target_pairs={{0,16},{16,0},{1,17},{17,1},{2,18},{18,2},{3,19},{19,3},{4,20},{20... | collective-permute-start | bytes 4718600 | tf_op jit(solution)/shard_map/ppermute | solution.py:308
  327.6 39.4 %collective-permute-start.40 = (bf16[128,2048]{1,0:T(8,128)(2,1)}, bf16[128,2048]{1,0:T(8,128)(2,1)S(1)}, u32[]{:S(2)}, u32[]{:S(2)}) collective-permute-start(bf16[128,2048]{1,0:T(8,128)(2,1)} %block_sum.10), channel_id=1, source_target_pairs={{0,4},{1,5},{2,6},{3,7},{4,0},{5,1},{6,2},{7,3},{8,12},{9,13},{10,... | collective-permute-start | bytes 1572872 | tf_op jit(solution)/shard_map/ppermute | solution.py:305
  343.6 42.2 %collective-permute-start.31 = (bf16[128,2048]{1,0:T(8,128)(2,1)S(1)}, bf16[128,2048]{1,0:T(8,128)(2,1)}, u32[]{:S(2)}, u32[]{:S(2)}) collective-permute-start(bf16[128,2048]{1,0:T(8,128)(2,1)S(1)} %block_sum.9), channel_id=1, source_target_pairs={{0,8},{1,9},{2,10},{3,11},{4,12},{5,13},{6,14},{7,15},{8,0},{9,1},... | collective-permute-start | bytes 1572872 | tf_op jit(solution)/shard_map/ppermute | solution.py:305
  348.7 63.1 %collective-permute-start.22 = (bf16[128,2048]{1,0:T(8,128)(2,1)S(1)}, bf16[128,2048]{1,0:T(8,128)(2,1)}, u32[]{:S(2)}, u32[]{:S(2)}) collective-permute-start(bf16[128,2048]{1,0:T(8,128)(2,1)S(1)} %block_sum.8), channel_id=1, source_target_pairs={{0,12},{1,13},{2,14},{3,15},{4,8},{5,9},{6,10},{7,11},{8,4},{9,5},... | collective-permute-start | bytes 1572872 | tf_op jit(solution)/shard_map/ppermute | solution.py:305
  367.0 63.6 %collective-permute-start.57 = (bf16[2048,384]{1,0:T(8,128)(2,1)S(1)}, bf16[2048,384]{1,0:T(8,128)(2,1)S(1)}, u32[]{:S(2)}, u32[]{:S(2)}) collective-permute-start(bf16[2048,384]{1,0:T(8,128)(2,1)S(1)} %get-tuple-element.111), channel_id=1, source_target_pairs={{0,16},{16,0},{1,17},{17,1},{2,18},{18,2},{3,19},{19,3},{4,20},{20... | collective-permute-start | bytes 4718600 | tf_op jit(solution)/shard_map/ppermute | solution.py:308
  368.6 62.4 %collective-permute-start.58 = (bf16[2048,384]{1,0:T(8,128)(2,1)S(1)}, bf16[2048,384]{1,0:T(8,128)(2,1)S(1)}, u32[]{:S(2)}, u32[]{:S(2)}) collective-permute-start(bf16[2048,384]{1,0:T(8,128)(2,1)S(1)} %get-tuple-element.113), channel_id=1, source_target_pairs={{0,16},{16,0},{1,17},{17,1},{2,18},{18,2},{3,19},{19,3},{4,20},{20... | collective-permute-start | bytes 4718600 | tf_op jit(solution)/shard_map/ppermute | solution.py:308
  385.9 32.2 %collective-permute-start.53 = (bf16[128,2048]{1,0:T(8,128)(2,1)S(1)}, bf16[128,2048]{1,0:T(8,128)(2,1)S(1)}, u32[]{:S(2)}, u32[]{:S(2)}) collective-permute-start(bf16[128,2048]{1,0:T(8,128)(2,1)S(1)} %block_sum.13), channel_id=1, source_target_pairs={{0,8},{1,9},{2,10},{3,11},{4,12},{5,13},{6,14},{7,15},{8,0},{9,1},... | collective-permute-start | bytes 1572872 | tf_op jit(solution)/shard_map/ppermute | solution.py:305
  (102 other events, 2337.4 us)

commit v2 on v0

v2 whole, which is shorter than its diff:
```python
import functools

import jax
import jax.numpy as jnp
from jax import lax
from jax.experimental import pallas as pl
from jax.experimental.pallas import tpu as pltpu
from jax.sharding import PartitionSpec as P

F32 = jnp.float32
BF16 = jnp.bfloat16
MIB = 1 << 20
CHUNKS = 4
HBM = pl.BlockSpec(memory_space=pl.ANY)
WHOLE = pl.BlockSpec(memory_space=pltpu.VMEM)
SCALAR = pl.BlockSpec(memory_space=pltpu.SMEM)


def mask_of(table, expert, capacity):
    top = table.shape[0] // 2
    tokens = table.shape[1]
    wanted = (expert * capacity + lax.broadcasted_iota(jnp.int32, (capacity, tokens), 0)).astype(F32)
    hit = jnp.zeros((capacity, tokens), F32)
    for k in range(top):
        hit = hit + jnp.where(table[k : k + 1] == wanted, 1.0, 0.0)
    return hit


def gate_column(table, expert, capacity):
    top = table.shape[0] // 2
    tokens = table.shape[1]
    wanted = (expert * capacity + lax.broadcasted_iota(jnp.int32, (capacity, tokens), 0)).astype(F32)
    gate = jnp.zeros((capacity, tokens), F32)
    for k in range(top):
        gate = gate + jnp.where(table[k : k + 1] == wanted, table[top + k : top + k + 1], 0.0)
    return jnp.sum(gate, axis=1, keepdims=True)


def pick_kernel(capacity, flip, blocks, n_deps, me_ref, *refs):
    tables, arrays = refs[:2], refs[2:4]
    own, sent = refs[4 + n_deps :]
    me = me_ref[0]
    for expert, out in ((me ^ flip, sent), (me, own)):
        for half in range(2):
            for b in range(blocks):
                mask = mask_of(tables[half][b], expert, capacity).astype(BF16)
                tokens = mask.shape[1]
                row = (half * blocks + b) * capacity
                source = arrays[half][b * tokens : (b + 1) * tokens, :]
                out[row : row + capacity, :] = jnp.dot(
                    mask, source, preferred_element_type=F32
                ).astype(BF16)


def pick(me, flip, capacity, tables, here, there, deps=()):
    blocks = tables[0].shape[0]
    in_rows, width = here.shape
    tile = 1024
    rows = 2 * blocks * capacity
    table_spec = pl.BlockSpec(tables[0].shape, lambda i: (0, 0, 0))
    in_spec = pl.BlockSpec((in_rows, tile), lambda i: (0, i))
    out_spec = pl.BlockSpec((rows, tile), lambda i: (0, i))
    return pl.pallas_call(
        functools.partial(pick_kernel, capacity, flip, blocks, len(deps)),
        grid=(width // tile,),
        in_specs=[SCALAR, table_spec, table_spec, in_spec, in_spec] + [HBM] * len(deps),
        out_specs=[out_spec] * 2,
        out_shape=[jax.ShapeDtypeStruct((rows, width), BF16)] * 2,
        compiler_params=pltpu.CompilerParams(vmem_limit_bytes=24 * MIB),
        cost_estimate=pl.CostEstimate(
            flops=8 * capacity * in_rows * width,
            bytes_accessed=4 * (in_rows + rows) * width,
            transcendentals=0,
        ),
        name="pick",
    )(me, *tables, here, there, *deps)


def expert_kernel(capacity, n_deps, me_ref, tables, weights, *refs):
    own_t, got_t, own_g, got_g = refs[:4]
    (out_own, out_sent, back_own, back_sent, gate_rows, act_out, dgate_out, dup_out) = refs[
        4 + n_deps : 12 + n_deps
    ]
    (w, x, g, gate_up, act_ref, dgate_ref, dup_ref, out, back, row_sem, w_sem, out_sem) = refs[
        12 + n_deps :
    ]
    half = weights.shape[3]
    hidden = 2 * half
    rows, width = x.shape
    side, quarter = rows // 2, rows // 4

    def started(source, target, sem):
        copy = pltpu.make_async_copy(source, target, sem)
        copy.start()
        return copy

    def row_quarters(q):
        return pl.ds(q * quarter, quarter)

    first, second = pl.ds(0, side), pl.ds(side, side)
    x_copies = [
        started(own_t, x.at[first], row_sem.at[0]),
        started(got_t, x.at[second], row_sem.at[1]),
    ]
    w_copies = [
        [started(weights.at[j, i], w.at[i, :, pl.ds(j * half, half)], w_sem.at[i, j]) for j in (0, 1)]
        for i in (0, 1)
    ]
    g_copies = [
        started(own_g.at[row_quarters(0)], g.at[row_quarters(0)], row_sem.at[2]),
        started(got_g.at[row_quarters(0)], g.at[row_quarters(1)], row_sem.at[3]),
        started(own_g.at[row_quarters(1)], g.at[row_quarters(2)], row_sem.at[4]),
        started(got_g.at[row_quarters(1)], g.at[row_quarters(3)], row_sem.at[5]),
    ]
    w_copies.append(
        [started(weights.at[j, 2], w.at[2, :, pl.ds(j * half, half)], w_sem.at[2, j]) for j in (0, 1)]
    )
    me = me_ref[0]
    groups = tables.shape[0]
    gates = jnp.concatenate(
        [gate_column(tables[i], me, capacity) for i in range(groups)], axis=0
    )
    step = 256

    def pre(i):
        def tile(n, carry):
            cols = pl.ds(pl.multiple_of(n * step, step), step)
            gate_up[i, :, cols] = jnp.dot(x[...], w[i, :, cols], preferred_element_type=F32)
            return carry

        lax.fori_loop(0, hidden // step, tile, 0, unroll=True)

    for copy in x_copies + w_copies[0]:
        copy.wait()
    pre(0)
    for copy in w_copies[1]:
        copy.wait()
    pre(1)
    for copy in g_copies + w_copies[2]:
        copy.wait()

    def hidden_tile(n, total):
        cols = pl.ds(pl.multiple_of(n * step, step), step)
        gate_pre, up_pre = gate_up[0, :, cols], gate_up[1, :, cols]
        pulled = jnp.dot(g[...], w[2, :, cols], preferred_element_type=F32)
        sig = jax.nn.sigmoid(gate_pre)
        silu = gate_pre * sig
        act = silu * up_pre
        grad_act = pulled * gates
        act_ref[:, cols] = (act * gates).astype(BF16)
        dgate_ref[:, cols] = (grad_act * up_pre * sig * (1.0 + gate_pre * (1.0 - sig))).astype(BF16)
        dup_ref[:, cols] = (grad_act * silu).astype(BF16)
        return total + jnp.sum(act * pulled, axis=1, keepdims=True)

    total = lax.fori_loop(0, hidden // step, hidden_tile, jnp.zeros((rows, 1), F32), unroll=True)
    copies = [
        started(act_ref, act_out, out_sem.at[0]),
        started(dgate_ref, dgate_out, out_sem.at[1]),
        started(dup_ref, dup_out, out_sem.at[2]),
    ]
    for i in range(groups):
        mask = mask_of(tables[i], me, capacity)
        gate_rows[i : i + 1, :] = jnp.sum(
            mask * total[i * capacity : (i + 1) * capacity], axis=0, keepdims=True
        )
    nt = (((1,), (1,)), ((), ()))

    def out_tile(n, carry):
        cols = pl.ds(pl.multiple_of(n * step, step), step)
        out[:, cols] = lax.dot_general(
            act_ref[...], w[2, cols, :], nt, preferred_element_type=F32
        ).astype(BF16)
        return carry

    def back_tile(n, carry):
        cols = pl.ds(pl.multiple_of(n * step, step), step)
        total = lax.dot_general(dgate_ref[...], w[0, cols, :], nt, preferred_element_type=F32)
        total += lax.dot_general(dup_ref[...], w[1, cols, :], nt, preferred_element_type=F32)
        back[:, cols] = total.astype(BF16)
        return carry

    lax.fori_loop(0, width // step, out_tile, 0, unroll=True)
    copies += [
        started(out.at[first], out_own, out_sem.at[3]),
        started(out.at[second], out_sent, out_sem.at[4]),
    ]
    lax.fori_loop(0, width // step, back_tile, 0, unroll=True)
    copies += [
        started(back.at[row_quarters(0)], back_own.at[row_quarters(0)], out_sem.at[5]),
        started(back.at[row_quarters(1)], back_sent.at[row_quarters(0)], out_sem.at[6]),
        started(back.at[row_quarters(2)], back_own.at[row_quarters(1)], out_sem.at[7]),
        started(back.at[row_quarters(3)], back_sent.at[row_quarters(1)], out_sem.at[8]),
    ]
    for copy in copies:
        copy.wait()


def expert(me, capacity, tables, weights, own_t, got_t, own_g, got_g, deps=()):
    rows, width = 2 * own_t.shape[0], own_t.shape[1]
    hidden = 2 * weights.shape[3]
    groups, _, tokens = tables.shape
    return pl.pallas_call(
        functools.partial(expert_kernel, capacity, len(deps)),
        in_specs=[SCALAR, WHOLE, HBM] + [HBM] * 4 + [HBM] * len(deps),
        out_specs=[HBM] * 4 + [WHOLE] + [HBM] * 3,
        out_shape=[jax.ShapeDtypeStruct((rows // 2, width), BF16)] * 4
        + [jax.ShapeDtypeStruct((groups, tokens), F32)]
        + [jax.ShapeDtypeStruct((rows, hidden), BF16)] * 3,
        scratch_shapes=[
            pltpu.VMEM((3, width, hidden), BF16),
            pltpu.VMEM((rows, width), BF16),
            pltpu.VMEM((rows, width), BF16),
            pltpu.VMEM((2, rows, hidden), F32),
            pltpu.VMEM((rows, hidden), BF16),
            pltpu.VMEM((rows, hidden), BF16),
            pltpu.VMEM((rows, hidden), BF16),
            pltpu.VMEM((rows, width), BF16),
            pltpu.VMEM((rows, width), BF16),
            pltpu.SemaphoreType.DMA((6,)),
            pltpu.SemaphoreType.DMA((3, 2)),
            pltpu.SemaphoreType.DMA((9,)),
        ],
        compiler_params=pltpu.CompilerParams(vmem_limit_bytes=60 * MIB),
        cost_estimate=pl.CostEstimate(
            flops=12 * rows * width * hidden,
            bytes_accessed=24 * width * hidden,
            transcendentals=rows * hidden,
        ),
        name="expert",
    )(me, tables, weights, own_t, got_t, own_g, got_g, *deps)


def sum_kernel(capacity, flip, n_other, n_deps, me_ref, tables, own, received, *refs):
    others, out = refs[:n_other], refs[n_other + n_deps]
    blocks, _, tokens = tables.shape
    me = me_ref[0]
    for b in range(blocks):
        here = slice(b * tokens, (b + 1) * tokens)
        slots = slice(b * capacity, (b + 1) * capacity)
        mask = jnp.concatenate(
            [mask_of(tables[b], me, capacity), mask_of(tables[b], me ^ flip, capacity)], axis=0
        )
        rows = jnp.concatenate([own[slots, :], received[slots, :]], axis=0)
        total = jnp.dot(mask.T.astype(BF16), rows, preferred_element_type=F32)
        for other in others:
            total = total + other[here, :].astype(F32)
        out[here, :] = total.astype(BF16)


def token_sum(me, flip, capacity, tables, own, received, half, others=(), deps=()):
    blocks, _, tokens = tables.shape
    width = own.shape[1]
    tile = 1024
    row_spec = pl.BlockSpec((blocks * capacity, tile), lambda i: (half, i))
    sum_spec = pl.BlockSpec((blocks * tokens, tile), lambda i: (0, i))
    return pl.pallas_call(
        functools.partial(sum_kernel, capacity, flip, len(others), len(deps)),
        grid=(width // tile,),
        in_specs=[SCALAR, pl.BlockSpec(tables.shape, lambda i: (0, 0, 0)), row_spec, row_spec]
        + [sum_spec] * len(others)
        + [HBM] * len(deps),
        out_specs=sum_spec,
        out_shape=jax.ShapeDtypeStruct((blocks * tokens, width), BF16),
        compiler_params=pltpu.CompilerParams(vmem_limit_bytes=24 * MIB),
        cost_estimate=pl.CostEstimate(
            flops=4 * blocks * tokens * capacity * width,
            bytes_accessed=2 * blocks * (tokens * (1 + len(others)) + 2 * capacity) * width,
            transcendentals=0,
        ),
        name="token_sum",
    )(me, tables, own, received, *others, *deps)


def pair_kernel(capacity, n_more, me_ref, tables, *refs):
    mores, outs = refs[6 : 6 + 2 * n_more], refs[6 + 2 * n_more :]
    blocks, _, tokens = tables.shape
    me = me_ref[0]
    for b in range(blocks):
        here = slice(b * tokens, (b + 1) * tokens)
        slots = slice(b * capacity, (b + 1) * capacity)
        mine = mask_of(tables[b], me, capacity)
        for a, flip in ((0, 1), (1, 2)):
            own, got, part = refs[3 * a : 3 * a + 3]
            mask = jnp.concatenate([mine, mask_of(tables[b], me ^ flip, capacity)], axis=0)
            rows = jnp.concatenate([own[slots, :], got[slots, :]], axis=0)
            total = jnp.dot(mask.T.astype(BF16), rows, preferred_element_type=F32)
            total = total + part[here, :].astype(F32)
            for more in mores[a::2]:
                total = total + more[here, :].astype(F32)
            if len(outs) == 1:
                outs[0][a, here, :] = total.astype(BF16)
            else:
                outs[a][here, :] = total.astype(BF16)


def pair_sum(me, capacity, tables, out, back, mores=(), split=False):
    blocks, _, tokens = tables.shape
    width = out[0].shape[1]
    tile = 512
    rows = blocks * tokens
    row_spec = pl.BlockSpec((blocks * capacity, tile), lambda i: (0, i))
    sum_spec = pl.BlockSpec((rows, tile), lambda i: (0, i))
    pair_spec = pl.BlockSpec((2, rows, tile), lambda i: (0, 0, i))
    single = jax.ShapeDtypeStruct((rows, width), BF16)
    half_specs = [pl.BlockSpec((None, rows, tile), lambda i, a=a: (a, 0, i)) for a in range(2)]
    mores = [
        (m, [sum_spec] * 2) if isinstance(m, (list, tuple)) else ((m, m), half_specs) for m in mores
    ]
    result = pl.pallas_call(
        functools.partial(pair_kernel, capacity, len(mores)),
        grid=(width // tile,),
        in_specs=[SCALAR, pl.BlockSpec(tables.shape, lambda i: (0, 0, 0))]
        + [row_spec, row_spec, sum_spec] * 2
        + [s for _, specs in mores for s in specs],
        out_specs=[sum_spec] * 2 if split else pair_spec,
        out_shape=[single] * 2 if split else jax.ShapeDtypeStruct((2, rows, width), BF16),
        compiler_params=pltpu.CompilerParams(vmem_limit_bytes=24 * MIB),
        cost_estimate=pl.CostEstimate(
            flops=8 * rows * capacity * width,
            bytes_accessed=4 * blocks * (tokens * (2 + len(mores)) + 2 * capacity) * width,
            transcendentals=0,
        ),
        name="pair_sum",
    )(me, tables, *out, *back, *[m for pair, _ in mores for m in pair])
    return result


def weight_kernel(n_chunk, n_out, reorder, n_held, me_ref, *refs):
    left = jnp.concatenate([r[...] for r in refs[: 2 * n_chunk]], axis=0)
    rights = refs[2 * n_chunk : (2 + n_out) * n_chunk]
    own, other = refs[(2 + n_out) * n_chunk + n_held :]
    lower = me_ref[1] == 0
    tn = (((0,), (0,)), ((), ()))
    for i in range(n_out):
        parts = []
        for r in rights[i * n_chunk : (i + 1) * n_chunk]:
            quarter = r.shape[0] // 4
            for q in (0, 2, 1, 3) if reorder else range(4):
                parts.append(r[q * quarter : (q + 1) * quarter, :])
        right = jnp.concatenate(parts, axis=0)
        total = lax.dot_general(left, right, tn, preferred_element_type=F32)
        half = total.shape[1] // 2
        own[i] = jnp.where(lower, total[:, :half], total[:, half:])
        other[i] = jnp.where(lower, total[:, half:], total[:, :half]).astype(BF16)


def weight_sums(me, pieces, rights, reorder, at, before=()):
    width = pieces[0].shape[1]
    hidden = rights[0][0].shape[1]
    rows = sum(p.shape[0] for p in pieces)
    tile = 256
    n_out = len(rights)
    flat = [r for group in rights for r in group]
    n_in = 1 + len(pieces) + len(flat)
    return pl.pallas_call(
        functools.partial(weight_kernel, len(rights[0]), n_out, reorder, len(before)),
        grid=(width // tile,),
        in_specs=[SCALAR]
        + [pl.BlockSpec((p.shape[0], tile), lambda i: (0, i)) for p in pieces]
        + [pl.BlockSpec(r.shape, lambda i: (0, 0)) for r in flat]
        + [HBM] * len(before),
        out_specs=[pl.BlockSpec((n_out, tile, hidden // 2), lambda i: (at // n_out, i, 0))] * 2,
        out_shape=[
            jax.ShapeDtypeStruct((3, width, hidden // 2), F32),
            jax.ShapeDtypeStruct((3, width, hidden // 2), BF16),
        ],
        input_output_aliases={n_in + i: i for i in range(len(before))},
        compiler_params=pltpu.CompilerParams(vmem_limit_bytes=60 * MIB),
        cost_estimate=pl.CostEstimate(
            flops=2 * rows * width * hidden * n_out,
            bytes_accessed=n_out * 20 * width * hidden,
            transcendentals=0,
        ),
        name="weight_sums",
    )(me, *pieces, *flat, *before)


class Held(dict):
    def fence(self):
        names = list(self)
        for name, value in zip(names, lax.optimization_barrier([self[n] for n in names])):
            self[name] = value


def after(array, *deps):
    return lax.optimization_barrier((array, *deps))[0]


def local(tokens, gates, expert_ids, slots, grad_out, expert_weights):
    n_expert = lax.axis_size("expert")
    tok_count, top_count = expert_ids.shape
    capacity = tok_count * top_count // n_expert
    depth = n_expert // 4
    many = depth // CHUNKS
    FLIP_X, FLIP_Y, FLIP_NEAR, FLIP_FAR = 1, 2, 4 * many, 8 * many

    def swap(array, flip):
        return lax.ppermute(array, "expert", [(i, i ^ flip) for i in range(n_expert)])

    def swap_dp(array):
        return lax.ppermute(array, "dp", [(0, 1), (1, 0)])

    def gathered(block):
        parts = [block] + [swap(block, 4 * r) for r in range(1, many)]
        return parts[0] if many == 1 else jnp.concatenate(parts, axis=0)

    index = lax.axis_index("expert").astype(jnp.int32)
    me = jnp.stack([index, lax.axis_index("dp").astype(jnp.int32)])
    held = Held()
    weights = lax.all_gather(expert_weights[0], "dp", axis=0, tiled=False)

    here_t, here_g = gathered(tokens), gathered(grad_out)
    held["t", 0], held["g", 0] = here_t, here_g
    near_t, near_g = swap(here_t, FLIP_NEAR), swap(here_g, FLIP_NEAR)
    far_t = swap(here_t, FLIP_FAR)

    key = jnp.where(slots >= 0, expert_ids * capacity + slots, -1)
    table = jnp.concatenate([key.T.astype(F32), gates.T], axis=0)
    held["tab"] = jnp.stack([table] + [swap(table, 4 * r) for r in range(1, many)])

    def table_of(c, which):
        return held["tabs"][which] if c == 0 else held["near tabs"][which] if c == 1 else (
            held["far tabs"][c - 2, which]
        )

    def send_full(c):
        held["t there", c] = swap(held["t", c], FLIP_Y)
        held["g there", c] = swap(held["g", c], FLIP_X)

    def pick_rows(c):
        here = table_of(c, 0)
        held["t own", c], sent_t = pick(
            me, FLIP_X, capacity, (here, table_of(c, 1)), held["t", c], held["t there", c]
        )
        held["g own", c], sent_g = pick(
            me, FLIP_Y, capacity, (here, table_of(c, 2)), held["g", c], held["g there", c]
        )
        held["t got", c] = swap(sent_t, FLIP_X)
        held["g got", c] = swap(sent_g, FLIP_Y)
        return sent_t, sent_g

    def run_expert(c):
        tables = jnp.concatenate([table_of(c, i) for i in range(3)] + [held["diagonal", c]])
        names = ("out own", "out sent", "back own", "back sent", "sums", "act", "dgate", "dup")
        rows = [held[n, c] for n in ("t own", "t got", "g own", "g got")]
        for name, value in zip(names, expert(me, capacity, tables, held["weights"], *rows)):
            held[name, c] = value

    def send_rows(c):
        held["out got", c] = swap(held["out sent", c], FLIP_X)
        held["back got", c] = swap(held["back sent", c], FLIP_Y)

    def sum_there(c):
        return (
            token_sum(me, FLIP_X, capacity, table_of(c, 1), held["out own", c], held["out got", c], 1),
            token_sum(me, FLIP_Y, capacity, table_of(c, 2), held["back own", c], held["back got", c], 1),
        )

    def send_parts(c, part_t, part_g):
        held["out part", c] = swap(part_t, FLIP_Y)
        held["back part", c] = swap(part_g, FLIP_X)

    def sum_here(c, mores=(), split=False):
        out, back = ([held[n + k, c] for k in (" own", " got", " part")] for n in ("out", "back"))
        return pair_sum(me, capacity, table_of(c, 0), out, back, mores, split)

    def sum_weights(left, names, reorder, at, before=()):
        pieces = [held[left + which, c] for c in range(CHUNKS) for which in (" own", " got")]
        rights = [[held[n, c] for c in range(CHUNKS)] for n in names]
        return weight_sums(me, pieces, rights, reorder, at, before)

    send_full(0)
    tab_x, tab_y = swap(held["tab"], FLIP_X), swap(held["tab"], FLIP_Y)
    held["tabs"] = jnp.stack([held["tab"], tab_y, tab_x])
    held.fence()
    sent = pick_rows(0)
    far_g = swap(after(here_g, near_t, near_g, far_t, *sent), FLIP_FAR)
    last_t, last_g = swap(after(far_t, near_t, near_g), FLIP_NEAR), swap(far_g, FLIP_NEAR)
    held["diagonal", 0] = swap(held["tabs"][1], FLIP_X)
    near_tabs = swap(held["tabs"], FLIP_NEAR)
    held["weights"] = weights
    held["t", 1], held["g", 1] = near_t, near_g
    held.fence()
    send_full(1)
    run_expert(0)
    held["near tabs"] = near_tabs
    held.fence()
    pick_rows(1)
    arrived = held["t got", 1], held["g got", 1]
    held["t", 2], held["g", 2] = after(far_t, *arrived), after(far_g, *arrived)
    send_full(2)
    held["t", 3], held["g", 3] = last_t, last_g
    held["diagonal", 1] = swap(held["near tabs"][1], FLIP_X)
    held["far tabs"] = swap(jnp.stack([held["tabs"], held["near tabs"]]), FLIP_FAR)
    held.fence()
    send_full(3)
    pick_rows(2)
    run_expert(1)
    diagonal = swap(held["far tabs"][:, 1], FLIP_X)
    held["diagonal", 2], held["diagonal", 3] = diagonal[0], diagonal[1]
    held.fence()
    pick_rows(3)
    run_expert(2)
    held.fence()
    send_rows(2)
    run_expert(3)
    held.fence()
    send_rows(3)
    held["part 2"] = sum_there(2)
    held.fence()
    held["weight sums"] = sum_weights("g", ["act"], True, 2)
    send_parts(3, *sum_there(3))
    sums = jnp.stack([held["sums", c] for c in range(CHUNKS)])
    sums = sums.reshape(CHUNKS, 2, 2, many, tok_count)
    held["sums"] = sums[:, 0], swap(sums[:, 1], FLIP_X)
    held.fence()
    held["weight sums"] = sum_weights("t", ["dgate", "dup"], False, 0, held["weight sums"])
    send_parts(2, *held["part 2"])
    send_rows(1)
    last = swap(sum_here(3), FLIP_NEAR)
    held["sum 2"] = sum_here(2, [last], True)
    sums = jnp.stack(held["sums"])
    held["sums"] = sums[:, :, 0], swap(sums[:, :, 1], FLIP_Y)
    held.fence()
    held["far t"] = swap(held["sum 2"][0], FLIP_FAR)
    send_parts(1, *sum_there(1))
    held["weights got"] = swap_dp(held["weight sums"][1])
    sums = jnp.stack(held["sums"])
    even = jnp.stack([sums[:, :, 0], sums[:, :, 2]])
    held["sums"] = even, swap(jnp.stack([sums[:, :, 1], sums[:, :, 3]]), FLIP_NEAR)
    held.fence()
    held["far g"] = swap(held["sum 2"][1], FLIP_FAR)
    held["near"] = swap(sum_here(1), FLIP_NEAR)
    send_rows(0)
    send_parts(0, *sum_there(0))
    weight_grads = held["weight sums"][0] + held["weights got"].astype(F32)
    held["weight grads"] = weight_grads.astype(BF16)[None]
    even, odd = held["sums"]
    held["sums"] = even[0], odd[0], swap(jnp.stack([even[1], odd[1]]), FLIP_FAR)
    held.fence()
    far = [held["far t"], held["far g"]]
    total_t, total_g = sum_here(0, [held["near"], far], True)
    here, near, far = held["sums"]
    sums = jnp.stack([here, near, far[0], far[1]])
    parts = [sums[:, :, :, 0]] + [swap(sums[:, :, :, r], 4 * r) for r in range(1, many)]
    sums = jnp.stack(parts, axis=1).reshape(n_expert, tok_count)
    source = jnp.arange(n_expert, dtype=jnp.int32) ^ index
    hit = (expert_ids[:, :, None] == source[None, None, :]) & (slots >= 0)[:, :, None]
    gate_grads = jnp.sum(jnp.where(hit, sums.T[:, None, :], 0.0), axis=2)

    def scattered(total):
        if many == 1:
            return total
        parts = [total[r * tok_count : (r + 1) * tok_count] for r in range(many)]
        result = parts[0].astype(F32)
        for r in range(1, many):
            result = result + swap(parts[r], 4 * r).astype(F32)
        return result.astype(BF16)

    return (
        scattered(total_t),
        gate_grads,
        scattered(total_g),
        held["weight grads"],
    )


def solution(mesh):
    placed = (
        P(("dp", "expert"), None),
        P(("dp", "expert"), None),
        P(("dp", "expert"), None),
        P(("dp", "expert"), None),
        P(("dp", "expert"), None),
        P("expert", None, None, "dp"),
    )
    return jax.shard_map(
        local,
        mesh=mesh,
        in_specs=placed,
        out_specs=(
            P(("dp", "expert"), None),
            P(("dp", "expert"), None),
            P(("dp", "expert"), None),
            P("expert", None, None, "dp"),
        ),
        check_vma=False,
    )
```

time: 497 us -> 292 us (0.59)
  waiting for transfers between devices: 288 us -> 85.2 us
  Pallas kernels: 0 us -> 103 us
  matrix products: 71.3 us -> 0 us
  local copies, waits for them, and re-layouts: 57.3 us -> 11.1 us
  starting transfers between devices: 32.6 us -> 61.5 us
  other arithmetic: 25.5 us -> 11.5 us
    all_to_all x4 -> x0, waiting for transfers between devices: 287 us -> none  [the longest x1 75.9 us: local(): lax.all_to_all(results, 'expert', split_axis=0, concat_axis=0, tiled=True)]
    pallas_call x0 -> x26, Pallas kernels: none -> 103 us  [the longest x4 43.6 us: expert(): pl.pallas_call(functools.partial(expert_kernel, capacity, len(deps)), in_...]
    ppermute x0 -> x54, waiting for transfers between devices: none -> 84.5 us  [the longest x53 84.5 us: swap(): lax.ppermute(array, 'expert', [(i, i ^ flip) for i in range(n_expert)])]
    dot_general x11 -> x0, matrix products: 71.3 us -> none  [the longest x3 21.8 us: contract_last(): lax.dot_general(left, right, (((1,), (1,)), ((), ())), preferred_element_...]
    ppermute x0 -> x54, starting transfers between devices: none -> 61.4 us  [the longest x53 61.4 us: swap(): lax.ppermute(array, 'expert', [(i, i ^ flip) for i in range(n_expert)])]
    gather x4 -> x0, local copies, waits for them, and re-layouts: 35.2 us -> none  [the longest x1 11.6 us: local(): jnp.concatenate([back_out, padding], 0)[target]]
    all_to_all x4 -> x0, starting transfers between devices: 32.3 us -> none  [the longest x1 8.94 us: local(): lax.all_to_all(send_grads, 'expert', split_axis=0, concat_axis=0, tiled=T...]
    convert_element_type x2 -> x1, other arithmetic: 12.2 us -> 0.01 us  [local(): table = jnp.concatenate([key.T.astype(F32), gates.T], axis=0)]
  transfers between devices with their start and end apart: 6 -> 55, of which waited for: 4 -> 16; matrix products, arithmetic and copies ran while one was open for 21% -> 4% of each run, Pallas kernels for 0% -> 32%
where the time goes in v2:
time: 292 us; the launch traced here: 287 us
  Pallas kernels  103 us (35%)
  waiting for transfers between devices  85.2 us (29%)
  starting transfers between devices  61.5 us (21%)
  between operations  14.8 us (5%)
  other arithmetic  11.5 us (4%)
  local copies, waits for them, and re-layouts  11.1 us (4%)
    ppermute x53, waiting for transfers between devices, swap(): lax.ppermute(array, 'expert', [(i, i ^ flip) for i in range(n_expert)])  84.5 us
    ppermute x53, starting transfers between devices, swap(): lax.ppermute(array, 'expert', [(i, i ^ flip) for i in range(n_expert)])  61.4 us
    pallas_call x4, Pallas kernels, expert(): pl.pallas_call(functools.partial(expert_kernel, capacity, len(deps)), in_...  43.6 us
    pallas_call x2, Pallas kernels, weight_sums(): pl.pallas_call(functools.partial(weight_kernel, len(rights[0]), n_out, re...  22.8 us
    pallas_call x4, Pallas kernels, pair_sum(): pl.pallas_call(functools.partial(pair_kernel, capacity, len(mores)), grid...  13.3 us
    pallas_call x8, Pallas kernels, pick(): pl.pallas_call(functools.partial(pick_kernel, capacity, flip, blocks, len...  12.2 us
    pallas_call x8, Pallas kernels, token_sum(): pl.pallas_call(functools.partial(sum_kernel, capacity, flip, len(others),...  11.1 us
    unnamed x90, local copies, waits for them, and re-layouts  11 us
  transfers between devices with their start and end apart: 55, of which 16 were waited for; matrix products, arithmetic and copies ran while one was open for 4% of the time, Pallas kernels for 32%

profile of v2, /device:TPU:8, one launch (start us, length us, event | category | flops | bytes accessed | tf_op | source)
XLA Modules:
  0.0 287.1 jit_solution(5796186742640332555)
XLA Ops:
  12.5 10.7 %collective-permute-done.3 = f32[1,16,128]{2,1,0:T(8,128)S(1)} collective-permute-done((f32[1,16,128]{2,1,0:T(8,128)S(1)}, f32[1,16,128]{2,1,0:T(8,128)S(1)}, u32[]{:S(2)}, u32[]{:S(2)}) %collective-permute-start.3) | collective-permute-done | bytes 8224 | tf_op jit(solution)/shard_map/ppermute | solution.py:398
  23.7 2.6 collective-permute-start.14
  33.6 11.6 %collective-permute-done.8.refs_2_ = bf16[128,2048]{1,0:T(8,128)(2,1)S(1)} collective-permute-done((bf16[128,2048]{1,0:T(8,128)(2,1)S(1)}, bf16[128,2048]{1,0:T(8,128)(2,1)S(1)}, u32[]{:S(2)}, u32[]{:S(2)}) %collective-permute-start.8) | collective-permute-done | bytes 524320 | tf_op jit(solution)/shard_map/ppermute | solution.py:398
  45.3 2.5 collective-permute-start.11
  48.4 2.4 collective-permute-start.15
  55.2 10.9 %expert.4 = (bf16[128,2048]{1,0:T(8,128)(2,1)}, bf16[128,2048]{1,0:T(8,128)(2,1)}, bf16[128,2048]{1,0:T(8,128)(2,1)}, bf16[128,2048]{1,0:T(8,128)(2,1)}, f32[4,1...) custom-call(s32[2]{0:T(128)} %copy-done.15, ...), custom_call_target="tpu_custom_call" | custom-call | flops 4831838208 | bytes 37748736 | tf_op jit(solution)/shard_map/expert/pallas_call | solution.py:202
  74.3 5.8 %collective-permute-done.12.refs_1_.refs_3_ = bf16[128,2048]{1,0:T(8,128)(2,1)S(1)} collective-permute-done((bf16[128,2048]{1,0:T(8,128)(2,1)S(1)}, bf16[128,2048]{1,0:T(8,128)(2,1)S(1)}, u32[]{:S(2)}, u32[]{:S(2)}) %collective-permute-start.12) | collective-permute-done | bytes 524320 | tf_op jit(solution)/shard_map/ppermute | solution.py:398
  80.1 2.9 %collective-permute-done.13.refs_3_ = bf16[128,2048]{1,0:T(8,128)(2,1)S(1)} collective-permute-done((bf16[128,2048]{1,0:T(8,128)(2,1)S(1)}, bf16[128,2048]{1,0:T(8,128)(2,1)S(1)}, u32[]{:S(2)}, u32[]{:S(2)}) %collective-permute-start.13) | collective-permute-done | bytes 524320 | tf_op jit(solution)/shard_map/ppermute | solution.py:398
  88.6 5.7 %collective-permute-done.19.refs_2_ = bf16[128,2048]{1,0:T(8,128)(2,1)S(1)} collective-permute-done((bf16[128,2048]{1,0:T(8,128)(2,1)S(1)}, bf16[128,2048]{1,0:T(8,128)(2,1)S(1)}, u32[]{:S(2)}, u32[]{:S(2)}) %collective-permute-start.19) | collective-permute-done | bytes 524320 | tf_op jit(solution)/shard_map/ppermute | solution.py:398
  98.2 2.0 pick.12
  105.4 10.9 %expert.5 = (bf16[128,2048]{1,0:T(8,128)(2,1)}, bf16[128,2048]{1,0:T(8,128)(2,1)}, bf16[128,2048]{1,0:T(8,128)(2,1)}, bf16[128,2048]{1,0:T(8,128)(2,1)}, f32[4,1...) custom-call(s32[2]{0:T(128)} %copy-done.15, ...), custom_call_target="tpu_custom_call" | custom-call | flops 4831838208 | bytes 37748736 | tf_op jit(solution)/shard_map/expert/pallas_call | solution.py:202
  116.3 2.4 collective-permute-done.26
  125.1 10.9 %expert.6 = (bf16[128,2048]{1,0:T(8,128)(2,1)}, bf16[128,2048]{1,0:T(8,128)(2,1)}, bf16[128,2048]{1,0:T(8,128)(2,1)}, bf16[128,2048]{1,0:T(8,128)(2,1)}, f32[4,1...) custom-call(s32[2]{0:T(128)} %copy-done.15, ...), custom_call_target="tpu_custom_call" | custom-call | flops 4831838208 | bytes 37748736 | tf_op jit(solution)/shard_map/expert/pallas_call | solution.py:202
  139.6 10.9 %expert.7 = (bf16[128,2048]{1,0:T(8,128)(2,1)}, bf16[128,2048]{1,0:T(8,128)(2,1)}, bf16[128,2048]{1,0:T(8,128)(2,1)}, bf16[128,2048]{1,0:T(8,128)(2,1)}, f32[4,1...) custom-call(s32[2]{0:T(128)} %copy-done.15, ...), custom_call_target="tpu_custom_call" | custom-call | flops 4831838208 | bytes 37748736 | tf_op jit(solution)/shard_map/expert/pallas_call | solution.py:202
  156.7 3.5 %collective-permute-done.31.received.refs_1_ = bf16[128,2048]{1,0:T(8,128)(2,1)S(1)} collective-permute-done((bf16[128,2048]{1,0:T(8,128)(2,1)}, bf16[128,2048]{1,0:T(8,128)(2,1)S(1)}, u32[]{:S(2)}, u32[]{:S(2)}) %collective-permute-start.31) | collective-permute-done | bytes 524320 | tf_op jit(solution)/shard_map/ppermute | solution.py:398
  160.1 2.1 collective-permute-done.32.received.refs_4_
  169.5 9.9 %weight_sums.2 = (f32[3,2048,384]{2,1,0:T(8,128)}, bf16[3,2048,384]{2,1,0:T(8,128)(2,1)}) custom-call(s32[2]{0:T(128)} %copy-done.15, bf16[128,2048]{1,0:T(8,128)(2,1)} %copy-done.22, bf16[128,2048]{1,0:T(8,128)(2,1)} %copy-done.40, bf16[128,2048]{1,0:T(8,128)(2,1)} %copy-done.24, bf16[128,2048]{1,0:T(8,128)(2,1)} %copy-done.42, ...), custom_call_target="tpu_custom_call" | custom-call | flops 3221225472 | bytes 31457280 | tf_op jit(solution)/shard_map/weight_sums/pallas_call | solution.py:355
  179.4 4.1 %pair_sum.4 = bf16[2,128,2048]{2,1,0:T(8,128)(2,1)} custom-call(s32[2]{0:T(128)S(1)} %copy-done.19, f32[1,16,128]{2,1,0:T(8,128)S(1)} %get-tuple-element.800.tables, bf16[128,2048]{1,0:T(8,128)(2,1)S(1)} %copy-done.5, bf16[128,2048]{1,0:T(8,128)(2,1)S(1)} %collective-permute-done.31.received.refs_1_, bf16[128,2048]{1,0:T(8,128)(2,1)} %collective-permute-done.33.refs_2_, ...), custom_call_target="tpu_custom_call" | custom-call | flops 134217728 | bytes 3145728 | tf_op jit(solution)/shard_map/pair_sum/pallas_call | solution.py:309
  183.5 2.2 collective-permute-start.41
  185.7 2.0 collective-permute-start.37
  189.8 12.9 %weight_sums.3 = (f32[3,2048,384]{2,1,0:T(8,128)}, bf16[3,2048,384]{2,1,0:T(8,128)(2,1)}) custom-call(s32[2]{0:T(128)} %copy-done.15, bf16[128,2048]{1,0:T(8,128)(2,1)} %copy-done.21, bf16[128,2048]{1,0:T(8,128)(2,1)} %copy-done.39, bf16[128,2048]{1,0:T(8,128)(2,1)} %copy-done.23, ...), custom_call_target="tpu_custom_call", output_to_operand_aliasing={{0}: (17, {}), {1}: (18, {})} | custom-call | flops 6442450944 | bytes 62914560 | tf_op jit(solution)/shard_map/weight_sums/pallas_call | solution.py:355
  202.8 2.0 collective-permute-start.36
  205.9 4.0 %pair_sum.5 = (bf16[128,2048]{1,0:T(8,128)(2,1)S(1)}, bf16[128,2048]{1,0:T(8,128)(2,1)}) custom-call(s32[2]{0:T(128)S(1)} %copy-done.20, f32[1,16,128]{2,1,0:T(8,128)S(1)} %get-tuple-element.801.tables, bf16[128,2048]{1,0:T(8,128)(2,1)S(1)} %copy-done.7, bf16[128,2048]{1,0:T(8,128)(2,1)S(1)} %collective-permute-done.29.received.refs_1_, ...), custom_call_target="tpu_custom_call" | custom-call | flops 134217728 | bytes 4194304 | tf_op jit(solution)/shard_map/pair_sum/pallas_call | solution.py:309
  210.0 4.1 %collective-permute-start.43 = (bf16[128,2048]{1,0:T(8,128)(2,1)S(1)}, bf16[128,2048]{1,0:T(8,128)(2,1)S(1)}, u32[]{:S(2)}, u32[]{:S(2)}) collective-permute-start(bf16[128,2048]{1,0:T(8,128)(2,1)S(1)} %get-tuple-element.764), channel_id=1, source_target_pairs={{0,8},{1,9},{2,10},{3,11},{4,12},{5,13},{6,14},{7,15},{8,0},{9,1},... | collective-permute-start | bytes 1572872 | tf_op jit(solution)/shard_map/ppermute | solution.py:398
  218.7 8.4 %collective-permute-done.42 = f32[2,2,2,1,128]{4,2,1,3,0:T(2,128)S(1)} collective-permute-done((f32[2,2,2,1,128]{4,2,1,3,0:T(2,128)S(1)}, f32[2,2,2,1,128]{4,2,1,3,0:T(2,128)S(1)}, u32[]{:S(2)}, u32[]{:S(2)}) %collective-permute-start.42) | collective-permute-done | bytes 4128 | tf_op jit(solution)/shard_map/ppermute | solution.py:398
  227.1 10.0 %collective-permute-done.43.refs_8_ = bf16[128,2048]{1,0:T(8,128)(2,1)S(1)} collective-permute-done((bf16[128,2048]{1,0:T(8,128)(2,1)S(1)}, bf16[128,2048]{1,0:T(8,128)(2,1)S(1)}, u32[]{:S(2)}, u32[]{:S(2)}) %collective-permute-start.43) | collective-permute-done | bytes 524320 | tf_op jit(solution)/shard_map/ppermute | solution.py:398
  238.6 3.4 %collective-permute-start.47 = (f32[2,2,2,1,128]{4,2,1,3,0:T(2,128)S(1)}, f32[2,2,2,1,128]{4,2,1,3,0:T(2,128)S(1)}, u32[]{:S(2)}, u32[]{:S(2)}) collective-permute-start(f32[2,2,2,1,128]{4,2,1,3,0:T(2,128)S(1)} %pad_maximum_fusion.12), channel_id=1, source_target_pairs={{0,8},{1,9},{2,10},{3,11},{4,12},{5,13},{6,14},{7,15},{8,0},{9,1},... | collective-permute-start | bytes 12296 | tf_op jit(solution)/shard_map/ppermute | solution.py:398
  242.7 2.0 pair_sum.6
  244.9 6.0 %collective-permute-done.50.received.refs_1_ = bf16[128,2048]{1,0:T(8,128)(2,1)S(1)} collective-permute-done((bf16[128,2048]{1,0:T(8,128)(2,1)S(1)}, bf16[128,2048]{1,0:T(8,128)(2,1)S(1)}, u32[]{:S(2)}, u32[]{:S(2)}) %collective-permute-start.50) | collective-permute-done | bytes 524320 | tf_op jit(solution)/shard_map/ppermute | solution.py:398
  255.1 8.2 %fusion = bf16[1,3,2048,384]{3,2,1,0:T(8,128)(2,1)} fusion(f32[3,2048,384]{2,1,0:T(8,128)} %get-tuple-element.774, bf16[3,2048,384]{2,1,0:T(8,128)(2,1)} %copy-done.29), kind=kLoop, calls=%fused_computation.1 | loop fusion | flops 7077888 | bytes 18874368 | tf_op jit(solution)/shard_map/broadcast_in_dim | solution.py:537
  264.3 12.1 %collective-permute-done.49.refs_6_.refs_7_ = bf16[2,128,2048]{2,1,0:T(8,128)(2,1)S(1)} collective-permute-done((bf16[2,128,2048]{2,1,0:T(8,128)(2,1)S(1)}, bf16[2,128,2048]{2,1,0:T(8,128)(2,1)S(1)}, u32[]{:S(2)}, u32[]{:S(2)}) %collective-permute-start.49) | collective-permute-done | bytes 1048608 | tf_op jit(solution)/shard_map/ppermute | solution.py:398
  277.1 3.1 %pair_sum.7 = (bf16[128,2048]{1,0:T(8,128)(2,1)}, bf16[128,2048]{1,0:T(8,128)(2,1)}) custom-call(s32[2]{0:T(128)S(1)} %copy-done.20, f32[1,16,128]{2,1,0:T(8,128)S(1)} %slice_bitcast_fusion.11.tables, bf16[128,2048]{1,0:T(8,128)(2,1)S(1)} %copy-done, bf16[128,2048]{1,0:T(8,128)(2,1)S(1)} %collective-permute-done.50.received.refs_1_, ...), custom_call_target="tpu_custom_call" | custom-call | flops 134217728 | bytes 5242880 | tf_op jit(solution)/shard_map/pair_sum/pallas_call | solution.py:309
  (237 shorter events, 80.1 us)
Async XLA Ops:
  7.2 44.4 %all-gather.2.cloned.1.call-start = ((), (), s32[]{:S(2)}) async-start(), calls=%async_computation | async-start | bytes 14155776 | tf_op jit(solution)/shard_map/all_gather | solution.py:410
  8.2 18.1 %collective-permute-start = (bf16[128,2048]{1,0:T(8,128)(2,1)S(1)}, bf16[128,2048]{1,0:T(8,128)(2,1)}, u32[]{:S(2)}, u32[]{:S(2)}) collective-permute-start(bf16[128,2048]{1,0:T(8,128)(2,1)S(1)} %copy-done.13), channel_id=1, source_target_pairs={{0,2},{1,3},{2,0},{3,1},{4,6},{5,7},{6,4},{7,5},{8,10},{9,11},{10,... | collective-permute-start | bytes 1572872 | tf_op jit(solution)/shard_map/ppermute | solution.py:398
  9.7 16.6 %collective-permute-start.1 = (bf16[128,2048]{1,0:T(8,128)(2,1)S(1)}, bf16[128,2048]{1,0:T(8,128)(2,1)S(1)}, u32[]{:S(2)}, u32[]{:S(2)}) collective-permute-start(bf16[128,2048]{1,0:T(8,128)(2,1)S(1)} %copy-done.14), channel_id=1, source_target_pairs={{0,1},{1,0},{2,3},{3,2},{4,5},{5,4},{6,7},{7,6},{8,9},{9,8},{10,11... | collective-permute-start | bytes 1572872 | tf_op jit(solution)/shard_map/ppermute | solution.py:398
  12.4 20.7 %collective-permute-start.7 = (bf16[128,2048]{1,0:T(8,128)(2,1)S(1)}, bf16[128,2048]{1,0:T(8,128)(2,1)S(1)}, u32[]{:S(2)}, u32[]{:S(2)}) collective-permute-start(bf16[128,2048]{1,0:T(8,128)(2,1)S(1)} %copy-done.13), channel_id=1, source_target_pairs={{0,4},{1,5},{2,6},{3,7},{4,0},{5,1},{6,2},{7,3},{8,12},{9,13},{10,... | collective-permute-start | bytes 1572872 | tf_op jit(solution)/shard_map/ppermute | solution.py:398
  23.3 22.0 %collective-permute-start.8 = (bf16[128,2048]{1,0:T(8,128)(2,1)S(1)}, bf16[128,2048]{1,0:T(8,128)(2,1)S(1)}, u32[]{:S(2)}, u32[]{:S(2)}) collective-permute-start(bf16[128,2048]{1,0:T(8,128)(2,1)S(1)} %copy-done.14), channel_id=1, source_target_pairs={{0,4},{1,5},{2,6},{3,7},{4,0},{5,1},{6,2},{7,3},{8,12},{9,13},{10,... | collective-permute-start | bytes 1572872 | tf_op jit(solution)/shard_map/ppermute | solution.py:398
  23.7 24.6 %collective-permute-start.14 = (bf16[128,2048]{1,0:T(8,128)(2,1)S(1)}, bf16[128,2048]{1,0:T(8,128)(2,1)S(1)}, u32[]{:S(2)}, u32[]{:S(2)}) collective-permute-start(bf16[128,2048]{1,0:T(8,128)(2,1)S(1)} %copy-done.13), channel_id=1, source_target_pairs={{0,8},{1,9},{2,10},{3,11},{4,12},{5,13},{6,14},{7,15},{8,0},{9,1},... | collective-permute-start | bytes 1572872 | tf_op jit(solution)/shard_map/ppermute | solution.py:398
  29.0 21.8 %collective-permute-start.4 = (bf16[128,2048]{1,0:T(8,128)(2,1)S(1)}, bf16[128,2048]{1,0:T(8,128)(2,1)S(1)}, u32[]{:S(2)}, u32[]{:S(2)}) collective-permute-start(bf16[128,2048]{1,0:T(8,128)(2,1)S(1)} %get-tuple-element.409), channel_id=1, source_target_pairs={{0,1},{1,0},{2,3},{3,2},{4,5},{5,4},{6,7},{7,6},{8,9},{9,8},{10,11... | collective-permute-start | bytes 1572872 | tf_op jit(solution)/shard_map/ppermute | solution.py:398
  32.6 19.0 %collective-permute-start.5 = (bf16[128,2048]{1,0:T(8,128)(2,1)S(1)}, bf16[128,2048]{1,0:T(8,128)(2,1)S(1)}, u32[]{:S(2)}, u32[]{:S(2)}) collective-permute-start(bf16[128,2048]{1,0:T(8,128)(2,1)S(1)} %get-tuple-element.410), channel_id=1, source_target_pairs={{0,2},{1,3},{2,0},{3,1},{4,6},{5,7},{6,4},{7,5},{8,10},{9,11},{10,... | collective-permute-start | bytes 1572872 | tf_op jit(solution)/shard_map/ppermute | solution.py:398
  33.1 17.7 %collective-permute-start.6 = (f32[1,16,128]{2,1,0:T(8,128)S(1)}, f32[1,16,128]{2,1,0:T(8,128)S(1)}, u32[]{:S(2)}, u32[]{:S(2)}) collective-permute-start(f32[1,16,128]{2,1,0:T(8,128)S(1)} %get-tuple-element.829.refs_1_), channel_id=1, source_target_pairs={{0,1},{1,0},{2,3},{3,2},{4,5},{5,4},{6,7},{7,6},{8,9},{9,8},{10,11... | collective-permute-start | bytes 24584 | tf_op jit(solution)/shard_map/ppermute | solution.py:398
  45.3 20.8 %collective-permute-start.11 = (f32[3,1,16,128]{3,2,0,1:T(8,128)S(1)}, f32[3,1,16,128]{3,2,0,1:T(8,128)S(1)}, u32[]{:S(2)}, u32[]{:S(2)}) collective-permute-start(f32[3,1,16,128]{3,2,0,1:T(8,128)S(1)} %bitcast.135), channel_id=1, source_target_pairs={{0,4},{1,5},{2,6},{3,7},{4,0},{5,1},{6,2},{7,3},{8,12},{9,13},{10,... | collective-permute-start | bytes 73736 | tf_op jit(solution)/shard_map/ppermute | solution.py:398
  48.4 24.6 %collective-permute-start.15 = (bf16[128,2048]{1,0:T(8,128)(2,1)S(1)}, bf16[128,2048]{1,0:T(8,128)(2,1)S(1)}, u32[]{:S(2)}, u32[]{:S(2)}) collective-permute-start(bf16[128,2048]{1,0:T(8,128)(2,1)S(1)} %copy-done.14), channel_id=1, source_target_pairs={{0,8},{1,9},{2,10},{3,11},{4,12},{5,13},{6,14},{7,15},{8,0},{9,1},... | collective-permute-start | bytes 1572872 | tf_op jit(solution)/shard_map/ppermute | solution.py:398
  73.0 21.3 %collective-permute-start.19 = (bf16[128,2048]{1,0:T(8,128)(2,1)S(1)}, bf16[128,2048]{1,0:T(8,128)(2,1)S(1)}, u32[]{:S(2)}, u32[]{:S(2)}) collective-permute-start(bf16[128,2048]{1,0:T(8,128)(2,1)S(1)} %collective-permute-done.15.refs_2_), channel_id=1, source_target_pairs={{0,4},{1,5},{2,6},{3,7},{4,0},{5,1},{6,2},{7,3},{8,12},{9,13},{10,... | collective-permute-start | bytes 1572872 | tf_op jit(solution)/shard_map/ppermute | solution.py:398
  94.9 23.9 %collective-permute-start.22 = (bf16[128,2048]{1,0:T(8,128)(2,1)S(1)}, bf16[128,2048]{1,0:T(8,128)(2,1)S(1)}, u32[]{:S(2)}, u32[]{:S(2)}) collective-permute-start(bf16[128,2048]{1,0:T(8,128)(2,1)S(1)} %collective-permute-done.18.refs_2_), channel_id=1, source_target_pairs={{0,2},{1,3},{2,0},{3,1},{4,6},{5,7},{6,4},{7,5},{8,10},{9,11},{10,... | collective-permute-start | bytes 1572872 | tf_op jit(solution)/shard_map/ppermute | solution.py:398
  96.7 22.1 %collective-permute-start.23 = (bf16[128,2048]{1,0:T(8,128)(2,1)S(1)}, bf16[128,2048]{1,0:T(8,128)(2,1)S(1)}, u32[]{:S(2)}, u32[]{:S(2)}) collective-permute-start(bf16[128,2048]{1,0:T(8,128)(2,1)S(1)} %collective-permute-done.19.refs_2_), channel_id=1, source_target_pairs={{0,1},{1,0},{2,3},{3,2},{4,5},{5,4},{6,7},{7,6},{8,9},{9,8},{10,11... | collective-permute-start | bytes 1572872 | tf_op jit(solution)/shard_map/ppermute | solution.py:398
  100.1 18.6 %collective-permute-start.24 = (bf16[128,2048]{1,0:T(8,128)(2,1)}, bf16[128,2048]{1,0:T(8,128)(2,1)}, u32[]{:S(2)}, u32[]{:S(2)}) collective-permute-start(bf16[128,2048]{1,0:T(8,128)(2,1)} %get-tuple-element.484), channel_id=1, source_target_pairs={{0,1},{1,0},{2,3},{3,2},{4,5},{5,4},{6,7},{7,6},{8,9},{9,8},{10,11... | collective-permute-start | bytes 1572872 | tf_op jit(solution)/shard_map/ppermute | solution.py:398
  103.0 15.8 %collective-permute-start.25 = (bf16[128,2048]{1,0:T(8,128)(2,1)S(1)}, bf16[128,2048]{1,0:T(8,128)(2,1)S(1)}, u32[]{:S(2)}, u32[]{:S(2)}) collective-permute-start(bf16[128,2048]{1,0:T(8,128)(2,1)S(1)} %get-tuple-element.485), channel_id=1, source_target_pairs={{0,2},{1,3},{2,0},{3,1},{4,6},{5,7},{6,4},{7,5},{8,10},{9,11},{10,... | collective-permute-start | bytes 1572872 | tf_op jit(solution)/shard_map/ppermute | solution.py:398
  103.3 15.4 %collective-permute-start.26 = (f32[2,1,16,128]{3,2,1,0:T(8,128)S(1)}, f32[2,1,16,128]{3,2,1,0:T(8,128)S(1)}, u32[]{:S(2)}, u32[]{:S(2)}) collective-permute-start(f32[2,1,16,128]{3,2,1,0:T(8,128)S(1)} %slice_bitcast_fusion), channel_id=1, source_target_pairs={{0,1},{1,0},{2,3},{3,2},{4,5},{5,4},{6,7},{7,6},{8,9},{9,8},{10,11... | collective-permute-start | bytes 49160 | tf_op jit(solution)/shard_map/ppermute | solution.py:398
  183.5 21.3 %collective-permute-start.41 = (bf16[2,128,2048]{2,1,0:T(8,128)(2,1)}, bf16[2,128,2048]{2,1,0:T(8,128)(2,1)S(1)}, u32[]{:S(2)}, u32[]{:S(2)}) collective-permute-start(bf16[2,128,2048]{2,1,0:T(8,128)(2,1)} %pair_sum.4), channel_id=1, source_target_pairs={{0,4},{1,5},{2,6},{3,7},{4,0},{5,1},{6,2},{7,3},{8,12},{9,13},{10,... | collective-permute-start | bytes 3145736 | tf_op jit(solution)/shard_map/ppermute | solution.py:398
  185.7 17.0 %collective-permute-start.37 = (bf16[128,2048]{1,0:T(8,128)(2,1)}, bf16[128,2048]{1,0:T(8,128)(2,1)}, u32[]{:S(2)}, u32[]{:S(2)}) collective-permute-start(bf16[128,2048]{1,0:T(8,128)(2,1)} %copy-done.12), channel_id=1, source_target_pairs={{0,2},{1,3},{2,0},{3,1},{4,6},{5,7},{6,4},{7,5},{8,10},{9,11},{10,... | collective-permute-start | bytes 1572872 | tf_op jit(solution)/shard_map/ppermute | solution.py:398
  187.7 17.1 %collective-permute-start.38 = (bf16[128,2048]{1,0:T(8,128)(2,1)}, bf16[128,2048]{1,0:T(8,128)(2,1)}, u32[]{:S(2)}, u32[]{:S(2)}) collective-permute-start(bf16[128,2048]{1,0:T(8,128)(2,1)} %copy-done.11), channel_id=1, source_target_pairs={{0,1},{1,0},{2,3},{3,2},{4,5},{5,4},{6,7},{7,6},{8,9},{9,8},{10,11... | collective-permute-start | bytes 1572872 | tf_op jit(solution)/shard_map/ppermute | solution.py:398
  188.5 21.4 %collective-permute-start.39 = (bf16[128,2048]{1,0:T(8,128)(2,1)}, bf16[128,2048]{1,0:T(8,128)(2,1)S(1)}, u32[]{:S(2)}, u32[]{:S(2)}) collective-permute-start(bf16[128,2048]{1,0:T(8,128)(2,1)} %get-tuple-element.719), channel_id=1, source_target_pairs={{0,1},{1,0},{2,3},{3,2},{4,5},{5,4},{6,7},{7,6},{8,9},{9,8},{10,11... | collective-permute-start | bytes 1572872 | tf_op jit(solution)/shard_map/ppermute | solution.py:398
  189.7 20.2 %collective-permute-start.40 = (bf16[128,2048]{1,0:T(8,128)(2,1)}, bf16[128,2048]{1,0:T(8,128)(2,1)S(1)}, u32[]{:S(2)}, u32[]{:S(2)}) collective-permute-start(bf16[128,2048]{1,0:T(8,128)(2,1)} %get-tuple-element.721), channel_id=1, source_target_pairs={{0,2},{1,3},{2,0},{3,1},{4,6},{5,7},{6,4},{7,5},{8,10},{9,11},{10,... | collective-permute-start | bytes 1572872 | tf_op jit(solution)/shard_map/ppermute | solution.py:398
  209.9 27.2 %collective-permute-start.46 = (bf16[3,2048,384]{2,1,0:T(8,128)(2,1)}, bf16[3,2048,384]{2,1,0:T(8,128)(2,1)S(1)}, u32[]{:S(2)}, u32[]{:S(2)}) collective-permute-start(bf16[3,2048,384]{2,1,0:T(8,128)(2,1)} %get-tuple-element.759), channel_id=1, source_target_pairs={{0,16},{16,0},{1,17},{17,1},{2,18},{18,2},{3,19},{19,3},{4,20},{20... | collective-permute-start | bytes 14155784 | tf_op jit(solution)/shard_map/ppermute | solution.py:401
  210.0 27.1 %collective-permute-start.43 = (bf16[128,2048]{1,0:T(8,128)(2,1)S(1)}, bf16[128,2048]{1,0:T(8,128)(2,1)S(1)}, u32[]{:S(2)}, u32[]{:S(2)}) collective-permute-start(bf16[128,2048]{1,0:T(8,128)(2,1)S(1)} %get-tuple-element.764), channel_id=1, source_target_pairs={{0,8},{1,9},{2,10},{3,11},{4,12},{5,13},{6,14},{7,15},{8,0},{9,1},... | collective-permute-start | bytes 1572872 | tf_op jit(solution)/shard_map/ppermute | solution.py:398
  215.3 21.8 %collective-permute-start.44 = (bf16[128,2048]{1,0:T(8,128)(2,1)S(1)}, bf16[128,2048]{1,0:T(8,128)(2,1)S(1)}, u32[]{:S(2)}, u32[]{:S(2)}) collective-permute-start(bf16[128,2048]{1,0:T(8,128)(2,1)S(1)} %token_sum.12), channel_id=1, source_target_pairs={{0,2},{1,3},{2,0},{3,1},{4,6},{5,7},{6,4},{7,5},{8,10},{9,11},{10,... | collective-permute-start | bytes 1572872 | tf_op jit(solution)/shard_map/ppermute | solution.py:398
  217.7 19.4 %collective-permute-start.45 = (bf16[128,2048]{1,0:T(8,128)(2,1)S(1)}, bf16[128,2048]{1,0:T(8,128)(2,1)S(1)}, u32[]{:S(2)}, u32[]{:S(2)}) collective-permute-start(bf16[128,2048]{1,0:T(8,128)(2,1)S(1)} %token_sum.13), channel_id=1, source_target_pairs={{0,1},{1,0},{2,3},{3,2},{4,5},{5,4},{6,7},{7,6},{8,9},{9,8},{10,11... | collective-permute-start | bytes 1572872 | tf_op jit(solution)/shard_map/ppermute | solution.py:398
  237.7 15.5 %collective-permute-start.51 = (bf16[128,2048]{1,0:T(8,128)(2,1)S(1)}, bf16[128,2048]{1,0:T(8,128)(2,1)S(1)}, u32[]{:S(2)}, u32[]{:S(2)}) collective-permute-start(bf16[128,2048]{1,0:T(8,128)(2,1)S(1)} %copy-done.37), channel_id=1, source_target_pairs={{0,2},{1,3},{2,0},{3,1},{4,6},{5,7},{6,4},{7,5},{8,10},{9,11},{10,... | collective-permute-start | bytes 1572872 | tf_op jit(solution)/shard_map/ppermute | solution.py:398
  238.6 24.6 %collective-permute-start.47 = (f32[2,2,2,1,128]{4,2,1,3,0:T(2,128)S(1)}, f32[2,2,2,1,128]{4,2,1,3,0:T(2,128)S(1)}, u32[]{:S(2)}, u32[]{:S(2)}) collective-permute-start(f32[2,2,2,1,128]{4,2,1,3,0:T(2,128)S(1)} %pad_maximum_fusion.12), channel_id=1, source_target_pairs={{0,8},{1,9},{2,10},{3,11},{4,12},{5,13},{6,14},{7,15},{8,0},{9,1},... | collective-permute-start | bytes 12296 | tf_op jit(solution)/shard_map/ppermute | solution.py:398
  242.0 22.3 %collective-permute-start.48 = (bf16[128,2048]{1,0:T(8,128)(2,1)}, bf16[128,2048]{1,0:T(8,128)(2,1)S(1)}, u32[]{:S(2)}, u32[]{:S(2)}) collective-permute-start(bf16[128,2048]{1,0:T(8,128)(2,1)} %get-tuple-element.779), channel_id=1, source_target_pairs={{0,8},{1,9},{2,10},{3,11},{4,12},{5,13},{6,14},{7,15},{8,0},{9,1},... | collective-permute-start | bytes 1572872 | tf_op jit(solution)/shard_map/ppermute | solution.py:398
  244.7 31.7 %collective-permute-start.49 = (bf16[2,128,2048]{2,1,0:T(8,128)(2,1)S(1)}, bf16[2,128,2048]{2,1,0:T(8,128)(2,1)S(1)}, u32[]{:S(2)}, u32[]{:S(2)}) collective-permute-start(bf16[2,128,2048]{2,1,0:T(8,128)(2,1)S(1)} %pair_sum.6), channel_id=1, source_target_pairs={{0,4},{1,5},{2,6},{3,7},{4,0},{5,1},{6,2},{7,3},{8,12},{9,13},{10,... | collective-permute-start | bytes 3145736 | tf_op jit(solution)/shard_map/ppermute | solution.py:398
  252.2 24.2 %collective-permute-start.52 = (bf16[128,2048]{1,0:T(8,128)(2,1)S(1)}, bf16[128,2048]{1,0:T(8,128)(2,1)S(1)}, u32[]{:S(2)}, u32[]{:S(2)}) collective-permute-start(bf16[128,2048]{1,0:T(8,128)(2,1)S(1)} %token_sum.14), channel_id=1, source_target_pairs={{0,2},{1,3},{2,0},{3,1},{4,6},{5,7},{6,4},{7,5},{8,10},{9,11},{10,... | collective-permute-start | bytes 1572872 | tf_op jit(solution)/shard_map/ppermute | solution.py:398
  254.4 21.9 %collective-permute-start.53 = (bf16[128,2048]{1,0:T(8,128)(2,1)S(1)}, bf16[128,2048]{1,0:T(8,128)(2,1)S(1)}, u32[]{:S(2)}, u32[]{:S(2)}) collective-permute-start(bf16[128,2048]{1,0:T(8,128)(2,1)S(1)} %token_sum.15), channel_id=1, source_target_pairs={{0,1},{1,0},{2,3},{3,2},{4,5},{5,4},{6,7},{7,6},{8,9},{9,8},{10,11... | collective-permute-start | bytes 1572872 | tf_op jit(solution)/shard_map/ppermute | solution.py:398
  (68 other events, 776.6 us)
Sparse Core Ops, SparseCore 0:
  9.6 23.2 all-gather.1

commit v3 on v2

--- a/solution.py
+++ b/solution.py
@@ -271,6 +271,44 @@
     )(me, tables, own, received, *others, *deps)
 
 
+def there_kernel(capacity, me_ref, tables_t, tables_g, *refs):
+    me = me_ref[0]
+    for a, flip, tables in ((0, 1, tables_t), (1, 2, tables_g)):
+        own, got = refs[2 * a : 2 * a + 2]
+        blocks, _, tokens = tables.shape
+        for b in range(blocks):
+            slots = slice(b * capacity, (b + 1) * capacity)
+            mask = jnp.concatenate(
+                [mask_of(tables[b], me, capacity), mask_of(tables[b], me ^ flip, capacity)], axis=0
+            )
+            rows = jnp.concatenate([own[slots, :], got[slots, :]], axis=0)
+            total = jnp.dot(mask.T.astype(BF16), rows, preferred_element_type=F32)
+            refs[4 + a][b * tokens : (b + 1) * tokens, :] = total.astype(BF16)
+
+
+def there_sum(me, capacity, tables_t, tables_g, out, back):
+    blocks, _, tokens = tables_t.shape
+    width = out[0].shape[1]
+    tile = 1024
+    rows = blocks * tokens
+    table_spec = pl.BlockSpec(tables_t.shape, lambda i: (0, 0, 0))
+    row_spec = pl.BlockSpec((blocks * capacity, tile), lambda i: (1, i))
+    return pl.pallas_call(
+        functools.partial(there_kernel, capacity),
+        grid=(width // tile,),
+        in_specs=[SCALAR, table_spec, table_spec] + [row_spec] * 4,
+        out_specs=[pl.BlockSpec((rows, tile), lambda i: (0, i))] * 2,
+        out_shape=[jax.ShapeDtypeStruct((rows, width), BF16)] * 2,
+        compiler_params=pltpu.CompilerParams(vmem_limit_bytes=60 * MIB),
+        cost_estimate=pl.CostEstimate(
+            flops=8 * rows * capacity * width,
+            bytes_accessed=4 * blocks * (tokens + 2 * capacity) * width,
+            transcendentals=0,
+        ),
+        name="there_sum",
+    )(me, tables_t, tables_g, *out, *back)
+
+
 def pair_kernel(capacity, n_more, me_ref, tables, *refs):
     mores, outs = refs[6 : 6 + 2 * n_more], refs[6 + 2 * n_more :]
     blocks, _, tokens = tables.shape
@@ -296,7 +334,7 @@
 def pair_sum(me, capacity, tables, out, back, mores=(), split=False):
     blocks, _, tokens = tables.shape
     width = out[0].shape[1]
-    tile = 512
+    tile = 1024
     rows = blocks * tokens
     row_spec = pl.BlockSpec((blocks * capacity, tile), lambda i: (0, i))
     sum_spec = pl.BlockSpec((rows, tile), lambda i: (0, i))
@@ -314,7 +352,7 @@
         + [s for _, specs in mores for s in specs],
         out_specs=[sum_spec] * 2 if split else pair_spec,
         out_shape=[single] * 2 if split else jax.ShapeDtypeStruct((2, rows, width), BF16),
-        compiler_params=pltpu.CompilerParams(vmem_limit_bytes=24 * MIB),
+        compiler_params=pltpu.CompilerParams(vmem_limit_bytes=60 * MIB),
         cost_estimate=pl.CostEstimate(
             flops=8 * rows * capacity * width,
             bytes_accessed=4 * blocks * (tokens * (2 + len(mores)) + 2 * capacity) * width,
@@ -440,7 +478,7 @@
         return sent_t, sent_g
 
     def run_expert(c):
-        tables = jnp.concatenate([table_of(c, i) for i in range(3)] + [held["diagonal", c]])
+        tables = jnp.concatenate([table_of(c, i) for i in range(4)])
         names = ("out own", "out sent", "back own", "back sent", "sums", "act", "dgate", "dup")
         rows = [held[n, c] for n in ("t own", "t got", "g own", "g got")]
         for name, value in zip(names, expert(me, capacity, tables, held["weights"], *rows)):
@@ -451,10 +489,8 @@
         held["back got", c] = swap(held["back sent", c], FLIP_Y)
 
     def sum_there(c):
-        return (
-            token_sum(me, FLIP_X, capacity, table_of(c, 1), held["out own", c], held["out got", c], 1),
-            token_sum(me, FLIP_Y, capacity, table_of(c, 2), held["back own", c], held["back got", c], 1),
-        )
+        out, back = ([held[n + k, c] for k in (" own", " got")] for n in ("out", "back"))
+        return there_sum(me, capacity, table_of(c, 1), table_of(c, 2), out, back)
 
     def send_parts(c, part_t, part_g):
         held["out part", c] = swap(part_t, FLIP_Y)
@@ -470,35 +506,34 @@
         return weight_sums(me, pieces, rights, reorder, at, before)
 
     send_full(0)
+    held.fence()
     tab_x, tab_y = swap(held["tab"], FLIP_X), swap(held["tab"], FLIP_Y)
     held["tabs"] = jnp.stack([held["tab"], tab_y, tab_x])
     held.fence()
-    sent = pick_rows(0)
-    far_g = swap(after(here_g, near_t, near_g, far_t, *sent), FLIP_FAR)
-    last_t, last_g = swap(after(far_t, near_t, near_g), FLIP_NEAR), swap(far_g, FLIP_NEAR)
-    held["diagonal", 0] = swap(held["tabs"][1], FLIP_X)
-    near_tabs = swap(held["tabs"], FLIP_NEAR)
+    pick_rows(0)
+    diagonal = swap(held["tabs"][1], FLIP_X)
+    held["tabs"] = jnp.concatenate([held["tabs"], diagonal[None]])
     held["weights"] = weights
-    held["t", 1], held["g", 1] = near_t, near_g
+    held["t", 1], held["g", 1], held["t", 2] = near_t, near_g, far_t
     held.fence()
     send_full(1)
+    held["near tabs"] = swap(held["tabs"], FLIP_NEAR)
+    far_g = swap(held["g", 0], FLIP_FAR)
+    held.fence()
+    sent = pick_rows(1)
+    held["g", 2] = after(far_g, *sent)
+    send_full(2)
     run_expert(0)
-    held["near tabs"] = near_tabs
-    held.fence()
-    pick_rows(1)
-    arrived = held["t got", 1], held["g got", 1]
-    held["t", 2], held["g", 2] = after(far_t, *arrived), after(far_g, *arrived)
-    send_full(2)
-    held["t", 3], held["g", 3] = last_t, last_g
-    held["diagonal", 1] = swap(held["near tabs"][1], FLIP_X)
+    last_g = swap(held["g", 2], FLIP_NEAR)
     held["far tabs"] = swap(jnp.stack([held["tabs"], held["near tabs"]]), FLIP_FAR)
-    held.fence()
+    held["t", 3] = swap(after(held["t", 2], held["far tabs"], *sent), FLIP_NEAR)
+    held.fence()
+    sent = pick_rows(2)
+    held["g", 3] = after(last_g, *sent)
     send_full(3)
-    pick_rows(2)
     run_expert(1)
-    diagonal = swap(held["far tabs"][:, 1], FLIP_X)
-    held["diagonal", 2], held["diagonal", 3] = diagonal[0], diagonal[1]
-    held.fence()
+    held.fence()
+    send_rows(1)
     pick_rows(3)
     run_expert(2)
     held.fence()
@@ -507,41 +542,53 @@
     held.fence()
     send_rows(3)
     held["part 2"] = sum_there(2)
-    held.fence()
-    held["weight sums"] = sum_weights("g", ["act"], True, 2)
-    send_parts(3, *sum_there(3))
     sums = jnp.stack([held["sums", c] for c in range(CHUNKS)])
     sums = sums.reshape(CHUNKS, 2, 2, many, tok_count)
     held["sums"] = sums[:, 0], swap(sums[:, 1], FLIP_X)
     held.fence()
-    held["weight sums"] = sum_weights("t", ["dgate", "dup"], False, 0, held["weight sums"])
-    send_parts(2, *held["part 2"])
-    send_rows(1)
-    last = swap(sum_here(3), FLIP_NEAR)
-    held["sum 2"] = sum_here(2, [last], True)
+    send_parts(3, *sum_there(3))
     sums = jnp.stack(held["sums"])
     held["sums"] = sums[:, :, 0], swap(sums[:, :, 1], FLIP_Y)
     held.fence()
+    total = sum_here(3)
+    held["part 2"] = [after(part, total) for part in held["part 2"]]
+    send_parts(2, *held["part 2"])
+    last = swap(total, FLIP_NEAR)
+    send_parts(1, *sum_there(1))
+    held["weight sums"] = sum_weights("t", ["dgate", "dup"], False, 0)
+    held["sum 2"] = sum_here(2, [last], True)
+    held.fence()
     held["far t"] = swap(held["sum 2"][0], FLIP_FAR)
-    send_parts(1, *sum_there(1))
-    held["weights got"] = swap_dp(held["weight sums"][1])
+    total_t, held["sum 1"] = sum_here(1, [], True)
+    held["near t"] = swap(total_t, FLIP_NEAR)
+    for name in (("out sent", 0), ("back sent", 0)):
+        held[name] = after(held[name], total_t)
+    send_rows(0)
+    held["part 0"] = sum_there(0)
+    held["weight sums"] = sum_weights("g", ["act"], True, 2, held["weight sums"])
     sums = jnp.stack(held["sums"])
-    even = jnp.stack([sums[:, :, 0], sums[:, :, 2]])
-    held["sums"] = even, swap(jnp.stack([sums[:, :, 1], sums[:, :, 3]]), FLIP_NEAR)
-    held.fence()
+    beyond = swap(after(sums[:, :, 2:], held["out got", 0], held["back got", 0]), FLIP_FAR)
+    held["sums"] = sums[:, :, :2], beyond
+    held.fence()
+
+    def last_sum(name, flip, which):
+        rows = (held[name + k, 0] for k in (" own", " got"))
+        others = held[name + " part", 0], held["near " + which], held["far " + which]
+        return token_sum(me, flip, capacity, table_of(0, 0), *rows, 0, others)
+
     held["far g"] = swap(held["sum 2"][1], FLIP_FAR)
-    held["near"] = swap(sum_here(1), FLIP_NEAR)
-    send_rows(0)
-    send_parts(0, *sum_there(0))
-    weight_grads = held["weight sums"][0] + held["weights got"].astype(F32)
+    held["near g"] = swap(held["sum 1"], FLIP_NEAR)
+    send_parts(0, *held["part 0"])
+    weights_got = swap_dp(held["weight sums"][1])
+    weight_grads = held["weight sums"][0] + weights_got.astype(F32)
     held["weight grads"] = weight_grads.astype(BF16)[None]
-    even, odd = held["sums"]
-    held["sums"] = even[0], odd[0], swap(jnp.stack([even[1], odd[1]]), FLIP_FAR)
-    held.fence()
-    far = [held["far t"], held["far g"]]
-    total_t, total_g = sum_here(0, [held["near"], far], True)
-    here, near, far = held["sums"]
-    sums = jnp.stack([here, near, far[0], far[1]])
+    held["total t"] = last_sum("out", FLIP_X, "t")
+    sums = jnp.stack(held["sums"])
+    beside = swap(after(sums[:, :, :, 1], held["total t"]), FLIP_NEAR)
+    held["sums"] = sums[:, :, :, 0], beside
+    held.fence()
+    total_t, total_g = held["total t"], last_sum("back", FLIP_Y, "g")
+    sums = jnp.stack(held["sums"], axis=1).reshape(CHUNKS, 2, 2, many, tok_count)
     parts = [sums[:, :, :, 0]] + [swap(sums[:, :, :, r], 4 * r) for r in range(1, many)]
     sums = jnp.stack(parts, axis=1).reshape(n_expert, tok_count)
     source = jnp.arange(n_expert, dtype=jnp.int32) ^ index

time: 292 us -> 280 us (0.959)
  waiting for transfers between devices: 85.2 us -> 73.1 us
  local copies, waits for them, and re-layouts: 11.1 us -> 14.2 us
    ppermute x53 -> x52, waiting for transfers between devices: 84.5 us -> 72.4 us  [swap(): lax.ppermute(array, 'expert', [(i, i ^ flip) for i in range(n_expert)])]
    pallas_call x0 -> x4, Pallas kernels: none -> 10.6 us  [there_sum(): pl.pallas_call(functools.partial(there_kernel, capacity), grid=(width //...]
    pallas_call x8 -> x2, Pallas kernels: 11.1 us -> 4.05 us  [token_sum(): pl.pallas_call(functools.partial(sum_kernel, capacity, flip, len(others),...]
    pallas_call x4 -> x3, Pallas kernels: 13.3 us -> 8.95 us  [pair_sum(): pl.pallas_call(functools.partial(pair_kernel, capacity, len(mores)), grid...]
    ppermute x53 -> x52, starting transfers between devices: 61.4 us -> 59.6 us  [swap(): lax.ppermute(array, 'expert', [(i, i ^ flip) for i in range(n_expert)])]
  transfers between devices with their start and end apart: 55 -> 54, of which waited for: 16 -> 22; matrix products, arithmetic and copies ran while one was open for 4% -> 5% of each run, Pallas kernels for 32% -> 33%
where the time goes in v3:
time: 280 us; the launch traced here: 276 us
  Pallas kernels  102 us (36%)
  waiting for transfers between devices  73.1 us (26%)
  starting transfers between devices  59.6 us (21%)
  between operations  14.6 us (5%)
  local copies, waits for them, and re-layouts  14.2 us (5%)
  other arithmetic  12.2 us (4%)
    ppermute x52, waiting for transfers between devices, swap(): lax.ppermute(array, 'expert', [(i, i ^ flip) for i in range(n_expert)])  72.4 us
    ppermute x52, starting transfers between devices, swap(): lax.ppermute(array, 'expert', [(i, i ^ flip) for i in range(n_expert)])  59.6 us
    pallas_call x4, Pallas kernels, expert(): pl.pallas_call(functools.partial(expert_kernel, capacity, len(deps)), in_...  43.6 us
    pallas_call x2, Pallas kernels, weight_sums(): pl.pallas_call(functools.partial(weight_kernel, len(rights[0]), n_out, re...  22.6 us
    pallas_call x8, Pallas kernels, pick(): pl.pallas_call(functools.partial(pick_kernel, capacity, flip, blocks, len...  12.1 us
    pallas_call x4, Pallas kernels, there_sum(): pl.pallas_call(functools.partial(there_kernel, capacity), grid=(width //...  10.6 us
    unnamed x90, local copies, waits for them, and re-layouts  10.4 us
    pallas_call x3, Pallas kernels, pair_sum(): pl.pallas_call(functools.partial(pair_kernel, capacity, len(mores)), grid...  8.95 us
  transfers between devices with their start and end apart: 54, of which 22 were waited for; matrix products, arithmetic and copies ran while one was open for 5% of the time, Pallas kernels for 33%

profile of v3, /device:TPU:8, one launch (start us, length us, event | category | flops | bytes accessed | tf_op | source)
XLA Modules:
  0.0 275.6 jit_solution(7305503710107283974)
XLA Ops:
  13.2 2.6 collective-permute-start.9
  15.9 6.1 %collective-permute-done.refs_3_ = bf16[128,2048]{1,0:T(8,128)(2,1)} collective-permute-done((bf16[128,2048]{1,0:T(8,128)(2,1)S(1)}, bf16[128,2048]{1,0:T(8,128)(2,1)}, u32[]{:S(2)}, u32[]{:S(2)}) %collective-permute-start) | collective-permute-done | bytes 524320 | tf_op jit(solution)/shard_map/ppermute | solution.py:436
  35.5 9.3 %collective-permute-done.8.refs_2_ = bf16[128,2048]{1,0:T(8,128)(2,1)S(1)} collective-permute-done((bf16[128,2048]{1,0:T(8,128)(2,1)S(1)}, bf16[128,2048]{1,0:T(8,128)(2,1)S(1)}, u32[]{:S(2)}, u32[]{:S(2)}) %collective-permute-start.8) | collective-permute-done | bytes 524320 | tf_op jit(solution)/shard_map/ppermute | solution.py:436
  44.8 3.0 %collective-permute-done.9.refs_2_ = bf16[128,2048]{1,0:T(8,128)(2,1)S(1)} collective-permute-done((bf16[128,2048]{1,0:T(8,128)(2,1)S(1)}, bf16[128,2048]{1,0:T(8,128)(2,1)S(1)}, u32[]{:S(2)}, u32[]{:S(2)}) %collective-permute-start.9) | collective-permute-done | bytes 524320 | tf_op jit(solution)/shard_map/ppermute | solution.py:436
  51.6 2.4 collective-permute-done.12
  54.0 6.8 %collective-permute-done.10.refs_3_ = bf16[128,2048]{1,0:T(8,128)(2,1)S(1)} collective-permute-done((bf16[128,2048]{1,0:T(8,128)(2,1)S(1)}, bf16[128,2048]{1,0:T(8,128)(2,1)S(1)}, u32[]{:S(2)}, u32[]{:S(2)}) %collective-permute-start.10) | collective-permute-done | bytes 524320 | tf_op jit(solution)/shard_map/ppermute | solution.py:436
  64.7 2.0 pick.11
  68.9 4.9 %collective-permute-done.15.refs_2_ = bf16[128,2048]{1,0:T(8,128)(2,1)S(1)} collective-permute-done((bf16[128,2048]{1,0:T(8,128)(2,1)S(1)}, bf16[128,2048]{1,0:T(8,128)(2,1)S(1)}, u32[]{:S(2)}, u32[]{:S(2)}) %collective-permute-start.15) | collective-permute-done | bytes 524320 | tf_op jit(solution)/shard_map/ppermute | solution.py:436
  76.8 2.9 %collective-permute-start.19 = (bf16[128,2048]{1,0:T(8,128)(2,1)S(1)}, bf16[128,2048]{1,0:T(8,128)(2,1)S(1)}, u32[]{:S(2)}, u32[]{:S(2)}) collective-permute-start(bf16[128,2048]{1,0:T(8,128)(2,1)S(1)} %collective-permute-done.9.refs_2_), channel_id=1, source_target_pairs={{0,4},{1,5},{2,6},{3,7},{4,0},{5,1},{6,2},{7,3},{8,12},{9,13},{10,... | collective-permute-start | bytes 1572872 | tf_op jit(solution)/shard_map/ppermute | solution.py:436
  81.1 10.9 %expert.4 = (bf16[128,2048]{1,0:T(8,128)(2,1)}, bf16[128,2048]{1,0:T(8,128)(2,1)}, bf16[128,2048]{1,0:T(8,128)(2,1)}, bf16[128,2048]{1,0:T(8,128)(2,1)}, f32[4,1...) custom-call(s32[2]{0:T(128)} %copy-done.12, ...), custom_call_target="tpu_custom_call" | custom-call | flops 4831838208 | bytes 37748736 | tf_op jit(solution)/shard_map/expert/pallas_call | solution.py:202
  98.0 3.7 %collective-permute-done.22.refs_2_ = bf16[128,2048]{1,0:T(8,128)(2,1)S(1)} collective-permute-done((bf16[128,2048]{1,0:T(8,128)(2,1)S(1)}, bf16[128,2048]{1,0:T(8,128)(2,1)S(1)}, u32[]{:S(2)}, u32[]{:S(2)}) %collective-permute-start.22) | collective-permute-done | bytes 524320 | tf_op jit(solution)/shard_map/ppermute | solution.py:436
  104.3 10.9 %expert.5 = (bf16[128,2048]{1,0:T(8,128)(2,1)}, bf16[128,2048]{1,0:T(8,128)(2,1)}, bf16[128,2048]{1,0:T(8,128)(2,1)}, bf16[128,2048]{1,0:T(8,128)(2,1)}, f32[4,1...) custom-call(s32[2]{0:T(128)} %copy-done.12, ...), custom_call_target="tpu_custom_call" | custom-call | flops 4831838208 | bytes 37748736 | tf_op jit(solution)/shard_map/expert/pallas_call | solution.py:202
  115.2 4.9 %collective-permute-done.23.refs_3_ = bf16[128,2048]{1,0:T(8,128)(2,1)S(1)} collective-permute-done((bf16[128,2048]{1,0:T(8,128)(2,1)S(1)}, bf16[128,2048]{1,0:T(8,128)(2,1)S(1)}, u32[]{:S(2)}, u32[]{:S(2)}) %collective-permute-start.23) | collective-permute-done | bytes 524320 | tf_op jit(solution)/shard_map/ppermute | solution.py:436
  128.7 10.9 %expert.6 = (bf16[128,2048]{1,0:T(8,128)(2,1)}, bf16[128,2048]{1,0:T(8,128)(2,1)}, bf16[128,2048]{1,0:T(8,128)(2,1)}, bf16[128,2048]{1,0:T(8,128)(2,1)}, f32[4,1...) custom-call(s32[2]{0:T(128)} %copy-done.12, ...), custom_call_target="tpu_custom_call" | custom-call | flops 4831838208 | bytes 37748736 | tf_op jit(solution)/shard_map/expert/pallas_call | solution.py:202
  139.6 2.9 %collective-permute-done.27.refs_1_.refs_7_ = bf16[128,2048]{1,0:T(8,128)(2,1)} collective-permute-done((bf16[128,2048]{1,0:T(8,128)(2,1)S(1)}, bf16[128,2048]{1,0:T(8,128)(2,1)}, u32[]{:S(2)}, u32[]{:S(2)}) %collective-permute-start.27) | collective-permute-done | bytes 524320 | tf_op jit(solution)/shard_map/ppermute | solution.py:436
  147.2 10.9 %expert.7 = (bf16[128,2048]{1,0:T(8,128)(2,1)}, bf16[128,2048]{1,0:T(8,128)(2,1)}, bf16[128,2048]{1,0:T(8,128)(2,1)}, bf16[128,2048]{1,0:T(8,128)(2,1)}, f32[4,1...) custom-call(s32[2]{0:T(128)} %copy-done.12, ...), custom_call_target="tpu_custom_call" | custom-call | flops 4831838208 | bytes 37748736 | tf_op jit(solution)/shard_map/expert/pallas_call | solution.py:202
  161.9 2.7 there_sum.4
  164.6 3.4 %collective-permute-done.33 = f32[4,2,1,128]{3,0,1,2:T(4,128)S(1)} collective-permute-done((f32[4,2,1,128]{3,0,1,2:T(4,128)S(1)}, f32[4,2,1,128]{3,0,1,2:T(4,128)S(1)}, u32[]{:S(2)}, u32[]{:S(2)}) %collective-permute-start.33) | collective-permute-done | bytes 4128 | tf_op jit(solution)/shard_map/ppermute | solution.py:436
  169.0 2.7 there_sum.5
  175.2 5.9 %collective-permute-done.34 = f32[2,4,1,128]{3,0,1,2:T(2,128)S(1)} collective-permute-done((f32[2,4,1,128]{3,0,1,2:T(2,128)S(1)}, f32[2,4,1,128]{3,0,1,2:T(2,128)S(1)}, u32[]{:S(2)}, u32[]{:S(2)}) %collective-permute-start.34) | collective-permute-done | bytes 4128 | tf_op jit(solution)/shard_map/ppermute | solution.py:436
  182.2 3.0 %pair_sum.3 = bf16[2,128,2048]{2,1,0:T(8,128)(2,1)} custom-call(s32[2]{0:T(128)} %copy-done.12, f32[1,16,128]{2,1,0:T(8,128)} %get-tuple-element.845.tables, bf16[128,2048]{1,0:T(8,128)(2,1)} %get-tuple-element.758.refs_0_, bf16[128,2048]{1,0:T(8,128)(2,1)} %copy-done.21, bf16[128,2048]{1,0:T(8,128)(2,1)} %copy-done.29, ...), custom_call_target="tpu_custom_call" | custom-call | flops 134217728 | bytes 3145728 | tf_op jit(solution)/shard_map/pair_sum/pallas_call | solution.py:347
  190.8 2.7 there_sum.6
  194.1 12.9 %weight_sums.2 = (f32[3,2048,384]{2,1,0:T(8,128)}, bf16[3,2048,384]{2,1,0:T(8,128)(2,1)}) custom-call(s32[2]{0:T(128)} %copy-done.12, bf16[128,2048]{1,0:T(8,128)(2,1)} %copy-done.16, bf16[128,2048]{1,0:T(8,128)(2,1)} %copy-done.41, bf16[128,2048]{1,0:T(8,128)(2,1)} %copy-done.17, bf16[128,2048]{1,0:T(8,128)(2,1)} %copy-done.43, ...), custom_call_target="tpu_custom_call" | custom-call | flops 6442450944 | bytes 62914560 | tf_op jit(solution)/shard_map/weight_sums/pallas_call | solution.py:393
  208.4 3.1 %pair_sum.4 = (bf16[128,2048]{1,0:T(8,128)(2,1)}, bf16[128,2048]{1,0:T(8,128)(2,1)}) custom-call(s32[2]{0:T(128)} %copy-done.12, f32[1,16,128]{2,1,0:T(8,128)} %get-tuple-element.844.tables, bf16[128,2048]{1,0:T(8,128)(2,1)} %get-tuple-element.751.refs_0_, bf16[128,2048]{1,0:T(8,128)(2,1)} %copy-done.25, bf16[128,2048]{1,0:T(8,128)(2,1)} %copy-done.33, ...), custom_call_target="tpu_custom_call" | custom-call | flops 134217728 | bytes 4194304 | tf_op jit(solution)/shard_map/pair_sum/pallas_call | solution.py:347
  212.4 2.8 %pair_sum.5 = (bf16[128,2048]{1,0:T(8,128)(2,1)}, bf16[128,2048]{1,0:T(8,128)(2,1)}) custom-call(s32[2]{0:T(128)} %copy-done.12, f32[1,16,128]{2,1,0:T(8,128)} %slice_bitcast_fusion.13.tables, bf16[128,2048]{1,0:T(8,128)(2,1)} %get-tuple-element.787.refs_0_, bf16[128,2048]{1,0:T(8,128)(2,1)} %copy-done.23, bf16[128,2048]{1,0:T(8,128)(2,1)} %copy-done.31, ...), custom_call_target="tpu_custom_call" | custom-call | flops 134217728 | bytes 3145728 | tf_op jit(solution)/shard_map/pair_sum/pallas_call | solution.py:347
  219.0 5.5 %collective-permute-start.45 = (bf16[128,2048]{1,0:T(8,128)(2,1)}, bf16[128,2048]{1,0:T(8,128)(2,1)S(1)}, u32[]{:S(2)}, u32[]{:S(2)}) collective-permute-start(bf16[128,2048]{1,0:T(8,128)(2,1)} %get-tuple-element.813), channel_id=1, source_target_pairs={{0,8},{1,9},{2,10},{3,11},{4,12},{5,13},{6,14},{7,15},{8,0},{9,1},... | collective-permute-start | bytes 1572872 | tf_op jit(solution)/shard_map/ppermute | solution.py:436
  225.1 9.7 %weight_sums.3 = (f32[3,2048,384]{2,1,0:T(8,128)}, bf16[3,2048,384]{2,1,0:T(8,128)(2,1)}) custom-call(s32[2]{0:T(128)} %copy-done.12, bf16[128,2048]{1,0:T(8,128)(2,1)} %copy-done.6, bf16[128,2048]{1,0:T(8,128)(2,1)} %collective-permute-done.6.refs_3_.refs_1_, bf16[128,2048]{1,0:T(8,128)(2,1)} %copy-done.7, ...), custom_call_target="tpu_custom_call", output_to_operand_aliasing={{0}: (13, {}), {1}: (14, {})} | custom-call | flops 3221225472 | bytes 31457280 | tf_op jit(solution)/shard_map/weight_sums/pallas_call | solution.py:393
  235.8 2.6 there_sum.7
  242.8 11.4 %collective-permute-done.47.refs_0_ = bf16[128,2048]{1,0:T(8,128)(2,1)S(1)} collective-permute-done((bf16[128,2048]{1,0:T(8,128)(2,1)}, bf16[128,2048]{1,0:T(8,128)(2,1)S(1)}, u32[]{:S(2)}, u32[]{:S(2)}) %collective-permute-start.47) | collective-permute-done | bytes 524320 | tf_op jit(solution)/shard_map/ppermute | solution.py:436
  255.2 2.0 token_sum.2
  257.3 8.2 %fusion = bf16[1,3,2048,384]{3,2,1,0:T(8,128)(2,1)} fusion(f32[3,2048,384]{2,1,0:T(8,128)} %get-tuple-element.828, bf16[3,2048,384]{2,1,0:T(8,128)(2,1)} %collective-permute-done.52), kind=kLoop, calls=%fused_computation.1 | loop fusion | flops 7077888 | bytes 18874368 | tf_op jit(solution)/shard_map/broadcast_in_dim | solution.py:584
  266.7 2.0 token_sum.3
  (228 shorter events, 85.2 us)
Async XLA Ops:
  7.2 41.4 %all-gather.2.cloned.1.call-start = ((), (), s32[]{:S(2)}) async-start(), calls=%async_computation | async-start | bytes 14155776 | tf_op jit(solution)/shard_map/all_gather | solution.py:448
  11.2 24.3 %collective-permute-start.7 = (bf16[128,2048]{1,0:T(8,128)(2,1)S(1)}, bf16[128,2048]{1,0:T(8,128)(2,1)S(1)}, u32[]{:S(2)}, u32[]{:S(2)}) collective-permute-start(bf16[128,2048]{1,0:T(8,128)(2,1)S(1)} %copy-done.10), channel_id=1, source_target_pairs={{0,4},{1,5},{2,6},{3,7},{4,0},{5,1},{6,2},{7,3},{8,12},{9,13},{10,... | collective-permute-start | bytes 1572872 | tf_op jit(solution)/shard_map/ppermute | solution.py:436
  11.7 33.1 %collective-permute-start.8 = (bf16[128,2048]{1,0:T(8,128)(2,1)S(1)}, bf16[128,2048]{1,0:T(8,128)(2,1)S(1)}, u32[]{:S(2)}, u32[]{:S(2)}) collective-permute-start(bf16[128,2048]{1,0:T(8,128)(2,1)S(1)} %copy-done.11), channel_id=1, source_target_pairs={{0,4},{1,5},{2,6},{3,7},{4,0},{5,1},{6,2},{7,3},{8,12},{9,13},{10,... | collective-permute-start | bytes 1572872 | tf_op jit(solution)/shard_map/ppermute | solution.py:436
  13.2 34.6 %collective-permute-start.9 = (bf16[128,2048]{1,0:T(8,128)(2,1)S(1)}, bf16[128,2048]{1,0:T(8,128)(2,1)S(1)}, u32[]{:S(2)}, u32[]{:S(2)}) collective-permute-start(bf16[128,2048]{1,0:T(8,128)(2,1)S(1)} %copy-done.10), channel_id=1, source_target_pairs={{0,8},{1,9},{2,10},{3,11},{4,12},{5,13},{6,14},{7,15},{8,0},{9,1},... | collective-permute-start | bytes 1572872 | tf_op jit(solution)/shard_map/ppermute | solution.py:436
  31.3 16.5 %collective-permute-start.5 = (bf16[128,2048]{1,0:T(8,128)(2,1)S(1)}, bf16[128,2048]{1,0:T(8,128)(2,1)S(1)}, u32[]{:S(2)}, u32[]{:S(2)}) collective-permute-start(bf16[128,2048]{1,0:T(8,128)(2,1)S(1)} %get-tuple-element.436), channel_id=1, source_target_pairs={{0,1},{1,0},{2,3},{3,2},{4,5},{5,4},{6,7},{7,6},{8,9},{9,8},{10,11... | collective-permute-start | bytes 1572872 | tf_op jit(solution)/shard_map/ppermute | solution.py:436
  49.7 24.2 %collective-permute-start.15 = (bf16[128,2048]{1,0:T(8,128)(2,1)S(1)}, bf16[128,2048]{1,0:T(8,128)(2,1)S(1)}, u32[]{:S(2)}, u32[]{:S(2)}) collective-permute-start(bf16[128,2048]{1,0:T(8,128)(2,1)S(1)} %copy-done.11), channel_id=1, source_target_pairs={{0,8},{1,9},{2,10},{3,11},{4,12},{5,13},{6,14},{7,15},{8,0},{9,1},... | collective-permute-start | bytes 1572872 | tf_op jit(solution)/shard_map/ppermute | solution.py:436
  62.4 18.0 %collective-permute-start.13 = (bf16[128,2048]{1,0:T(8,128)(2,1)S(1)}, bf16[128,2048]{1,0:T(8,128)(2,1)S(1)}, u32[]{:S(2)}, u32[]{:S(2)}) collective-permute-start(bf16[128,2048]{1,0:T(8,128)(2,1)S(1)} %get-tuple-element.462), channel_id=1, source_target_pairs={{0,1},{1,0},{2,3},{3,2},{4,5},{5,4},{6,7},{7,6},{8,9},{9,8},{10,11... | collective-permute-start | bytes 1572872 | tf_op jit(solution)/shard_map/ppermute | solution.py:436
  67.4 24.6 %collective-permute-start.14 = (bf16[128,2048]{1,0:T(8,128)(2,1)}, bf16[128,2048]{1,0:T(8,128)(2,1)}, u32[]{:S(2)}, u32[]{:S(2)}) collective-permute-start(bf16[128,2048]{1,0:T(8,128)(2,1)} %get-tuple-element.463), channel_id=1, source_target_pairs={{0,2},{1,3},{2,0},{3,1},{4,6},{5,7},{6,4},{7,5},{8,10},{9,11},{10,... | collective-permute-start | bytes 1572872 | tf_op jit(solution)/shard_map/ppermute | solution.py:436
  73.8 18.2 %collective-permute-start.16 = (bf16[128,2048]{1,0:T(8,128)(2,1)S(1)}, bf16[128,2048]{1,0:T(8,128)(2,1)S(1)}, u32[]{:S(2)}, u32[]{:S(2)}) collective-permute-start(bf16[128,2048]{1,0:T(8,128)(2,1)S(1)} %collective-permute-done.9.refs_2_), channel_id=1, source_target_pairs={{0,2},{1,3},{2,0},{3,1},{4,6},{5,7},{6,4},{7,5},{8,10},{9,11},{10,... | collective-permute-start | bytes 1572872 | tf_op jit(solution)/shard_map/ppermute | solution.py:436
  75.3 16.7 %collective-permute-start.17 = (bf16[128,2048]{1,0:T(8,128)(2,1)S(1)}, bf16[128,2048]{1,0:T(8,128)(2,1)S(1)}, u32[]{:S(2)}, u32[]{:S(2)}) collective-permute-start(bf16[128,2048]{1,0:T(8,128)(2,1)S(1)} %collective-permute-done.15.refs_2_), channel_id=1, source_target_pairs={{0,1},{1,0},{2,3},{3,2},{4,5},{5,4},{6,7},{7,6},{8,9},{9,8},{10,11... | collective-permute-start | bytes 1572872 | tf_op jit(solution)/shard_map/ppermute | solution.py:436
  81.1 20.6 %collective-permute-start.22 = (bf16[128,2048]{1,0:T(8,128)(2,1)S(1)}, bf16[128,2048]{1,0:T(8,128)(2,1)S(1)}, u32[]{:S(2)}, u32[]{:S(2)}) collective-permute-start(bf16[128,2048]{1,0:T(8,128)(2,1)S(1)} %collective-permute-done.15.refs_2_), channel_id=1, source_target_pairs={{0,4},{1,5},{2,6},{3,7},{4,0},{5,1},{6,2},{7,3},{8,12},{9,13},{10,... | collective-permute-start | bytes 1572872 | tf_op jit(solution)/shard_map/ppermute | solution.py:436
  94.6 20.6 %collective-permute-start.20 = (bf16[128,2048]{1,0:T(8,128)(2,1)S(1)}, bf16[128,2048]{1,0:T(8,128)(2,1)}, u32[]{:S(2)}, u32[]{:S(2)}) collective-permute-start(bf16[128,2048]{1,0:T(8,128)(2,1)S(1)} %get-tuple-element.501), channel_id=1, source_target_pairs={{0,1},{1,0},{2,3},{3,2},{4,5},{5,4},{6,7},{7,6},{8,9},{9,8},{10,11... | collective-permute-start | bytes 1572872 | tf_op jit(solution)/shard_map/ppermute | solution.py:436
  97.5 17.7 %collective-permute-start.21 = (bf16[128,2048]{1,0:T(8,128)(2,1)S(1)}, bf16[128,2048]{1,0:T(8,128)(2,1)S(1)}, u32[]{:S(2)}, u32[]{:S(2)}) collective-permute-start(bf16[128,2048]{1,0:T(8,128)(2,1)S(1)} %get-tuple-element.502), channel_id=1, source_target_pairs={{0,2},{1,3},{2,0},{3,1},{4,6},{5,7},{6,4},{7,5},{8,10},{9,11},{10,... | collective-permute-start | bytes 1572872 | tf_op jit(solution)/shard_map/ppermute | solution.py:436
  101.7 18.4 %collective-permute-start.23 = (bf16[128,2048]{1,0:T(8,128)(2,1)S(1)}, bf16[128,2048]{1,0:T(8,128)(2,1)S(1)}, u32[]{:S(2)}, u32[]{:S(2)}) collective-permute-start(bf16[128,2048]{1,0:T(8,128)(2,1)S(1)} %collective-permute-done.19.refs_2_), channel_id=1, source_target_pairs={{0,2},{1,3},{2,0},{3,1},{4,6},{5,7},{6,4},{7,5},{8,10},{9,11},{10,... | collective-permute-start | bytes 1572872 | tf_op jit(solution)/shard_map/ppermute | solution.py:436
  102.2 17.9 %collective-permute-start.24 = (bf16[128,2048]{1,0:T(8,128)(2,1)S(1)}, bf16[128,2048]{1,0:T(8,128)(2,1)S(1)}, u32[]{:S(2)}, u32[]{:S(2)}) collective-permute-start(bf16[128,2048]{1,0:T(8,128)(2,1)S(1)} %collective-permute-done.22.refs_2_), channel_id=1, source_target_pairs={{0,1},{1,0},{2,3},{3,2},{4,5},{5,4},{6,7},{7,6},{8,9},{9,8},{10,11... | collective-permute-start | bytes 1572872 | tf_op jit(solution)/shard_map/ppermute | solution.py:436
  120.2 19.4 %collective-permute-start.25 = (bf16[128,2048]{1,0:T(8,128)(2,1)}, bf16[128,2048]{1,0:T(8,128)(2,1)S(1)}, u32[]{:S(2)}, u32[]{:S(2)}) collective-permute-start(bf16[128,2048]{1,0:T(8,128)(2,1)} %get-tuple-element.541), channel_id=1, source_target_pairs={{0,1},{1,0},{2,3},{3,2},{4,5},{5,4},{6,7},{7,6},{8,9},{9,8},{10,11... | collective-permute-start | bytes 1572872 | tf_op jit(solution)/shard_map/ppermute | solution.py:436
  121.7 17.9 %collective-permute-start.26 = (bf16[128,2048]{1,0:T(8,128)(2,1)}, bf16[128,2048]{1,0:T(8,128)(2,1)S(1)}, u32[]{:S(2)}, u32[]{:S(2)}) collective-permute-start(bf16[128,2048]{1,0:T(8,128)(2,1)} %get-tuple-element.543), channel_id=1, source_target_pairs={{0,2},{1,3},{2,0},{3,1},{4,6},{5,7},{6,4},{7,5},{8,10},{9,11},{10,... | collective-permute-start | bytes 1572872 | tf_op jit(solution)/shard_map/ppermute | solution.py:436
  123.5 18.9 %collective-permute-start.27 = (bf16[128,2048]{1,0:T(8,128)(2,1)S(1)}, bf16[128,2048]{1,0:T(8,128)(2,1)}, u32[]{:S(2)}, u32[]{:S(2)}) collective-permute-start(bf16[128,2048]{1,0:T(8,128)(2,1)S(1)} %get-tuple-element.550), channel_id=1, source_target_pairs={{0,1},{1,0},{2,3},{3,2},{4,5},{5,4},{6,7},{7,6},{8,9},{9,8},{10,11... | collective-permute-start | bytes 1572872 | tf_op jit(solution)/shard_map/ppermute | solution.py:436
  127.4 15.9 %collective-permute-start.28 = (bf16[128,2048]{1,0:T(8,128)(2,1)S(1)}, bf16[128,2048]{1,0:T(8,128)(2,1)S(1)}, u32[]{:S(2)}, u32[]{:S(2)}) collective-permute-start(bf16[128,2048]{1,0:T(8,128)(2,1)S(1)} %get-tuple-element.551), channel_id=1, source_target_pairs={{0,2},{1,3},{2,0},{3,1},{4,6},{5,7},{6,4},{7,5},{8,10},{9,11},{10,... | collective-permute-start | bytes 1572872 | tf_op jit(solution)/shard_map/ppermute | solution.py:436
  185.2 21.8 %collective-permute-start.41 = (bf16[2,128,2048]{2,1,0:T(8,128)(2,1)}, bf16[2,128,2048]{2,1,0:T(8,128)(2,1)S(1)}, u32[]{:S(2)}, u32[]{:S(2)}) collective-permute-start(bf16[2,128,2048]{2,1,0:T(8,128)(2,1)} %pair_sum.3), channel_id=1, source_target_pairs={{0,4},{1,5},{2,6},{3,7},{4,0},{5,1},{6,2},{7,3},{8,12},{9,13},{10,... | collective-permute-start | bytes 3145736 | tf_op jit(solution)/shard_map/ppermute | solution.py:436
  186.7 20.3 %collective-permute-start.37 = (bf16[128,2048]{1,0:T(8,128)(2,1)}, bf16[128,2048]{1,0:T(8,128)(2,1)S(1)}, u32[]{:S(2)}, u32[]{:S(2)}) collective-permute-start(bf16[128,2048]{1,0:T(8,128)(2,1)} %get-tuple-element.768), channel_id=1, source_target_pairs={{0,2},{1,3},{2,0},{3,1},{4,6},{5,7},{6,4},{7,5},{8,10},{9,11},{10,... | collective-permute-start | bytes 1572872 | tf_op jit(solution)/shard_map/ppermute | solution.py:436
  188.5 18.5 %collective-permute-start.38 = (bf16[128,2048]{1,0:T(8,128)(2,1)}, bf16[128,2048]{1,0:T(8,128)(2,1)S(1)}, u32[]{:S(2)}, u32[]{:S(2)}) collective-permute-start(bf16[128,2048]{1,0:T(8,128)(2,1)} %get-tuple-element.770), channel_id=1, source_target_pairs={{0,1},{1,0},{2,3},{3,2},{4,5},{5,4},{6,7},{7,6},{8,9},{9,8},{10,11... | collective-permute-start | bytes 1572872 | tf_op jit(solution)/shard_map/ppermute | solution.py:436
  193.4 18.0 %collective-permute-start.39 = (bf16[128,2048]{1,0:T(8,128)(2,1)}, bf16[128,2048]{1,0:T(8,128)(2,1)S(1)}, u32[]{:S(2)}, u32[]{:S(2)}) collective-permute-start(bf16[128,2048]{1,0:T(8,128)(2,1)} %get-tuple-element.773), channel_id=1, source_target_pairs={{0,2},{1,3},{2,0},{3,1},{4,6},{5,7},{6,4},{7,5},{8,10},{9,11},{10,... | collective-permute-start | bytes 1572872 | tf_op jit(solution)/shard_map/ppermute | solution.py:436
  193.7 17.7 %collective-permute-start.40 = (bf16[128,2048]{1,0:T(8,128)(2,1)}, bf16[128,2048]{1,0:T(8,128)(2,1)S(1)}, u32[]{:S(2)}, u32[]{:S(2)}) collective-permute-start(bf16[128,2048]{1,0:T(8,128)(2,1)} %get-tuple-element.774), channel_id=1, source_target_pairs={{0,1},{1,0},{2,3},{3,2},{4,5},{5,4},{6,7},{7,6},{8,9},{9,8},{10,11... | collective-permute-start | bytes 1572872 | tf_op jit(solution)/shard_map/ppermute | solution.py:436
  215.2 23.1 %collective-permute-start.46 = (bf16[128,2048]{1,0:T(8,128)(2,1)}, bf16[128,2048]{1,0:T(8,128)(2,1)S(1)}, u32[]{:S(2)}, u32[]{:S(2)}) collective-permute-start(bf16[128,2048]{1,0:T(8,128)(2,1)} %get-tuple-element.793), channel_id=1, source_target_pairs={{0,4},{1,5},{2,6},{3,7},{4,0},{5,1},{6,2},{7,3},{8,12},{9,13},{10,... | collective-permute-start | bytes 1572872 | tf_op jit(solution)/shard_map/ppermute | solution.py:436
  215.8 19.0 %collective-permute-start.42 = (bf16[128,2048]{1,0:T(8,128)(2,1)}, bf16[128,2048]{1,0:T(8,128)(2,1)S(1)}, u32[]{:S(2)}, u32[]{:S(2)}) collective-permute-start(bf16[128,2048]{1,0:T(8,128)(2,1)} %get-tuple-element.794), channel_id=1, source_target_pairs={{0,1},{1,0},{2,3},{3,2},{4,5},{5,4},{6,7},{7,6},{8,9},{9,8},{10,11... | collective-permute-start | bytes 1572872 | tf_op jit(solution)/shard_map/ppermute | solution.py:436
  217.2 17.6 %collective-permute-start.43 = (bf16[128,2048]{1,0:T(8,128)(2,1)S(1)}, bf16[128,2048]{1,0:T(8,128)(2,1)S(1)}, u32[]{:S(2)}, u32[]{:S(2)}) collective-permute-start(bf16[128,2048]{1,0:T(8,128)(2,1)S(1)} %copy-done.42), channel_id=1, source_target_pairs={{0,2},{1,3},{2,0},{3,1},{4,6},{5,7},{6,4},{7,5},{8,10},{9,11},{10,... | collective-permute-start | bytes 1572872 | tf_op jit(solution)/shard_map/ppermute | solution.py:436
  219.0 19.4 %collective-permute-start.45 = (bf16[128,2048]{1,0:T(8,128)(2,1)}, bf16[128,2048]{1,0:T(8,128)(2,1)S(1)}, u32[]{:S(2)}, u32[]{:S(2)}) collective-permute-start(bf16[128,2048]{1,0:T(8,128)(2,1)} %get-tuple-element.813), channel_id=1, source_target_pairs={{0,8},{1,9},{2,10},{3,11},{4,12},{5,13},{6,14},{7,15},{8,0},{9,1},... | collective-permute-start | bytes 1572872 | tf_op jit(solution)/shard_map/ppermute | solution.py:436
  239.4 17.9 %collective-permute-start.52 = (bf16[3,2048,384]{2,1,0:T(8,128)(2,1)}, bf16[3,2048,384]{2,1,0:T(8,128)(2,1)}, u32[]{:S(2)}, u32[]{:S(2)}) collective-permute-start(bf16[3,2048,384]{2,1,0:T(8,128)(2,1)} %get-tuple-element.829), channel_id=1, source_target_pairs={{0,16},{16,0},{1,17},{17,1},{2,18},{18,2},{3,19},{19,3},{4,20},{20... | collective-permute-start | bytes 14155784 | tf_op jit(solution)/shard_map/ppermute | solution.py:439
  241.4 24.2 %collective-permute-start.49 = (bf16[128,2048]{1,0:T(8,128)(2,1)S(1)}, bf16[128,2048]{1,0:T(8,128)(2,1)S(1)}, u32[]{:S(2)}, u32[]{:S(2)}) collective-permute-start(bf16[128,2048]{1,0:T(8,128)(2,1)S(1)} %copy-done.44), channel_id=1, source_target_pairs={{0,8},{1,9},{2,10},{3,11},{4,12},{5,13},{6,14},{7,15},{8,0},{9,1},... | collective-permute-start | bytes 1572872 | tf_op jit(solution)/shard_map/ppermute | solution.py:436
  242.6 23.4 %collective-permute-start.50 = (bf16[128,2048]{1,0:T(8,128)(2,1)}, bf16[128,2048]{1,0:T(8,128)(2,1)S(1)}, u32[]{:S(2)}, u32[]{:S(2)}) collective-permute-start(bf16[128,2048]{1,0:T(8,128)(2,1)} %get-tuple-element.831), channel_id=1, source_target_pairs={{0,4},{1,5},{2,6},{3,7},{4,0},{5,1},{6,2},{7,3},{8,12},{9,13},{10,... | collective-permute-start | bytes 1572872 | tf_op jit(solution)/shard_map/ppermute | solution.py:436
  242.7 23.3 %collective-permute-start.51 = (bf16[128,2048]{1,0:T(8,128)(2,1)}, bf16[128,2048]{1,0:T(8,128)(2,1)S(1)}, u32[]{:S(2)}, u32[]{:S(2)}) collective-permute-start(bf16[128,2048]{1,0:T(8,128)(2,1)} %get-tuple-element.833), channel_id=1, source_target_pairs={{0,1},{1,0},{2,3},{3,2},{4,5},{5,4},{6,7},{7,6},{8,9},{9,8},{10,11... | collective-permute-start | bytes 1572872 | tf_op jit(solution)/shard_map/ppermute | solution.py:436
  (67 other events, 578.4 us)
Sparse Core Ops, SparseCore 0:
  9.6 23.3 all-gather.1

commit v4 on v3

--- a/solution.py
+++ b/solution.py
@@ -555,7 +555,7 @@
     send_parts(2, *held["part 2"])
     last = swap(total, FLIP_NEAR)
     send_parts(1, *sum_there(1))
-    held["weight sums"] = sum_weights("t", ["dgate", "dup"], False, 0)
+    held["weight sums"] = sum_weights("g", ["act"], True, 2)
     held["sum 2"] = sum_here(2, [last], True)
     held.fence()
     held["far t"] = swap(held["sum 2"][0], FLIP_FAR)
@@ -565,7 +565,7 @@
         held[name] = after(held[name], total_t)
     send_rows(0)
     held["part 0"] = sum_there(0)
-    held["weight sums"] = sum_weights("g", ["act"], True, 2, held["weight sums"])
+    held["weight sums"] = sum_weights("t", ["dgate", "dup"], False, 0, held["weight sums"])
     sums = jnp.stack(held["sums"])
     beyond = swap(after(sums[:, :, 2:], held["out got", 0], held["back got", 0]), FLIP_FAR)
     held["sums"] = sums[:, :, :2], beyond

time: 280 us -> 279 us (level)
  starting transfers between devices: 59.6 us -> 56.8 us
    unnamed x90 -> x92, local copies, waits for them, and re-layouts: 10.4 us -> 10.2 us
  transfers between devices with their start and end apart: 54 -> 54, of which waited for: 22 -> 23; matrix products, arithmetic and copies ran while one was open for 5% -> 5% of each run, Pallas kernels for 33% -> 33%
where the time goes in v4:
time: 279 us; the launch traced here: 275 us
  Pallas kernels  102 us (37%)
  waiting for transfers between devices  75 us (27%)
  starting transfers between devices  56.8 us (20%)
  between operations  14.6 us (5%)
  local copies, waits for them, and re-layouts  14 us (5%)
  other arithmetic  12.2 us (4%)
    ppermute x52, waiting for transfers between devices, swap(): lax.ppermute(array, 'expert', [(i, i ^ flip) for i in range(n_expert)])  74.4 us
    ppermute x52, starting transfers between devices, swap(): lax.ppermute(array, 'expert', [(i, i ^ flip) for i in range(n_expert)])  56.8 us
    pallas_call x4, Pallas kernels, expert(): pl.pallas_call(functools.partial(expert_kernel, capacity, len(deps)), in_...  43.6 us
    pallas_call x2, Pallas kernels, weight_sums(): pl.pallas_call(functools.partial(weight_kernel, len(rights[0]), n_out, re...  22.6 us
    pallas_call x8, Pallas kernels, pick(): pl.pallas_call(functools.partial(pick_kernel, capacity, flip, blocks, len...  12.1 us
    pallas_call x4, Pallas kernels, there_sum(): pl.pallas_call(functools.partial(there_kernel, capacity), grid=(width //...  10.6 us
    unnamed x92, local copies, waits for them, and re-layouts  10.2 us
    pallas_call x3, Pallas kernels, pair_sum(): pl.pallas_call(functools.partial(pair_kernel, capacity, len(mores)), grid...  8.95 us
  transfers between devices with their start and end apart: 54, of which 23 were waited for; matrix products, arithmetic and copies ran while one was open for 5% of the time, Pallas kernels for 33%

profile of v4, /device:TPU:8, one launch (start us, length us, event | category | flops | bytes accessed | tf_op | source)
XLA Modules:
  0.0 274.6 jit_solution(15277943569135307894)
XLA Ops:
  13.2 2.6 collective-permute-start.9
  15.9 6.1 %collective-permute-done.refs_3_ = bf16[128,2048]{1,0:T(8,128)(2,1)} collective-permute-done((bf16[128,2048]{1,0:T(8,128)(2,1)S(1)}, bf16[128,2048]{1,0:T(8,128)(2,1)}, u32[]{:S(2)}, u32[]{:S(2)}) %collective-permute-start) | collective-permute-done | bytes 524320 | tf_op jit(solution)/shard_map/ppermute | solution.py:436
  35.5 9.3 %collective-permute-done.8.refs_2_ = bf16[128,2048]{1,0:T(8,128)(2,1)S(1)} collective-permute-done((bf16[128,2048]{1,0:T(8,128)(2,1)S(1)}, bf16[128,2048]{1,0:T(8,128)(2,1)S(1)}, u32[]{:S(2)}, u32[]{:S(2)}) %collective-permute-start.8) | collective-permute-done | bytes 524320 | tf_op jit(solution)/shard_map/ppermute | solution.py:436
  44.8 3.0 %collective-permute-done.9.refs_2_ = bf16[128,2048]{1,0:T(8,128)(2,1)S(1)} collective-permute-done((bf16[128,2048]{1,0:T(8,128)(2,1)S(1)}, bf16[128,2048]{1,0:T(8,128)(2,1)S(1)}, u32[]{:S(2)}, u32[]{:S(2)}) %collective-permute-start.9) | collective-permute-done | bytes 524320 | tf_op jit(solution)/shard_map/ppermute | solution.py:436
  51.6 2.4 collective-permute-done.12
  54.0 6.8 %collective-permute-done.10.refs_3_ = bf16[128,2048]{1,0:T(8,128)(2,1)S(1)} collective-permute-done((bf16[128,2048]{1,0:T(8,128)(2,1)S(1)}, bf16[128,2048]{1,0:T(8,128)(2,1)S(1)}, u32[]{:S(2)}, u32[]{:S(2)}) %collective-permute-start.10) | collective-permute-done | bytes 524320 | tf_op jit(solution)/shard_map/ppermute | solution.py:436
  64.6 2.0 pick.11
  68.9 4.9 %collective-permute-done.15.refs_2_ = bf16[128,2048]{1,0:T(8,128)(2,1)S(1)} collective-permute-done((bf16[128,2048]{1,0:T(8,128)(2,1)S(1)}, bf16[128,2048]{1,0:T(8,128)(2,1)S(1)}, u32[]{:S(2)}, u32[]{:S(2)}) %collective-permute-start.15) | collective-permute-done | bytes 524320 | tf_op jit(solution)/shard_map/ppermute | solution.py:436
  76.8 3.0 %collective-permute-start.19 = (bf16[128,2048]{1,0:T(8,128)(2,1)S(1)}, bf16[128,2048]{1,0:T(8,128)(2,1)S(1)}, u32[]{:S(2)}, u32[]{:S(2)}) collective-permute-start(bf16[128,2048]{1,0:T(8,128)(2,1)S(1)} %collective-permute-done.9.refs_2_), channel_id=1, source_target_pairs={{0,4},{1,5},{2,6},{3,7},{4,0},{5,1},{6,2},{7,3},{8,12},{9,13},{10,... | collective-permute-start | bytes 1572872 | tf_op jit(solution)/shard_map/ppermute | solution.py:436
  81.2 10.9 %expert.4 = (bf16[128,2048]{1,0:T(8,128)(2,1)}, bf16[128,2048]{1,0:T(8,128)(2,1)}, bf16[128,2048]{1,0:T(8,128)(2,1)}, bf16[128,2048]{1,0:T(8,128)(2,1)}, f32[4,1...) custom-call(s32[2]{0:T(128)} %copy-done.8, ...), custom_call_target="tpu_custom_call" | custom-call | flops 4831838208 | bytes 37748736 | tf_op jit(solution)/shard_map/expert/pallas_call | solution.py:202
  98.0 3.7 %collective-permute-done.22.refs_2_ = bf16[128,2048]{1,0:T(8,128)(2,1)S(1)} collective-permute-done((bf16[128,2048]{1,0:T(8,128)(2,1)S(1)}, bf16[128,2048]{1,0:T(8,128)(2,1)S(1)}, u32[]{:S(2)}, u32[]{:S(2)}) %collective-permute-start.22) | collective-permute-done | bytes 524320 | tf_op jit(solution)/shard_map/ppermute | solution.py:436
  104.3 10.9 %expert.5 = (bf16[128,2048]{1,0:T(8,128)(2,1)}, bf16[128,2048]{1,0:T(8,128)(2,1)}, bf16[128,2048]{1,0:T(8,128)(2,1)}, bf16[128,2048]{1,0:T(8,128)(2,1)}, f32[4,1...) custom-call(s32[2]{0:T(128)} %copy-done.8, ...), custom_call_target="tpu_custom_call" | custom-call | flops 4831838208 | bytes 37748736 | tf_op jit(solution)/shard_map/expert/pallas_call | solution.py:202
  115.2 4.9 %collective-permute-done.23.refs_3_ = bf16[128,2048]{1,0:T(8,128)(2,1)S(1)} collective-permute-done((bf16[128,2048]{1,0:T(8,128)(2,1)S(1)}, bf16[128,2048]{1,0:T(8,128)(2,1)S(1)}, u32[]{:S(2)}, u32[]{:S(2)}) %collective-permute-start.23) | collective-permute-done | bytes 524320 | tf_op jit(solution)/shard_map/ppermute | solution.py:436
  127.9 10.9 %expert.6 = (bf16[128,2048]{1,0:T(8,128)(2,1)}, bf16[128,2048]{1,0:T(8,128)(2,1)}, bf16[128,2048]{1,0:T(8,128)(2,1)}, bf16[128,2048]{1,0:T(8,128)(2,1)}, f32[4,1...) custom-call(s32[2]{0:T(128)} %copy-done.8, ...), custom_call_target="tpu_custom_call" | custom-call | flops 4831838208 | bytes 37748736 | tf_op jit(solution)/shard_map/expert/pallas_call | solution.py:202
  138.9 3.4 %collective-permute-done.27.refs_1_.refs_7_ = bf16[128,2048]{1,0:T(8,128)(2,1)} collective-permute-done((bf16[128,2048]{1,0:T(8,128)(2,1)S(1)}, bf16[128,2048]{1,0:T(8,128)(2,1)}, u32[]{:S(2)}, u32[]{:S(2)}) %collective-permute-start.27) | collective-permute-done | bytes 524320 | tf_op jit(solution)/shard_map/ppermute | solution.py:436
  147.8 10.9 %expert.7 = (bf16[128,2048]{1,0:T(8,128)(2,1)}, bf16[128,2048]{1,0:T(8,128)(2,1)}, bf16[128,2048]{1,0:T(8,128)(2,1)}, bf16[128,2048]{1,0:T(8,128)(2,1)}, f32[4,1...) custom-call(s32[2]{0:T(128)} %copy-done.8, ...), custom_call_target="tpu_custom_call" | custom-call | flops 4831838208 | bytes 37748736 | tf_op jit(solution)/shard_map/expert/pallas_call | solution.py:202
  162.5 2.7 there_sum.4
  165.2 3.8 %collective-permute-done.33 = f32[4,2,1,128]{3,0,1,2:T(4,128)S(1)} collective-permute-done((f32[4,2,1,128]{3,0,1,2:T(4,128)S(1)}, f32[4,2,1,128]{3,0,1,2:T(4,128)S(1)}, u32[]{:S(2)}, u32[]{:S(2)}) %collective-permute-start.33) | collective-permute-done | bytes 4128 | tf_op jit(solution)/shard_map/ppermute | solution.py:436
  170.0 2.7 there_sum.5
  176.2 5.9 %collective-permute-done.34 = f32[2,4,1,128]{3,0,1,2:T(2,128)S(1)} collective-permute-done((f32[2,4,1,128]{3,0,1,2:T(2,128)S(1)}, f32[2,4,1,128]{3,0,1,2:T(2,128)S(1)}, u32[]{:S(2)}, u32[]{:S(2)}) %collective-permute-start.34) | collective-permute-done | bytes 4128 | tf_op jit(solution)/shard_map/ppermute | solution.py:436
  183.1 3.0 %pair_sum.3 = bf16[2,128,2048]{2,1,0:T(8,128)(2,1)} custom-call(s32[2]{0:T(128)} %copy-done.8, f32[1,16,128]{2,1,0:T(8,128)} %get-tuple-element.853.tables, bf16[128,2048]{1,0:T(8,128)(2,1)} %get-tuple-element.762.refs_0_, bf16[128,2048]{1,0:T(8,128)(2,1)} %copy-done.21, bf16[128,2048]{1,0:T(8,128)(2,1)} %copy-done.27, ...), custom_call_target="tpu_custom_call" | custom-call | flops 134217728 | bytes 3145728 | tf_op jit(solution)/shard_map/pair_sum/pallas_call | solution.py:347
  191.1 2.7 there_sum.6
  194.8 9.6 %weight_sums.2 = (f32[3,2048,384]{2,1,0:T(8,128)}, bf16[3,2048,384]{2,1,0:T(8,128)(2,1)}) custom-call(s32[2]{0:T(128)} %copy-done.8, bf16[128,2048]{1,0:T(8,128)(2,1)} %copy-done.14, bf16[128,2048]{1,0:T(8,128)(2,1)} %copy-done.41, bf16[128,2048]{1,0:T(8,128)(2,1)} %copy-done.16, bf16[128,2048]{1,0:T(8,128)(2,1)} %collective-permute-done.14.refs_3_, ...), custom_call_target="tpu_custom_call" | custom-call | flops 3221225472 | bytes 31457280 | tf_op jit(solution)/shard_map/weight_sums/pallas_call | solution.py:393
  206.3 3.1 %pair_sum.4 = (bf16[128,2048]{1,0:T(8,128)(2,1)}, bf16[128,2048]{1,0:T(8,128)(2,1)}) custom-call(s32[2]{0:T(128)} %copy-done.8, f32[1,16,128]{2,1,0:T(8,128)} %get-tuple-element.852.tables, bf16[128,2048]{1,0:T(8,128)(2,1)} %get-tuple-element.755.refs_0_, bf16[128,2048]{1,0:T(8,128)(2,1)} %copy-done.25, bf16[128,2048]{1,0:T(8,128)(2,1)} %copy-done.31, ...), custom_call_target="tpu_custom_call" | custom-call | flops 134217728 | bytes 4194304 | tf_op jit(solution)/shard_map/pair_sum/pallas_call | solution.py:347
  210.4 2.8 %pair_sum.5 = (bf16[128,2048]{1,0:T(8,128)(2,1)}, bf16[128,2048]{1,0:T(8,128)(2,1)}) custom-call(s32[2]{0:T(128)} %copy-done.8, f32[1,16,128]{2,1,0:T(8,128)} %slice_bitcast_fusion.13.tables, bf16[128,2048]{1,0:T(8,128)(2,1)} %get-tuple-element.791.refs_0_, bf16[128,2048]{1,0:T(8,128)(2,1)} %copy-done.23, bf16[128,2048]{1,0:T(8,128)(2,1)} %copy-done.29, ...), custom_call_target="tpu_custom_call" | custom-call | flops 134217728 | bytes 3145728 | tf_op jit(solution)/shard_map/pair_sum/pallas_call | solution.py:347
  217.0 3.2 %collective-permute-start.45 = (bf16[128,2048]{1,0:T(8,128)(2,1)}, bf16[128,2048]{1,0:T(8,128)(2,1)S(1)}, u32[]{:S(2)}, u32[]{:S(2)}) collective-permute-start(bf16[128,2048]{1,0:T(8,128)(2,1)} %get-tuple-element.821), channel_id=1, source_target_pairs={{0,8},{1,9},{2,10},{3,11},{4,12},{5,13},{6,14},{7,15},{8,0},{9,1},... | collective-permute-start | bytes 1572872 | tf_op jit(solution)/shard_map/ppermute | solution.py:436
  220.8 13.0 %weight_sums.3 = (f32[3,2048,384]{2,1,0:T(8,128)}, bf16[3,2048,384]{2,1,0:T(8,128)(2,1)}) custom-call(s32[2]{0:T(128)} %copy-done.8, bf16[128,2048]{1,0:T(8,128)(2,1)} %copy-done.12, bf16[128,2048]{1,0:T(8,128)(2,1)} %copy-done.39, bf16[128,2048]{1,0:T(8,128)(2,1)} %copy-done.13, ...), custom_call_target="tpu_custom_call", output_to_operand_aliasing={{0}: (17, {}), {1}: (18, {})} | custom-call | flops 6442450944 | bytes 62914560 | tf_op jit(solution)/shard_map/weight_sums/pallas_call | solution.py:393
  234.8 2.6 there_sum.7
  241.8 11.4 %collective-permute-done.47.refs_0_ = bf16[128,2048]{1,0:T(8,128)(2,1)S(1)} collective-permute-done((bf16[128,2048]{1,0:T(8,128)(2,1)}, bf16[128,2048]{1,0:T(8,128)(2,1)S(1)}, u32[]{:S(2)}, u32[]{:S(2)}) %collective-permute-start.47) | collective-permute-done | bytes 524320 | tf_op jit(solution)/shard_map/ppermute | solution.py:436
  254.3 2.0 token_sum.2
  256.4 8.2 %fusion = bf16[1,3,2048,384]{3,2,1,0:T(8,128)(2,1)} fusion(f32[3,2048,384]{2,1,0:T(8,128)} %get-tuple-element.836, bf16[3,2048,384]{2,1,0:T(8,128)(2,1)} %collective-permute-done.52), kind=kLoop, calls=%fused_computation.1 | loop fusion | flops 7077888 | bytes 18874368 | tf_op jit(solution)/shard_map/broadcast_in_dim | solution.py:584
  265.8 2.0 token_sum.3
  (230 shorter events, 85.6 us)
Async XLA Ops:
  7.2 41.4 %all-gather.2.cloned.1.call-start = ((), (), s32[]{:S(2)}) async-start(), calls=%async_computation | async-start | bytes 14155776 | tf_op jit(solution)/shard_map/all_gather | solution.py:448
  11.2 24.3 %collective-permute-start.7 = (bf16[128,2048]{1,0:T(8,128)(2,1)S(1)}, bf16[128,2048]{1,0:T(8,128)(2,1)S(1)}, u32[]{:S(2)}, u32[]{:S(2)}) collective-permute-start(bf16[128,2048]{1,0:T(8,128)(2,1)S(1)} %copy-done.6), channel_id=1, source_target_pairs={{0,4},{1,5},{2,6},{3,7},{4,0},{5,1},{6,2},{7,3},{8,12},{9,13},{10,... | collective-permute-start | bytes 1572872 | tf_op jit(solution)/shard_map/ppermute | solution.py:436
  11.7 33.1 %collective-permute-start.8 = (bf16[128,2048]{1,0:T(8,128)(2,1)S(1)}, bf16[128,2048]{1,0:T(8,128)(2,1)S(1)}, u32[]{:S(2)}, u32[]{:S(2)}) collective-permute-start(bf16[128,2048]{1,0:T(8,128)(2,1)S(1)} %copy-done.7), channel_id=1, source_target_pairs={{0,4},{1,5},{2,6},{3,7},{4,0},{5,1},{6,2},{7,3},{8,12},{9,13},{10,... | collective-permute-start | bytes 1572872 | tf_op jit(solution)/shard_map/ppermute | solution.py:436
  13.2 34.6 %collective-permute-start.9 = (bf16[128,2048]{1,0:T(8,128)(2,1)S(1)}, bf16[128,2048]{1,0:T(8,128)(2,1)S(1)}, u32[]{:S(2)}, u32[]{:S(2)}) collective-permute-start(bf16[128,2048]{1,0:T(8,128)(2,1)S(1)} %copy-done.6), channel_id=1, source_target_pairs={{0,8},{1,9},{2,10},{3,11},{4,12},{5,13},{6,14},{7,15},{8,0},{9,1},... | collective-permute-start | bytes 1572872 | tf_op jit(solution)/shard_map/ppermute | solution.py:436
  31.3 16.5 %collective-permute-start.5 = (bf16[128,2048]{1,0:T(8,128)(2,1)S(1)}, bf16[128,2048]{1,0:T(8,128)(2,1)S(1)}, u32[]{:S(2)}, u32[]{:S(2)}) collective-permute-start(bf16[128,2048]{1,0:T(8,128)(2,1)S(1)} %get-tuple-element.440), channel_id=1, source_target_pairs={{0,1},{1,0},{2,3},{3,2},{4,5},{5,4},{6,7},{7,6},{8,9},{9,8},{10,11... | collective-permute-start | bytes 1572872 | tf_op jit(solution)/shard_map/ppermute | solution.py:436
  49.7 24.1 %collective-permute-start.15 = (bf16[128,2048]{1,0:T(8,128)(2,1)S(1)}, bf16[128,2048]{1,0:T(8,128)(2,1)S(1)}, u32[]{:S(2)}, u32[]{:S(2)}) collective-permute-start(bf16[128,2048]{1,0:T(8,128)(2,1)S(1)} %copy-done.7), channel_id=1, source_target_pairs={{0,8},{1,9},{2,10},{3,11},{4,12},{5,13},{6,14},{7,15},{8,0},{9,1},... | collective-permute-start | bytes 1572872 | tf_op jit(solution)/shard_map/ppermute | solution.py:436
  62.4 18.0 %collective-permute-start.13 = (bf16[128,2048]{1,0:T(8,128)(2,1)S(1)}, bf16[128,2048]{1,0:T(8,128)(2,1)S(1)}, u32[]{:S(2)}, u32[]{:S(2)}) collective-permute-start(bf16[128,2048]{1,0:T(8,128)(2,1)S(1)} %get-tuple-element.466), channel_id=1, source_target_pairs={{0,1},{1,0},{2,3},{3,2},{4,5},{5,4},{6,7},{7,6},{8,9},{9,8},{10,11... | collective-permute-start | bytes 1572872 | tf_op jit(solution)/shard_map/ppermute | solution.py:436
  67.4 24.7 %collective-permute-start.14 = (bf16[128,2048]{1,0:T(8,128)(2,1)}, bf16[128,2048]{1,0:T(8,128)(2,1)}, u32[]{:S(2)}, u32[]{:S(2)}) collective-permute-start(bf16[128,2048]{1,0:T(8,128)(2,1)} %get-tuple-element.467), channel_id=1, source_target_pairs={{0,2},{1,3},{2,0},{3,1},{4,6},{5,7},{6,4},{7,5},{8,10},{9,11},{10,... | collective-permute-start | bytes 1572872 | tf_op jit(solution)/shard_map/ppermute | solution.py:436
  73.8 18.3 %collective-permute-start.16 = (bf16[128,2048]{1,0:T(8,128)(2,1)S(1)}, bf16[128,2048]{1,0:T(8,128)(2,1)S(1)}, u32[]{:S(2)}, u32[]{:S(2)}) collective-permute-start(bf16[128,2048]{1,0:T(8,128)(2,1)S(1)} %collective-permute-done.9.refs_2_), channel_id=1, source_target_pairs={{0,2},{1,3},{2,0},{3,1},{4,6},{5,7},{6,4},{7,5},{8,10},{9,11},{10,... | collective-permute-start | bytes 1572872 | tf_op jit(solution)/shard_map/ppermute | solution.py:436
  75.3 16.8 %collective-permute-start.17 = (bf16[128,2048]{1,0:T(8,128)(2,1)S(1)}, bf16[128,2048]{1,0:T(8,128)(2,1)S(1)}, u32[]{:S(2)}, u32[]{:S(2)}) collective-permute-start(bf16[128,2048]{1,0:T(8,128)(2,1)S(1)} %collective-permute-done.15.refs_2_), channel_id=1, source_target_pairs={{0,1},{1,0},{2,3},{3,2},{4,5},{5,4},{6,7},{7,6},{8,9},{9,8},{10,11... | collective-permute-start | bytes 1572872 | tf_op jit(solution)/shard_map/ppermute | solution.py:436
  76.8 15.8 %collective-permute-start.19 = (bf16[128,2048]{1,0:T(8,128)(2,1)S(1)}, bf16[128,2048]{1,0:T(8,128)(2,1)S(1)}, u32[]{:S(2)}, u32[]{:S(2)}) collective-permute-start(bf16[128,2048]{1,0:T(8,128)(2,1)S(1)} %collective-permute-done.9.refs_2_), channel_id=1, source_target_pairs={{0,4},{1,5},{2,6},{3,7},{4,0},{5,1},{6,2},{7,3},{8,12},{9,13},{10,... | collective-permute-start | bytes 1572872 | tf_op jit(solution)/shard_map/ppermute | solution.py:436
  81.2 20.5 %collective-permute-start.22 = (bf16[128,2048]{1,0:T(8,128)(2,1)S(1)}, bf16[128,2048]{1,0:T(8,128)(2,1)S(1)}, u32[]{:S(2)}, u32[]{:S(2)}) collective-permute-start(bf16[128,2048]{1,0:T(8,128)(2,1)S(1)} %collective-permute-done.15.refs_2_), channel_id=1, source_target_pairs={{0,4},{1,5},{2,6},{3,7},{4,0},{5,1},{6,2},{7,3},{8,12},{9,13},{10,... | collective-permute-start | bytes 1572872 | tf_op jit(solution)/shard_map/ppermute | solution.py:436
  94.6 20.7 %collective-permute-start.20 = (bf16[128,2048]{1,0:T(8,128)(2,1)S(1)}, bf16[128,2048]{1,0:T(8,128)(2,1)}, u32[]{:S(2)}, u32[]{:S(2)}) collective-permute-start(bf16[128,2048]{1,0:T(8,128)(2,1)S(1)} %get-tuple-element.505), channel_id=1, source_target_pairs={{0,1},{1,0},{2,3},{3,2},{4,5},{5,4},{6,7},{7,6},{8,9},{9,8},{10,11... | collective-permute-start | bytes 1572872 | tf_op jit(solution)/shard_map/ppermute | solution.py:436
  97.5 17.7 %collective-permute-start.21 = (bf16[128,2048]{1,0:T(8,128)(2,1)S(1)}, bf16[128,2048]{1,0:T(8,128)(2,1)S(1)}, u32[]{:S(2)}, u32[]{:S(2)}) collective-permute-start(bf16[128,2048]{1,0:T(8,128)(2,1)S(1)} %get-tuple-element.506), channel_id=1, source_target_pairs={{0,2},{1,3},{2,0},{3,1},{4,6},{5,7},{6,4},{7,5},{8,10},{9,11},{10,... | collective-permute-start | bytes 1572872 | tf_op jit(solution)/shard_map/ppermute | solution.py:436
  101.7 18.5 %collective-permute-start.23 = (bf16[128,2048]{1,0:T(8,128)(2,1)S(1)}, bf16[128,2048]{1,0:T(8,128)(2,1)S(1)}, u32[]{:S(2)}, u32[]{:S(2)}) collective-permute-start(bf16[128,2048]{1,0:T(8,128)(2,1)S(1)} %collective-permute-done.19.refs_2_), channel_id=1, source_target_pairs={{0,2},{1,3},{2,0},{3,1},{4,6},{5,7},{6,4},{7,5},{8,10},{9,11},{10,... | collective-permute-start | bytes 1572872 | tf_op jit(solution)/shard_map/ppermute | solution.py:436
  102.2 18.0 %collective-permute-start.24 = (bf16[128,2048]{1,0:T(8,128)(2,1)S(1)}, bf16[128,2048]{1,0:T(8,128)(2,1)S(1)}, u32[]{:S(2)}, u32[]{:S(2)}) collective-permute-start(bf16[128,2048]{1,0:T(8,128)(2,1)S(1)} %collective-permute-done.22.refs_2_), channel_id=1, source_target_pairs={{0,1},{1,0},{2,3},{3,2},{4,5},{5,4},{6,7},{7,6},{8,9},{9,8},{10,11... | collective-permute-start | bytes 1572872 | tf_op jit(solution)/shard_map/ppermute | solution.py:436
  120.2 18.7 %collective-permute-start.25 = (bf16[128,2048]{1,0:T(8,128)(2,1)}, bf16[128,2048]{1,0:T(8,128)(2,1)S(1)}, u32[]{:S(2)}, u32[]{:S(2)}) collective-permute-start(bf16[128,2048]{1,0:T(8,128)(2,1)} %get-tuple-element.545), channel_id=1, source_target_pairs={{0,1},{1,0},{2,3},{3,2},{4,5},{5,4},{6,7},{7,6},{8,9},{9,8},{10,11... | collective-permute-start | bytes 1572872 | tf_op jit(solution)/shard_map/ppermute | solution.py:436
  121.7 17.2 %collective-permute-start.26 = (bf16[128,2048]{1,0:T(8,128)(2,1)}, bf16[128,2048]{1,0:T(8,128)(2,1)S(1)}, u32[]{:S(2)}, u32[]{:S(2)}) collective-permute-start(bf16[128,2048]{1,0:T(8,128)(2,1)} %get-tuple-element.547), channel_id=1, source_target_pairs={{0,2},{1,3},{2,0},{3,1},{4,6},{5,7},{6,4},{7,5},{8,10},{9,11},{10,... | collective-permute-start | bytes 1572872 | tf_op jit(solution)/shard_map/ppermute | solution.py:436
  123.6 18.7 %collective-permute-start.27 = (bf16[128,2048]{1,0:T(8,128)(2,1)S(1)}, bf16[128,2048]{1,0:T(8,128)(2,1)}, u32[]{:S(2)}, u32[]{:S(2)}) collective-permute-start(bf16[128,2048]{1,0:T(8,128)(2,1)S(1)} %get-tuple-element.554), channel_id=1, source_target_pairs={{0,1},{1,0},{2,3},{3,2},{4,5},{5,4},{6,7},{7,6},{8,9},{9,8},{10,11... | collective-permute-start | bytes 1572872 | tf_op jit(solution)/shard_map/ppermute | solution.py:436
  126.7 16.7 %collective-permute-start.28 = (bf16[128,2048]{1,0:T(8,128)(2,1)S(1)}, bf16[128,2048]{1,0:T(8,128)(2,1)S(1)}, u32[]{:S(2)}, u32[]{:S(2)}) collective-permute-start(bf16[128,2048]{1,0:T(8,128)(2,1)S(1)} %get-tuple-element.555), channel_id=1, source_target_pairs={{0,2},{1,3},{2,0},{3,1},{4,6},{5,7},{6,4},{7,5},{8,10},{9,11},{10,... | collective-permute-start | bytes 1572872 | tf_op jit(solution)/shard_map/ppermute | solution.py:436
  186.1 19.2 %collective-permute-start.41 = (bf16[2,128,2048]{2,1,0:T(8,128)(2,1)}, bf16[2,128,2048]{2,1,0:T(8,128)(2,1)S(1)}, u32[]{:S(2)}, u32[]{:S(2)}) collective-permute-start(bf16[2,128,2048]{2,1,0:T(8,128)(2,1)} %pair_sum.3), channel_id=1, source_target_pairs={{0,4},{1,5},{2,6},{3,7},{4,0},{5,1},{6,2},{7,3},{8,12},{9,13},{10,... | collective-permute-start | bytes 3145736 | tf_op jit(solution)/shard_map/ppermute | solution.py:436
  187.5 16.9 %collective-permute-start.37 = (bf16[128,2048]{1,0:T(8,128)(2,1)}, bf16[128,2048]{1,0:T(8,128)(2,1)S(1)}, u32[]{:S(2)}, u32[]{:S(2)}) collective-permute-start(bf16[128,2048]{1,0:T(8,128)(2,1)} %get-tuple-element.772), channel_id=1, source_target_pairs={{0,2},{1,3},{2,0},{3,1},{4,6},{5,7},{6,4},{7,5},{8,10},{9,11},{10,... | collective-permute-start | bytes 1572872 | tf_op jit(solution)/shard_map/ppermute | solution.py:436
  189.0 15.4 %collective-permute-start.38 = (bf16[128,2048]{1,0:T(8,128)(2,1)}, bf16[128,2048]{1,0:T(8,128)(2,1)S(1)}, u32[]{:S(2)}, u32[]{:S(2)}) collective-permute-start(bf16[128,2048]{1,0:T(8,128)(2,1)} %get-tuple-element.774), channel_id=1, source_target_pairs={{0,1},{1,0},{2,3},{3,2},{4,5},{5,4},{6,7},{7,6},{8,9},{9,8},{10,11... | collective-permute-start | bytes 1572872 | tf_op jit(solution)/shard_map/ppermute | solution.py:436
  193.7 15.6 %collective-permute-start.39 = (bf16[128,2048]{1,0:T(8,128)(2,1)}, bf16[128,2048]{1,0:T(8,128)(2,1)S(1)}, u32[]{:S(2)}, u32[]{:S(2)}) collective-permute-start(bf16[128,2048]{1,0:T(8,128)(2,1)} %get-tuple-element.777), channel_id=1, source_target_pairs={{0,2},{1,3},{2,0},{3,1},{4,6},{5,7},{6,4},{7,5},{8,10},{9,11},{10,... | collective-permute-start | bytes 1572872 | tf_op jit(solution)/shard_map/ppermute | solution.py:436
  213.2 24.2 %collective-permute-start.46 = (bf16[128,2048]{1,0:T(8,128)(2,1)}, bf16[128,2048]{1,0:T(8,128)(2,1)S(1)}, u32[]{:S(2)}, u32[]{:S(2)}) collective-permute-start(bf16[128,2048]{1,0:T(8,128)(2,1)} %get-tuple-element.797), channel_id=1, source_target_pairs={{0,4},{1,5},{2,6},{3,7},{4,0},{5,1},{6,2},{7,3},{8,12},{9,13},{10,... | collective-permute-start | bytes 1572872 | tf_op jit(solution)/shard_map/ppermute | solution.py:436
  214.0 19.8 %collective-permute-start.42 = (bf16[128,2048]{1,0:T(8,128)(2,1)}, bf16[128,2048]{1,0:T(8,128)(2,1)S(1)}, u32[]{:S(2)}, u32[]{:S(2)}) collective-permute-start(bf16[128,2048]{1,0:T(8,128)(2,1)} %get-tuple-element.798), channel_id=1, source_target_pairs={{0,1},{1,0},{2,3},{3,2},{4,5},{5,4},{6,7},{7,6},{8,9},{9,8},{10,11... | collective-permute-start | bytes 1572872 | tf_op jit(solution)/shard_map/ppermute | solution.py:436
  215.2 18.6 %collective-permute-start.43 = (bf16[128,2048]{1,0:T(8,128)(2,1)S(1)}, bf16[128,2048]{1,0:T(8,128)(2,1)S(1)}, u32[]{:S(2)}, u32[]{:S(2)}) collective-permute-start(bf16[128,2048]{1,0:T(8,128)(2,1)S(1)} %copy-done.42), channel_id=1, source_target_pairs={{0,2},{1,3},{2,0},{3,1},{4,6},{5,7},{6,4},{7,5},{8,10},{9,11},{10,... | collective-permute-start | bytes 1572872 | tf_op jit(solution)/shard_map/ppermute | solution.py:436
  217.0 20.4 %collective-permute-start.45 = (bf16[128,2048]{1,0:T(8,128)(2,1)}, bf16[128,2048]{1,0:T(8,128)(2,1)S(1)}, u32[]{:S(2)}, u32[]{:S(2)}) collective-permute-start(bf16[128,2048]{1,0:T(8,128)(2,1)} %get-tuple-element.821), channel_id=1, source_target_pairs={{0,8},{1,9},{2,10},{3,11},{4,12},{5,13},{6,14},{7,15},{8,0},{9,1},... | collective-permute-start | bytes 1572872 | tf_op jit(solution)/shard_map/ppermute | solution.py:436
  238.4 17.9 %collective-permute-start.52 = (bf16[3,2048,384]{2,1,0:T(8,128)(2,1)}, bf16[3,2048,384]{2,1,0:T(8,128)(2,1)}, u32[]{:S(2)}, u32[]{:S(2)}) collective-permute-start(bf16[3,2048,384]{2,1,0:T(8,128)(2,1)} %get-tuple-element.837), channel_id=1, source_target_pairs={{0,16},{16,0},{1,17},{17,1},{2,18},{18,2},{3,19},{19,3},{4,20},{20... | collective-permute-start | bytes 14155784 | tf_op jit(solution)/shard_map/ppermute | solution.py:439
  240.4 24.2 %collective-permute-start.49 = (bf16[128,2048]{1,0:T(8,128)(2,1)S(1)}, bf16[128,2048]{1,0:T(8,128)(2,1)S(1)}, u32[]{:S(2)}, u32[]{:S(2)}) collective-permute-start(bf16[128,2048]{1,0:T(8,128)(2,1)S(1)} %copy-done.45), channel_id=1, source_target_pairs={{0,8},{1,9},{2,10},{3,11},{4,12},{5,13},{6,14},{7,15},{8,0},{9,1},... | collective-permute-start | bytes 1572872 | tf_op jit(solution)/shard_map/ppermute | solution.py:436
  241.7 23.4 %collective-permute-start.50 = (bf16[128,2048]{1,0:T(8,128)(2,1)}, bf16[128,2048]{1,0:T(8,128)(2,1)S(1)}, u32[]{:S(2)}, u32[]{:S(2)}) collective-permute-start(bf16[128,2048]{1,0:T(8,128)(2,1)} %get-tuple-element.839), channel_id=1, source_target_pairs={{0,4},{1,5},{2,6},{3,7},{4,0},{5,1},{6,2},{7,3},{8,12},{9,13},{10,... | collective-permute-start | bytes 1572872 | tf_op jit(solution)/shard_map/ppermute | solution.py:436
  241.7 23.3 %collective-permute-start.51 = (bf16[128,2048]{1,0:T(8,128)(2,1)}, bf16[128,2048]{1,0:T(8,128)(2,1)S(1)}, u32[]{:S(2)}, u32[]{:S(2)}) collective-permute-start(bf16[128,2048]{1,0:T(8,128)(2,1)} %get-tuple-element.841), channel_id=1, source_target_pairs={{0,1},{1,0},{2,3},{3,2},{4,5},{5,4},{6,7},{7,6},{8,9},{9,8},{10,11... | collective-permute-start | bytes 1572872 | tf_op jit(solution)/shard_map/ppermute | solution.py:436
  (68 other events, 613.2 us)
Sparse Core Ops, SparseCore 0:
  9.6 23.3 all-gather.1
